TPU v7x, 256 devices: a whole 4x4x8 slice. The times are simulated.
256 devices in a mesh: wide: 32 (over y, x, core), narrow: 8 (over z).
Axes of the slice: x: 4, y: 4, z: 8, core: 2. Of those that a mesh axis runs over, the one named last changes fastest.
Arguments:
- amplitudes: bfloat16 [4096, 10240], P(('narrow', 'wide')), may hold values from -6 to 6
- integrals: bfloat16 [10240, 20480], P('narrow', 'wide'), may hold values from -0.15625 to 0.15625
- other_terms: bfloat16 [4096, 20480], P('narrow', 'wide'), may hold values from -6 to 6
- occ_energy: float32 [64], replicated, may hold values from -2 to -0.5
- virt_energy: float32 [640], replicated, may hold values from 0.2 to 3
- occ_irrep: int32 [64], replicated, may hold values from 0 to 7
- virt_irrep: int32 [640], replicated, may hold values from 0 to 7
- tiles_e: int32 [1], replicated, may hold values from 0 to 39
- tiles_a: int32 [2], replicated, may hold values from 0 to 39
Outputs:
- new_amplitudes: float32 [4096, 20480], P('narrow', 'wide')
All inputs are finite; a program needn't handle non-finite values.
Results may differ from a plain program's by a relative error of at most 0.0003.
Values may be sent and summed in bfloat16 or wider, within the bound.
No kernel may reach another device: no remote copies, remote signals or barrier semaphores. Data moves between devices by JAX's collectives and lax.ppermute only.
A program may use at most 128 MiB of HBM per device.

v0:
```python
import jax
import jax.numpy as jnp
from jax import lax
from jax.sharding import PartitionSpec as P

TILE = 16


def pair_labels(tiles, lookup_table):
    offsets = jnp.arange(TILE, dtype=jnp.int32)
    orbital_index = (tiles[:, None] * TILE + offsets[None, :]).reshape(-1)
    matches = orbital_index[:, None] == jnp.arange(lookup_table.shape[0], dtype=jnp.int32)[None, :]
    return jnp.sum(
        jnp.where(matches, lookup_table[None, :], jnp.zeros((), lookup_table.dtype)), axis=1
    )


def shards(
    amplitudes,
    integrals,
    other_terms,
    occ_energy,
    virt_energy,
    occ_irrep,
    virt_irrep,
    tiles_e,
    tiles_a,
):
    gathered = lax.all_gather(amplitudes, "wide", axis=0, tiled=True)
    ef_sym = jnp.bitwise_xor(
        pair_labels(tiles_e, virt_irrep)[:, None], virt_irrep[None, :]
    ).reshape(-1)
    ab_sym_all = jnp.bitwise_xor(
        pair_labels(tiles_a, virt_irrep)[:, None], virt_irrep[None, :]
    ).reshape(-1)
    ab_energy_all = (pair_labels(tiles_a, virt_energy)[:, None] + virt_energy[None, :]).reshape(-1)
    col_width = integrals.shape[1]
    col_first = lax.axis_index("wide") * col_width
    col_sym = lax.dynamic_slice_in_dim(ab_sym_all, col_first, col_width)
    col_energy = lax.dynamic_slice_in_dim(ab_energy_all, col_first, col_width)
    row_height = gathered.shape[0]
    row_first = lax.axis_index("narrow") * row_height
    ij_sym = lax.dynamic_slice_in_dim(
        jnp.bitwise_xor(occ_irrep[:, None], occ_irrep[None, :]).reshape(-1), row_first, row_height
    )
    ij_energy = lax.dynamic_slice_in_dim(
        (occ_energy[:, None] + occ_energy[None, :]).reshape(-1), row_first, row_height
    )
    panel_rows = lax.all_gather(integrals, "narrow", axis=0, tiled=True)
    masked = jnp.where(
        ef_sym[:, None] == col_sym[None, :], panel_rows, jnp.zeros((), panel_rows.dtype)
    )
    ladder = jnp.dot(gathered, masked, preferred_element_type=jnp.float32)
    summed = ladder + other_terms.astype(jnp.float32)
    denom = ij_energy[:, None] - col_energy[None, :]
    return jnp.where(
        ij_sym[:, None] == col_sym[None, :], summed / denom, jnp.zeros((), jnp.float32)
    )


def solution(mesh):
    in_specs = (
        P(("narrow", "wide"), None),
        P("narrow", "wide"),
        P("narrow", "wide"),
        P(),
        P(),
        P(),
        P(),
        P(),
        P(),
    )
    out_specs = P("narrow", "wide")
    return jax.shard_map(shards, mesh=mesh, in_specs=in_specs, out_specs=out_specs, check_vma=False)
```

profile of v0, /device:TPU:1, one launch (start us, length us, event | category | flops | bytes accessed | tf_op | source)
XLA Modules:
  0.0 238.1 jit_solution(13137942508783967882)
XLA Ops:
  6.5 0.0 copy-start
  6.6 0.0 all-gather.5.cloned.1.call-start
  6.6 0.7 all-gather.5.cloned.1.call-update
  7.3 0.0 all-gather.3.cloned.1.call-start
  7.3 0.7 all-gather.3.cloned.1.call-update
  8.7 0.0 copy-done.5
  8.7 0.1 iota_add_fusion
  8.8 0.1 add.90
  8.9 0.0 copy-done.3
  8.9 0.1 broadcast_add_fusion.1
  8.9 0.1 add.99
  9.0 0.0 copy-done.4
  9.0 0.1 broadcast_xor_fusion.2
  9.1 0.1 xor.53
  9.2 0.1 dynamic_slice.14
  9.2 0.1 dynamic_slice.12
  9.3 0.0 copy-done.1
  9.3 0.2 select_reduce_fusion.2
  9.5 0.1 broadcast_xor_fusion.1
  9.6 0.2 select_reduce_fusion.1
  9.8 0.1 broadcast_xor_fusion
  9.9 0.0 copy-done.2
  9.9 0.2 select_reduce_fusion
  10.1 0.1 broadcast_add_fusion
  10.2 0.1 dynamic_slice.13
  10.3 0.1 dynamic_slice.15
  10.3 0.0 copy-done
  10.3 0.3 copy.12
  10.6 66.5 %all-gather.5.cloned.1.call-done = bf16[512,10240]{1,0:T(8,128)(2,1)} async-done(((bf16[16,10240]{1,0:T(8,128)(2,1)}), bf16[512,10240]{1,0:T(8,128)(2,1)}) %all-gather.5.cloned.1.call-update) | async-done | bytes 10485776 | tf_op jit(solution)/shard_map/all_gather | solution.py:29
  77.1 139.4 %all-gather.3.cloned.1.call-done = bf16[10240,640]{1,0:T(8,128)(2,1)} async-done(((bf16[1280,640]{1,0:T(8,128)(2,1)}), bf16[10240,640]{1,0:T(8,128)(2,1)}) %all-gather.3.cloned.1.call-update) | async-done | bytes 13107216 | tf_op jit(solution)/shard_map/all_gather | solution.py:49
  216.4 13.4 %fusion.7 = f32[512,640]{0,1:T(8,128)S(1)} fusion(bf16[512,10240]{1,0:T(8,128)(2,1)} %all-gather.5.cloned.1.call-done, bf16[10240,640]{1,0:T(8,128)(2,1)} %all-gather.3.cloned.1.call-done, s32[640]{0:T(1024)S(1)} %dynamic_slice.13, s32[10240]{0:T(1024)S(1)} %xor.59, bf16[512,640]{0,1:T(8,128)(2,1)S(1)} %copy.12, f32[640]{0:T(1024)S(1)} %dynamic_slice.15, ...), kind=kOutput, calls=%fused_computation.8 | convolution fusion | flops 6725959680 | bytes 25609216 | tf_op jit(solution)/shard_map/dot_general | solution.py:53
  229.8 1.5 copy.13
  (10 shorter events, 0.0 us)
Async XLA Ops:
  6.5 2.2 copy-start.5
  6.5 2.3 copy-start.3
  6.5 2.5 %copy-start.4 = (s32[64]{0:T(128)S(1)}, s32[64]{0:T(128)}, u32[]{:S(2)}) copy-start(s32[64]{0:T(128)} %param.14) | copy-start | bytes 772
  6.5 2.8 %copy-start.1 = (s32[640]{0:T(1024)S(1)}, s32[640]{0:T(1024)}, u32[]{:S(2)}) copy-start(s32[640]{0:T(1024)} %param.15) | copy-start | bytes 7684
  6.5 3.3 %copy-start.2 = (f32[640]{0:T(1024)S(1)}, f32[640]{0:T(1024)}, u32[]{:S(2)}) copy-start(f32[640]{0:T(1024)} %param.13) | copy-start | bytes 7684
  6.5 3.8 %copy-start = (bf16[512,640]{1,0:T(8,128)(2,1)S(1)}, bf16[512,640]{1,0:T(8,128)(2,1)}, u32[]{:S(2)}) copy-start(bf16[512,640]{1,0:T(8,128)(2,1)} %param.11) | copy-start | bytes 1966084
  6.6 70.5 %all-gather.5.cloned.1.call-start = ((), (), s32[]{:S(2)}) async-start(), calls=%async_computation.1 | async-start | bytes 10813440 | tf_op jit(solution)/shard_map/all_gather | solution.py:29
  7.3 209.1 %all-gather.3.cloned.1.call-start = ((), (), s32[]{:S(2)}) async-start(), calls=%async_computation | async-start | bytes 14745600 | tf_op jit(solution)/shard_map/all_gather | solution.py:49
Sparse Core Ops, SparseCore 0:
  9.9 67.0 all-gather.4
  78.8 137.5 all-gather.2
where the time goes:
time: 238 us
  waiting for transfers between devices  207 us (87%)
  between operations  14.1 us (6%)
  matrix products  13.4 us (6%)
    all_gather x1, waiting for transfers between devices, shards(): panel_rows = lax.all_gather(integrals, 'narrow', axis=0, tiled=True)  139 us
    all_gather x1, waiting for transfers between devices, shards(): gathered = lax.all_gather(amplitudes, 'wide', axis=0, tiled=True)  66.5 us
    dot_general x1, matrix products, shards(): ladder = jnp.dot(gathered, masked, preferred_element_type=jnp.float32)  13.4 us
  transfers between devices with their start and end apart: 2, of which 2 were waited for; matrix products, arithmetic and copies ran while one was open for 1% of the time, Pallas kernels for 0%

commit v1 on v0

--- a/solution.py
+++ b/solution.py
@@ -1,9 +1,163 @@
 import jax
 import jax.numpy as jnp
 from jax import lax
+from jax.experimental import pallas as pl
+from jax.experimental.pallas import tpu as pltpu
 from jax.sharding import PartitionSpec as P
 
 TILE = 16
+NVIR = 640
+NOCC = 64
+IRREPS = 8
+CAP = 112
+PITCH = 128
+E_LOCAL = 2
+VMEM_LIMIT = 56 * 1024 * 1024
+
+SMEM = pl.BlockSpec(memory_space=pltpu.SMEM)
+VMEM = pl.BlockSpec(memory_space=pltpu.VMEM)
+
+
+def selector(irrep_row):
+    group = lax.broadcasted_iota(jnp.int32, (IRREPS, NVIR), 0)
+    member = irrep_row == group
+    earlier = lax.broadcasted_iota(jnp.int32, (NVIR, NVIR), 0) < lax.broadcasted_iota(
+        jnp.int32, (NVIR, NVIR), 1
+    )
+    before = jnp.dot(
+        member.astype(jnp.bfloat16),
+        earlier.astype(jnp.bfloat16),
+        preferred_element_type=jnp.float32,
+    )
+    rank = jnp.sum(jnp.where(member, before, 0.0), axis=0, keepdims=True).astype(jnp.int32)
+    place = jnp.where(rank < CAP, irrep_row * PITCH + rank, -1)
+    slots = lax.broadcasted_iota(jnp.int32, (IRREPS * PITCH, NVIR), 0)
+    return (slots == place).astype(jnp.bfloat16)
+
+
+def pack_amplitudes(irrep_s, occ_s, tiles_e_s, irrep_row, rows_ref, out_ref, stacked):
+    wide, narrow = lax.axis_index("wide"), lax.axis_index("narrow")
+    e_count = rows_ref.shape[1] // NVIR
+    height = rows_ref.shape[0]
+    for e in range(e_count):
+        stacked[e * height:(e + 1) * height, :] = rows_ref[:, e * NVIR:(e + 1) * NVIR]
+    picked = lax.dot_general(
+        stacked[...],
+        selector(irrep_row[...]),
+        (((1,), (1,)), ((), ())),
+        preferred_element_type=jnp.float32,
+    )
+    first = (narrow * 32 + wide) * height
+    line = lax.broadcasted_iota(jnp.int32, (height, PITCH), 0)
+    occ = jnp.zeros((height, PITCH), jnp.int32)
+    for row in range(height):
+        pair = first + row
+        sym = occ_s[pair // NOCC] ^ occ_s[pair % NOCC]
+        occ = jnp.where(line == row, sym, occ)
+    for e in range(e_count):
+        wanted = occ ^ irrep_s[tiles_e_s[0] * TILE + e]
+        block = jnp.zeros((height, PITCH), jnp.float32)
+        for g in range(IRREPS):
+            block = jnp.where(
+                wanted == g,
+                picked[e * height:(e + 1) * height, g * PITCH:(g + 1) * PITCH],
+                block,
+            )
+        out_ref[:, e * PITCH:(e + 1) * PITCH] = block.astype(out_ref.dtype)
+
+
+def pack_integrals(irrep_s, tiles_e_s, tiles_a_s, irrep_row, panel_ref, out_ref):
+    wide, narrow = lax.axis_index("wide"), lax.axis_index("narrow")
+    a = tiles_a_s[wide // TILE] * TILE + wide % TILE
+    picks = selector(irrep_row[...])
+    for local in range(E_LOCAL):
+        e = tiles_e_s[0] * TILE + narrow * E_LOCAL + local
+        wanted = irrep_row[...] ^ (irrep_s[a] ^ irrep_s[e])
+        panel = panel_ref[local * NVIR:(local + 1) * NVIR, :]
+        block = jnp.zeros((CAP, NVIR), jnp.float32)
+        for g in range(IRREPS):
+            picked = jnp.dot(
+                picks[g * PITCH:g * PITCH + CAP, :], panel, preferred_element_type=jnp.float32
+            )
+            block = jnp.where(wanted == g, picked, block)
+        out_ref[local * CAP:(local + 1) * CAP, :] = block.astype(out_ref.dtype)
+
+
+def as_column(row):
+    width = row.shape[1]
+    across = lax.broadcasted_iota(jnp.int32, (width, width), 1)
+    down = lax.broadcasted_iota(jnp.int32, (width, width), 0)
+    return jnp.sum(jnp.where(across == down, row, jnp.zeros_like(row)), axis=1, keepdims=True)
+
+
+def contract(
+    irrep_s, energy_s, occ_irrep_s, occ_energy_s, tiles_a_s,
+    irrep_row, energy_row, occ_irrep_row, occ_energy_row,
+    amplitudes, panel, other, out_ref, spread,
+):
+    wide, narrow = lax.axis_index("wide"), lax.axis_index("narrow")
+    e_count = amplitudes.shape[1] // PITCH
+    for e in range(e_count):
+        spread[e * PITCH:e * PITCH + CAP, :] = panel[e * CAP:(e + 1) * CAP, :]
+        spread[e * PITCH + CAP:(e + 1) * PITCH, :] = jnp.zeros(
+            (PITCH - CAP, NVIR), spread.dtype
+        )
+    a = tiles_a_s[wide // TILE] * TILE + wide % TILE
+    col_sym = irrep_row[...] ^ irrep_s[a]
+    col_energy = energy_s[a] + energy_row[...]
+    j_sym = as_column(occ_irrep_row[...])
+    j_energy = as_column(occ_energy_row[...])
+    i_count = out_ref.shape[0] // NOCC
+    ladder = jnp.dot(amplitudes[...], spread[...], preferred_element_type=jnp.float32)
+    for local in range(i_count):
+        i = narrow * i_count + local
+        rows = slice(local * NOCC, (local + 1) * NOCC)
+        summed = ladder[rows, :] + other[rows, :].astype(jnp.float32)
+        denom = (occ_energy_s[i] + j_energy) - col_energy
+        same = (j_sym ^ occ_irrep_s[i]) == col_sym
+        out_ref[rows, :] = jnp.where(same, summed / denom, 0.0)
+
+
+def packed_plan(
+    amplitudes, integrals, other_terms, occ_energy, virt_energy, occ_irrep, virt_irrep, tiles_e, tiles_a
+):
+    irrep_row = virt_irrep.reshape(1, NVIR)
+    params = pltpu.CompilerParams(vmem_limit_bytes=VMEM_LIMIT)
+    height, width = amplitudes.shape
+    e_count = width // NVIR
+    small = pl.pallas_call(
+        pack_amplitudes,
+        out_shape=jax.ShapeDtypeStruct((height, e_count * PITCH), amplitudes.dtype),
+        in_specs=[SMEM, SMEM, SMEM, VMEM, VMEM],
+        out_specs=VMEM,
+        scratch_shapes=[pltpu.VMEM((e_count * height, NVIR), amplitudes.dtype)],
+        compiler_params=params,
+        name="pack_amplitudes",
+    )(virt_irrep, occ_irrep, tiles_e, irrep_row, amplitudes)
+    rows = lax.all_gather(small, "wide", axis=0, tiled=True)
+    strip = pl.pallas_call(
+        pack_integrals,
+        out_shape=jax.ShapeDtypeStruct((E_LOCAL * CAP, NVIR), integrals.dtype),
+        in_specs=[SMEM, SMEM, SMEM, VMEM, VMEM],
+        out_specs=VMEM,
+        compiler_params=params,
+        name="pack_integrals",
+    )(virt_irrep, tiles_e, tiles_a, irrep_row, integrals)
+    panel = lax.all_gather(strip, "narrow", axis=0, tiled=True)
+    return pl.pallas_call(
+        contract,
+        out_shape=jax.ShapeDtypeStruct(other_terms.shape, jnp.float32),
+        in_specs=[SMEM] * 5 + [VMEM] * 7,
+        out_specs=VMEM,
+        scratch_shapes=[pltpu.VMEM((e_count * PITCH, NVIR), integrals.dtype)],
+        compiler_params=params,
+        name="contract",
+    )(
+        virt_irrep, virt_energy, occ_irrep, occ_energy, tiles_a,
+        irrep_row, virt_energy.reshape(1, NVIR),
+        occ_irrep.reshape(1, NOCC), occ_energy.reshape(1, NOCC),
+        rows, panel, other_terms,
+    )
 
 
 def pair_labels(tiles, lookup_table):
@@ -15,16 +169,8 @@
     )
 
 
-def shards(
-    amplitudes,
-    integrals,
-    other_terms,
-    occ_energy,
-    virt_energy,
-    occ_irrep,
-    virt_irrep,
-    tiles_e,
-    tiles_a,
+def dense_plan(
+    amplitudes, integrals, other_terms, occ_energy, virt_energy, occ_irrep, virt_irrep, tiles_e, tiles_a
 ):
     gathered = lax.all_gather(amplitudes, "wide", axis=0, tiled=True)
     ef_sym = jnp.bitwise_xor(
@@ -58,6 +204,14 @@
     )
 
 
+def shards(*args):
+    virt_irrep = args[6]
+    held = jnp.sum(
+        virt_irrep[None, :] == jnp.arange(IRREPS, dtype=jnp.int32)[:, None], axis=1, dtype=jnp.int32
+    )
+    return lax.cond(jnp.max(held) <= CAP, packed_plan, dense_plan, *args)
+
+
 def solution(mesh):
     in_specs = (
         P(("narrow", "wide"), None),

time: 238 us -> 124 us (0.52)
  waiting for transfers between devices: 207 us -> 92.8 us
  matrix products: 13.4 us -> 0 us
  Pallas kernels: 0 us -> 12.5 us
    all_gather x2, waiting for transfers between devices: 206 us -> 92.8 us  [the longest x1 53.9 us: packed_plan(): rows = lax.all_gather(small, 'wide', axis=0, tiled=True)]
    dot_general x1 -> x0, matrix products: 13.4 us -> none  [shards(): ladder = jnp.dot(gathered, masked, preferred_element_type=jnp.float32)]
    pallas_call x0 -> x3, Pallas kernels: none -> 12.5 us  [the longest x1 5.48 us: packed_plan(): pl.pallas_call(pack_integrals, out_shape=jax.ShapeDtypeStruct((E_LOCAL *...]
  transfers between devices with their start and end apart: 2 -> 2, of which waited for: 2 -> 2; matrix products, arithmetic and copies ran while one was open for 1% -> 0% of each run, Pallas kernels for 0% -> 2%
where the time goes in v1:
time: 124 us
  waiting for transfers between devices  92.8 us (75%)
  between operations  14 us (11%)
  Pallas kernels  12.5 us (10%)
  local copies, waits for them, and re-layouts  3.06 us (2%)
  other arithmetic  1.44 us (1%)
    all_gather x1, waiting for transfers between devices, packed_plan(): rows = lax.all_gather(small, 'wide', axis=0, tiled=True)  53.9 us
    all_gather x1, waiting for transfers between devices, packed_plan(): panel = lax.all_gather(strip, 'narrow', axis=0, tiled=True)  38.9 us
    pallas_call x1, Pallas kernels, packed_plan(): pl.pallas_call(pack_integrals, out_shape=jax.ShapeDtypeStruct((E_LOCAL *...  5.48 us
    pallas_call x1, Pallas kernels, packed_plan(): pl.pallas_call(contract, out_shape=jax.ShapeDtypeStruct(other_terms.shape...  4.17 us
    pallas_call x1, Pallas kernels, packed_plan(): pl.pallas_call(pack_amplitudes, out_shape=jax.ShapeDtypeStruct((height, e...  2.82 us
  transfers between devices with their start and end apart: 2, of which 2 were waited for; matrix products, arithmetic and copies ran while one was open for 0% of the time, Pallas kernels for 2%

profile of v1, /device:TPU:1, one launch (start us, length us, event | category | flops | bytes accessed | tf_op | source)
XLA Modules:
  0.0 124.1 jit_solution(3818442341910098645)
XLA Ops:
  6.5 0.8 convert_reduce_fusion
  7.3 0.6 reduce_max.9
  8.6 107.5 %conditional.1 = (f32[512,640]{1,0:T(8,128)S(1)}) conditional(s32[]{:T(128)} %convert_element_type.10, (s32[64]{0:T(128)}, s32[2]{0:T(128)}, s32[640]{0:T(1024)}, s32[1]{0:T(128)}, bf16[1280,640]{1,0:T(8,128)(2,1)}, /*index=5*/bf16[16,10240]{1,0:T(8,128)(2,1)}, bf16[512,640]{1,0:T(8,128)(2,1)}, f32[64]{0:T(128)}, f32[640]{0:T(1024)}) %tuple.11, ...), branch_computations={%region_2.6_spmd, %region_6.7_spmd} | conditional | flops 6726172672 | bytes 109611336 | solution.py:212
  8.6 0.0 copy-start.3
  8.7 0.0 copy-start.5
  8.7 0.0 copy-start.9
  8.7 0.0 copy-start.7
  8.7 0.0 copy-start.1
  8.7 0.0 copy-start.11
  8.7 0.0 copy-start.13
  8.7 0.0 all-gather.11.cloned.1.call-start
  8.8 1.4 %reshape.83.irrep_row = s32[1,640]{1,0:T(1,128)} reshape(s32[640]{0:T(1024)} %get-tuple-element.53.irrep_s) | data formatting | bytes 5120 | tf_op jit(solution)/shard_map/cond/branch_1_fun/reshape | solution.py:124
  10.2 5.5 %pack_integrals.1 = bf16[224,640]{1,0:T(8,128)(2,1)} custom-call(s32[640]{0:T(1024)} %get-tuple-element.53.irrep_s, s32[1]{0:T(128)} %get-tuple-element.58.tiles_e_s, s32[2]{0:T(128)} %get-tuple-element.57.tiles_a_s, s32[1,640]{1,0:T(1,128)} %reshape.83.irrep_row, bf16[1280,640]{1,0:T(8,128)(2,1)} %get-tuple-element.60.panel_ref), custom_call_target="tpu_custom_call" | custom-call | tf_op jit(solution)/shard_map/cond/branch_1_fun/pack_integrals/pallas_call | solution.py:138
  15.7 0.0 all-gather.11.cloned.1.call-update
  15.7 0.0 all-gather.9.cloned.1.call-start
  15.7 0.0 copy-done.3
  15.7 0.0 copy-done.5
  15.8 0.0 copy-done.9
  15.8 2.8 %pack_amplitudes.1 = bf16[16,2048]{1,0:T(8,128)(2,1)} custom-call(s32[640]{0:T(1024)S(1)} %copy-done.5, s32[64]{0:T(128)S(1)} %copy-done.9, s32[1]{0:T(128)} %get-tuple-element.58.tiles_e_s, s32[1,640]{1,0:T(1,128)} %reshape.83.irrep_row, bf16[16,10240]{1,0:T(8,128)(2,1)S(1)} %copy-done.3), custom_call_target="tpu_custom_call" | custom-call | tf_op jit(solution)/shard_map/cond/branch_1_fun/pack_amplitudes/pallas_call | solution.py:128
  18.6 0.0 all-gather.9.cloned.1.call-update
  18.6 0.0 copy-done.7
  18.6 0.6 reshape.84.energy_row
  19.2 38.9 %all-gather.11.cloned.1.call-done.panel = bf16[1792,640]{1,0:T(8,128)(2,1)} async-done(((bf16[224,640]{1,0:T(8,128)(2,1)}), bf16[1792,640]{1,0:T(8,128)(2,1)}) %all-gather.11.cloned.1.call-update) | async-done | bytes 2293776 | tf_op jit(solution)/shard_map/cond/branch_1_fun/all_gather | solution.py:146
  58.1 53.9 %all-gather.9.cloned.1.call-done.amplitudes = bf16[512,2048]{1,0:T(8,128)(2,1)} async-done(((bf16[16,2048]{1,0:T(8,128)(2,1)}), bf16[512,2048]{1,0:T(8,128)(2,1)}) %all-gather.9.cloned.1.call-update) | async-done | bytes 2097168 | tf_op jit(solution)/shard_map/cond/branch_1_fun/all_gather | solution.py:137
  112.0 0.0 copy-done.1
  112.0 0.0 copy-done.11
  112.0 0.0 copy-done.13
  112.0 4.2 %contract.1 = f32[512,640]{1,0:T(8,128)S(1)} custom-call(s32[640]{0:T(1024)S(1)} %copy-done.5, f32[640]{0:T(1024)S(1)} %copy-done.7, s32[64]{0:T(128)S(1)} %copy-done.9, f32[64]{0:T(128)S(1)} %copy-done.11, s32[2]{0:T(128)S(1)} %copy-done.13, s32[1,640]{1,0:T(1,128)} %reshape.83.irrep_row, f32[1,640]{1,0:T(1,128)} %reshape.84.energy_row, ...), custom_call_target="tpu_custom_call" | custom-call | tf_op jit(solution)/shard_map/cond/branch_1_fun/contract/pallas_call | solution.py:147
  116.2 0.0 copy-start.2
  116.2 1.0 copy-done.2
Async XLA Ops:
  8.6 7.1 %copy-start.3 = (bf16[16,10240]{1,0:T(8,128)(2,1)S(1)}, bf16[16,10240]{1,0:T(8,128)(2,1)}, u32[]{:S(2)}) copy-start(bf16[16,10240]{1,0:T(8,128)(2,1)} %get-tuple-element.59.rows_ref) | copy-start | bytes 983044 | tf_op jit(solution)/shard_map/cond
  8.7 7.1 %copy-start.5 = (s32[640]{0:T(1024)S(1)}, s32[640]{0:T(1024)}, u32[]{:S(2)}) copy-start(s32[640]{0:T(1024)} %get-tuple-element.53.irrep_s) | copy-start | bytes 7684 | tf_op jit(solution)/shard_map/cond
  8.7 7.1 %copy-start.9 = (s32[64]{0:T(128)S(1)}, s32[64]{0:T(128)}, u32[]{:S(2)}) copy-start(s32[64]{0:T(128)} %get-tuple-element.55.occ_s.occ_irrep_s) | copy-start | bytes 772 | tf_op jit(solution)/shard_map/cond
  8.7 9.9 %copy-start.7 = (f32[640]{0:T(1024)S(1)}, f32[640]{0:T(1024)}, u32[]{:S(2)}) copy-start(f32[640]{0:T(1024)} %get-tuple-element.54.energy_s) | copy-start | bytes 7684 | tf_op jit(solution)/shard_map/cond
  8.7 103.3 %copy-start.1 = (bf16[512,640]{1,0:T(8,128)(2,1)S(1)}, bf16[512,640]{1,0:T(8,128)(2,1)}, u32[]{:S(2)}) copy-start(bf16[512,640]{1,0:T(8,128)(2,1)} %get-tuple-element.61.other) | copy-start | bytes 1966084 | tf_op jit(solution)/shard_map/cond
  8.7 103.3 %copy-start.11 = (f32[64]{0:T(128)S(1)}, f32[64]{0:T(128)}, u32[]{:S(2)}) copy-start(f32[64]{0:T(128)} %get-tuple-element.56.occ_energy_s) | copy-start | bytes 772 | tf_op jit(solution)/shard_map/cond
  8.7 103.3 %copy-start.13 = (s32[2]{0:T(128)S(1)}, s32[2]{0:T(128)}, u32[]{:S(2)}) copy-start(s32[2]{0:T(128)} %get-tuple-element.57.tiles_a_s) | copy-start | bytes 28 | tf_op jit(solution)/shard_map/cond
  8.7 49.4 %all-gather.11.cloned.1.call-start = ((), (), s32[]{:S(2)}) async-start(), calls=%async_computation.3 | async-start | bytes 2580480 | tf_op jit(solution)/shard_map/cond/branch_1_fun/all_gather | solution.py:146
  15.7 96.3 %all-gather.9.cloned.1.call-start = ((), (), s32[]{:S(2)}) async-start(), calls=%async_computation.2 | async-start | bytes 2162688 | tf_op jit(solution)/shard_map/cond/branch_1_fun/all_gather | solution.py:137
  116.2 1.1 copy-start.2
Sparse Core Ops, SparseCore 0:
  15.8 42.2 all-gather.10
  60.7 51.2 all-gather.8

commit v2 on v0

v2 whole, which is shorter than its diff:
```python
import jax
import jax.numpy as jnp
from jax import lax
from jax.experimental import pallas as pl
from jax.experimental.pallas import tpu as pltpu
from jax.sharding import PartitionSpec as P

TILE = 16
NVIR = 640
NOCC = 64
IRREPS = 8
CAP = 112
PITCH = 128
E_LOCAL = 2
RING = 8
SIDE = 4
ROWS = 16
VMEM_LIMIT = 56 * 1024 * 1024

SMEM = pl.BlockSpec(memory_space=pltpu.SMEM)
VMEM = pl.BlockSpec(memory_space=pltpu.VMEM)


def pack(
    base_s, irrep_s, occ_s, tiles_e_s, tiles_a_s, irrep_row, rows_ref, panel_ref,
    first_ref, second_ref, out_ref, stacked,
):
    wide, narrow = lax.axis_index("wide"), lax.axis_index("narrow")
    e_first = tiles_e_s[0] * TILE
    irreps = irrep_row[...]

    group = lax.broadcasted_iota(jnp.int32, (IRREPS, NVIR), 0)
    member = irreps == group
    earlier = lax.broadcasted_iota(jnp.int32, (NVIR, NVIR), 0) < lax.broadcasted_iota(
        jnp.int32, (NVIR, NVIR), 1
    )
    before = jnp.dot(
        member.astype(jnp.bfloat16),
        earlier.astype(jnp.bfloat16),
        preferred_element_type=jnp.float32,
    )
    rank = jnp.sum(jnp.where(member, before, 0.0), axis=0, keepdims=True).astype(jnp.int32)
    place = rank - base_s[0]
    slots = lax.broadcasted_iota(jnp.int32, (PITCH, NVIR), 0)
    picks = ((slots == place) & (slots < CAP)).astype(jnp.bfloat16)

    a = tiles_a_s[wide // TILE] * TILE + wide % TILE
    irrep_col = jnp.transpose(jnp.broadcast_to(irreps, (PITCH, NVIR)))
    for local, strip_ref in enumerate((first_ref, second_ref)):
        wanted = irreps ^ (irrep_s[a] ^ irrep_s[e_first + narrow * E_LOCAL + local])
        for tile in range(NVIR // PITCH):
            lanes = slice(tile * PITCH, (tile + 1) * PITCH)
            kept = jnp.where(
                irrep_col == wanted[:, lanes],
                panel_ref[local * NVIR:(local + 1) * NVIR, lanes].astype(jnp.float32),
                0.0,
            ).astype(jnp.bfloat16)
            strip_ref[:, lanes] = jnp.dot(
                picks[:CAP, :], kept, preferred_element_type=jnp.float32
            ).astype(strip_ref.dtype)

    first = (narrow * 32 + wide) * ROWS
    line = lax.broadcasted_iota(jnp.int32, (ROWS, NVIR), 0)
    occ = jnp.zeros((ROWS, NVIR), jnp.int32)
    for row in range(ROWS):
        pair = first + row
        occ = jnp.where(line == row, occ_s[pair // NOCC] ^ occ_s[pair % NOCC], occ)
    kin = occ ^ irreps
    for e in range(TILE):
        stacked[e * ROWS:(e + 1) * ROWS, :] = jnp.where(
            kin == irrep_s[e_first + e],
            rows_ref[:, e * NVIR:(e + 1) * NVIR].astype(jnp.float32),
            0.0,
        ).astype(jnp.bfloat16)
    picked = lax.dot_general(
        stacked[...], picks, (((1,), (1,)), ((), ())), preferred_element_type=jnp.float32
    ).astype(out_ref.dtype)
    for e in range(TILE):
        out_ref[:, e * PITCH:(e + 1) * PITCH] = picked[e * ROWS:(e + 1) * ROWS, :]


def as_column(row):
    width = row.shape[1]
    across = lax.broadcasted_iota(jnp.int32, (width, width), 1)
    down = lax.broadcasted_iota(jnp.int32, (width, width), 0)
    return jnp.sum(jnp.where(across == down, row, jnp.zeros_like(row)), axis=1, keepdims=True)


def reach(index):
    return (0, -1, 1, 2)[index]


def contract(
    irrep_s, energy_s, occ_irrep_s, occ_energy_s, tiles_a_s,
    irrep_row, energy_row, occ_irrep_row, occ_energy_row, other, own, twin, *refs,
):
    strips, out_ref, amplitudes, panel = refs[:2 * RING], refs[-3], refs[-2], refs[-1]
    wide, narrow = lax.axis_index("wide"), lax.axis_index("narrow")
    y, x, core = wide // 8, wide // 2 % SIDE, wide % 2
    for ref, side in ((own, core), (twin, 1 - core)):
        for outer in range(SIDE):
            for inner in range(SIDE):
                dx = jnp.where(side == 0, reach(inner), reach(outer))
                dy = jnp.where(side == 0, reach(outer), reach(inner))
                place = (y + dy + SIDE) % SIDE * 8 + (x + dx + SIDE) % SIDE * 2 + side
                block = (outer * SIDE + inner) * ROWS
                amplitudes[pl.ds(pl.multiple_of(place * ROWS, ROWS), ROWS), :] = ref[
                    block:block + ROWS, :
                ]
    blank = jnp.zeros((PITCH - CAP, NVIR), panel.dtype)
    for step in range(RING):
        source = (narrow - step + RING) % RING
        for local in range(E_LOCAL):
            start = pl.multiple_of((source * E_LOCAL + local) * PITCH, PITCH)
            panel[pl.ds(start, CAP), :] = strips[step * E_LOCAL + local][...]
            panel[pl.ds(pl.multiple_of(start + CAP, 16), PITCH - CAP), :] = blank
    a = tiles_a_s[wide // TILE] * TILE + wide % TILE
    col_sym = irrep_row[...] ^ irrep_s[a]
    col_energy = energy_s[a] + energy_row[...]
    j_sym = as_column(occ_irrep_row[...])
    j_energy = as_column(occ_energy_row[...])
    i_count = out_ref.shape[0] // NOCC
    ladder = jnp.dot(amplitudes[...], panel[...], preferred_element_type=jnp.float32)
    for local in range(i_count):
        i = narrow * i_count + local
        rows = slice(local * NOCC, (local + 1) * NOCC)
        summed = ladder[rows, :] + other[rows, :].astype(jnp.float32)
        denom = (occ_energy_s[i] + j_energy) - col_energy
        same = (j_sym ^ occ_irrep_s[i]) == col_sym
        out_ref[rows, :] = jnp.where(same, summed / denom, 0.0)


def ring(shift):
    return [(i, (i + shift) % RING) for i in range(RING)]


def plane(along_x, along_y):
    pairs = []
    for i in range(32):
        y, x, core = i // 8, i // 2 % SIDE, i % 2
        dx, dy = (along_x, along_y) if core == 0 else (along_y, along_x)
        pairs.append((i, (y + dy) % SIDE * 8 + (x + dx) % SIDE * 2 + core))
    return pairs


def spread(block, steps):
    parts = [block] + [lax.ppermute(block, "wide", pairs) for pairs in steps]
    return jnp.concatenate(parts, axis=0)


def one_pass(
    base, amplitudes, integrals, other_terms,
    occ_energy, virt_energy, occ_irrep, virt_irrep, tiles_e, tiles_a,
):
    irrep_row = virt_irrep.reshape(1, NVIR)
    params = pltpu.CompilerParams(vmem_limit_bytes=VMEM_LIMIT)
    strip = jax.ShapeDtypeStruct((CAP, NVIR), integrals.dtype)
    first, second, block = pl.pallas_call(
        pack,
        out_shape=(strip, strip, jax.ShapeDtypeStruct((ROWS, TILE * PITCH), amplitudes.dtype)),
        in_specs=[SMEM] * 5 + [VMEM] * 3,
        out_specs=(VMEM,) * 3,
        scratch_shapes=[pltpu.VMEM((TILE * ROWS, NVIR), amplitudes.dtype)],
        compiler_params=params,
        name="pack",
    )(base, virt_irrep, occ_irrep, tiles_e, tiles_a, irrep_row, amplitudes, integrals)

    strips = [None] * RING
    strips[0] = [first, second]
    up, down = strips[0], strips[0]
    for step in range(1, RING // 2):
        up = [lax.ppermute(part, "narrow", ring(1)) for part in up]
        down = [lax.ppermute(part, "narrow", ring(-1)) for part in down]
        strips[step], strips[RING - step] = up, down
    strips[RING // 2] = [
        lax.ppermute(up[0], "narrow", ring(1)), lax.ppermute(down[1], "narrow", ring(-1))
    ]

    own = spread(block, [plane(1, 0), plane(-1, 0), plane(2, 0)])
    own = spread(own, [plane(0, 1), plane(0, -1), plane(0, 2)])
    twin = lax.ppermute(own, "wide", [(i, i ^ 1) for i in range(32)])

    return pl.pallas_call(
        contract,
        out_shape=jax.ShapeDtypeStruct(other_terms.shape, jnp.float32),
        in_specs=[SMEM] * 5 + [VMEM] * (7 + 2 * RING),
        out_specs=VMEM,
        scratch_shapes=[
            pltpu.VMEM((other_terms.shape[0], TILE * PITCH), amplitudes.dtype),
            pltpu.VMEM((TILE * PITCH, NVIR), integrals.dtype),
        ],
        compiler_params=params,
        name="contract",
    )(
        virt_irrep, virt_energy, occ_irrep, occ_energy, tiles_a,
        irrep_row, virt_energy.reshape(1, NVIR),
        occ_irrep.reshape(1, NOCC), occ_energy.reshape(1, NOCC),
        other_terms, own, twin, *[part for pair in strips for part in pair],
    )


def shards(amplitudes, integrals, other_terms, *tables):
    virt_irrep = tables[3]
    held = jnp.sum(
        virt_irrep[None, :] == jnp.arange(IRREPS, dtype=jnp.int32)[:, None], axis=1, dtype=jnp.int32
    )
    most = jnp.max(held)

    def more(state):
        return state[0] < most

    def add_pass(state):
        base, total = state
        part = one_pass(
            base.reshape(1), amplitudes, integrals, jnp.zeros_like(other_terms), *tables
        )
        return base + CAP, total + part

    whole = one_pass(jnp.zeros((1,), jnp.int32), amplitudes, integrals, other_terms, *tables)
    return lax.while_loop(more, add_pass, (jnp.int32(CAP), whole))[1]


def solution(mesh):
    in_specs = (
        P(("narrow", "wide"), None),
        P("narrow", "wide"),
        P("narrow", "wide"),
        P(),
        P(),
        P(),
        P(),
        P(),
        P(),
    )
    out_specs = P("narrow", "wide")
    return jax.shard_map(shards, mesh=mesh, in_specs=in_specs, out_specs=out_specs, check_vma=False)
```

time: 238 us -> 67.9 us (0.29)
  the two profiles are of different devices: /device:TPU:1 before, /device:TPU:96 now
where the time goes in v2:
time: 67.9 us; the launch traced here: 67.7 us
  starting transfers between devices  29.9 us (44%)
  waiting for transfers between devices  22.3 us (33%)
  Pallas kernels  7.91 us (12%)
  local copies, waits for them, and re-layouts  4.91 us (7%)
  between operations  0.94 us (1%)
  loops' own time  0.85 us (1%)
  other arithmetic  0.82 us (1%)
    ppermute x6, starting transfers between devices, one_pass(): up = [lax.ppermute(part, 'narrow', ring(1)) for part in up]  17.2 us
    ppermute x6, starting transfers between devices, spread(): parts = [block] + [lax.ppermute(block, 'wide', pairs) for pairs in steps]  10.7 us
    ppermute x6, waiting for transfers between devices, spread(): parts = [block] + [lax.ppermute(block, 'wide', pairs) for pairs in steps]  10.3 us
    ppermute x6, waiting for transfers between devices, one_pass(): down = [lax.ppermute(part, 'narrow', ring(-1)) for part in down]  6.77 us
    pallas_call x1, Pallas kernels, one_pass(): pl.pallas_call(contract, out_shape=jax.ShapeDtypeStruct(other_terms.shape...  4.78 us
    pallas_call x1, Pallas kernels, one_pass(): pl.pallas_call(pack, out_shape=(strip, strip, jax.ShapeDtypeStruct((ROWS,...  3.13 us
    unnamed x47, local copies, waits for them, and re-layouts  3 us
    ppermute x1, waiting for transfers between devices, one_pass(): lax.ppermute(down[1], 'narrow', ring(-1))  2.87 us
  transfers between devices with their start and end apart: 21, of which 13 were waited for; matrix products, arithmetic and copies ran while one was open for 3% of the time, Pallas kernels for 0%

profile of v2, /device:TPU:96, one launch (start us, length us, event | category | flops | bytes accessed | tf_op | source)
XLA Modules:
  0.0 67.7 jit_solution(9782243271245071726)
XLA Ops:
  0.7 1.3 %reshape.28.irrep_row = s32[1,640]{1,0:T(1,128)} reshape(s32[640]{0:T(1024)} %irrep_s.3) | data formatting | bytes 5120 | tf_op jit(solution)/shard_map/reshape | solution.py:155
  1.9 3.1 %pack.2 = (bf16[112,640]{1,0:T(8,128)(2,1)}, bf16[112,640]{1,0:T(8,128)(2,1)}, bf16[16,2048]{1,0:T(8,128)(2,1)}) custom-call(s32[1]{0:T(128)} %constant.3.clone.1.base_s, s32[640]{0:T(1024)} %irrep_s.3, s32[64]{0:T(128)} %occ_irrep_s.1, s32[1]{0:T(128)S(6)} %copy.34.tiles_e_s, s32[2]{0:T(128)} %tiles_a_s.3, s32[1,640]{1,0:T(1,128)} %reshape.28.irrep_row, ...), custom_call_target="tpu_custom_call" | custom-call | tf_op jit(solution)/shard_map/pack/pallas_call | solution.py:158
  5.1 3.1 %collective-permute-start.23 = (bf16[16,2048]{1,0:T(8,128)(2,1)}, bf16[16,2048]{1,0:T(8,128)(2,1)S(1)}, u32[]{:S(2)}, u32[]{:S(2)}) collective-permute-start(bf16[16,2048]{1,0:T(8,128)(2,1)} %get-tuple-element.69), channel_id=1, source_target_pairs={{0,32},{8,136},{16,48},{24,152},{32,0},{40,168},{48,16},{56,184},{... | collective-permute-start | bytes 196616 | tf_op jit(solution)/shard_map/ppermute | solution.py:147
  8.2 1.1 %collective-permute-start.22 = (bf16[16,2048]{1,0:T(8,128)(2,1)}, bf16[16,2048]{1,0:T(8,128)(2,1)S(1)}, u32[]{:S(2)}, u32[]{:S(2)}) collective-permute-start(bf16[16,2048]{1,0:T(8,128)(2,1)} %get-tuple-element.69), channel_id=1, source_target_pairs={{0,48},{8,200},{16,0},{24,216},{32,16},{40,232},{48,32},{56,248},{... | collective-permute-start | bytes 196616 | tf_op jit(solution)/shard_map/ppermute | solution.py:147
  9.4 0.9 %collective-permute-start.21 = (bf16[16,2048]{1,0:T(8,128)(2,1)}, bf16[16,2048]{1,0:T(8,128)(2,1)S(1)}, u32[]{:S(2)}, u32[]{:S(2)}) collective-permute-start(bf16[16,2048]{1,0:T(8,128)(2,1)} %get-tuple-element.69), channel_id=1, source_target_pairs={{0,16},{8,72},{16,32},{24,88},{32,48},{40,104},{48,0},{56,120},{64... | collective-permute-start | bytes 196616 | tf_op jit(solution)/shard_map/ppermute | solution.py:147
  10.3 0.9 %constant_dynamic-update-slice_fusion.14 = (bf16[64,2048]{1,0:T(8,128)(2,1)S(1)}, bf16[256,2048]{1,0:T(8,128)(2,1)S(1)}) fusion(bf16[16,2048]{1,0:T(8,128)(2,1)} %get-tuple-element.69), kind=kLoop, calls=%fused_computation.14 | loop fusion | bytes 196608
  11.1 3.9 %collective-permute-done.21 = bf16[16,2048]{1,0:T(8,128)(2,1)S(1)} collective-permute-done((bf16[16,2048]{1,0:T(8,128)(2,1)}, bf16[16,2048]{1,0:T(8,128)(2,1)S(1)}, u32[]{:S(2)}, u32[]{:S(2)}) %collective-permute-start.21) | collective-permute-done | bytes 65568 | tf_op jit(solution)/shard_map/ppermute | solution.py:147
  15.1 1.7 %collective-permute-start.24 = (bf16[64,2048]{1,0:T(8,128)(2,1)S(1)}, bf16[64,2048]{1,0:T(8,128)(2,1)S(1)}, u32[]{:S(2)}, u32[]{:S(2)}) collective-permute-start(bf16[64,2048]{1,0:T(8,128)(2,1)S(1)} %get-tuple-element.103), channel_id=1, source_target_pairs={{0,64},{8,24},{16,80},{24,40},{32,96},{40,56},{48,112},{56,8},{64,... | collective-permute-start | bytes 786440 | tf_op jit(solution)/shard_map/ppermute | solution.py:147
  16.8 1.9 %collective-permute-start.25 = (bf16[64,2048]{1,0:T(8,128)(2,1)S(1)}, bf16[64,2048]{1,0:T(8,128)(2,1)S(1)}, u32[]{:S(2)}, u32[]{:S(2)}) collective-permute-start(bf16[64,2048]{1,0:T(8,128)(2,1)S(1)} %get-tuple-element.103), channel_id=1, source_target_pairs={{0,192},{8,56},{16,208},{24,8},{32,224},{40,24},{48,240},{56,40},{... | collective-permute-start | bytes 786440 | tf_op jit(solution)/shard_map/ppermute | solution.py:147
  18.7 2.1 %collective-permute-start.26 = (bf16[64,2048]{1,0:T(8,128)(2,1)S(1)}, bf16[64,2048]{1,0:T(8,128)(2,1)S(1)}, u32[]{:S(2)}, u32[]{:S(2)}) collective-permute-start(bf16[64,2048]{1,0:T(8,128)(2,1)S(1)} %get-tuple-element.103), channel_id=1, source_target_pairs={{0,128},{8,40},{16,144},{24,56},{32,160},{40,8},{48,176},{56,24},{... | collective-permute-start | bytes 786440 | tf_op jit(solution)/shard_map/ppermute | solution.py:147
  20.7 2.2 %collective-permute-done.24 = bf16[64,2048]{1,0:T(8,128)(2,1)S(1)} collective-permute-done((bf16[64,2048]{1,0:T(8,128)(2,1)S(1)}, bf16[64,2048]{1,0:T(8,128)(2,1)S(1)}, u32[]{:S(2)}, u32[]{:S(2)}) %collective-permute-start.24) | collective-permute-done | bytes 262176 | tf_op jit(solution)/shard_map/ppermute | solution.py:147
  22.9 2.4 %collective-permute-done.25 = bf16[64,2048]{1,0:T(8,128)(2,1)S(1)} collective-permute-done((bf16[64,2048]{1,0:T(8,128)(2,1)S(1)}, bf16[64,2048]{1,0:T(8,128)(2,1)S(1)}, u32[]{:S(2)}, u32[]{:S(2)}) %collective-permute-start.25) | collective-permute-done | bytes 262176 | tf_op jit(solution)/shard_map/ppermute | solution.py:147
  25.4 1.8 %collective-permute-done.26 = bf16[64,2048]{1,0:T(8,128)(2,1)S(1)} collective-permute-done((bf16[64,2048]{1,0:T(8,128)(2,1)S(1)}, bf16[64,2048]{1,0:T(8,128)(2,1)S(1)}, u32[]{:S(2)}, u32[]{:S(2)}) %collective-permute-start.26) | collective-permute-done | bytes 262176 | tf_op jit(solution)/shard_map/ppermute | solution.py:147
  27.3 3.2 %collective-permute-start.28 = (bf16[112,640]{1,0:T(8,128)(2,1)S(1)}, bf16[112,640]{1,0:T(8,128)(2,1)S(1)}, u32[]{:S(2)}, u32[]{:S(2)}) collective-permute-start(bf16[112,640]{1,0:T(8,128)(2,1)S(1)} %copy-done.17), channel_id=1, source_target_pairs={{0,1},{1,2},{2,3},{3,4},{4,5},{5,6},{6,7},{7,0},{8,9},{9,10},{10,1... | collective-permute-start | bytes 430088 | tf_op jit(solution)/shard_map/ppermute | solution.py:172
  30.6 3.3 %collective-permute-start.29 = (bf16[112,640]{1,0:T(8,128)(2,1)S(1)}, bf16[112,640]{1,0:T(8,128)(2,1)S(1)}, u32[]{:S(2)}, u32[]{:S(2)}) collective-permute-start(bf16[112,640]{1,0:T(8,128)(2,1)S(1)} %copy-done.18), channel_id=1, source_target_pairs={{0,1},{1,2},{2,3},{3,4},{4,5},{5,6},{6,7},{7,0},{8,9},{9,10},{10,1... | collective-permute-start | bytes 430088 | tf_op jit(solution)/shard_map/ppermute | solution.py:172
  33.8 0.6 collective-permute-done.28.refs_2_
  34.5 3.7 %collective-permute-start.30 = (bf16[112,640]{1,0:T(8,128)(2,1)S(1)}, bf16[112,640]{1,0:T(8,128)(2,1)S(1)}, u32[]{:S(2)}, u32[]{:S(2)}) collective-permute-start(bf16[112,640]{1,0:T(8,128)(2,1)S(1)} %collective-permute-done.28.refs_2_), channel_id=1, source_target_pairs={{0,1},{1,2},{2,3},{3,4},{4,5},{5,6},{6,7},{7,0},{8,9},{9,10},{10,1... | collective-permute-start | bytes 430088 | tf_op jit(solution)/shard_map/ppermute | solution.py:172
  38.4 2.3 %collective-permute-done.39.refs_14_ = bf16[112,640]{1,0:T(8,128)(2,1)S(1)} collective-permute-done((bf16[112,640]{1,0:T(8,128)(2,1)S(1)}, bf16[112,640]{1,0:T(8,128)(2,1)S(1)}, u32[]{:S(2)}, u32[]{:S(2)}) %collective-permute-start.39) | collective-permute-done | bytes 143392 | tf_op jit(solution)/shard_map/ppermute | solution.py:173
  40.7 3.2 %collective-permute-start.31 = (bf16[112,640]{1,0:T(8,128)(2,1)S(1)}, bf16[112,640]{1,0:T(8,128)(2,1)S(1)}, u32[]{:S(2)}, u32[]{:S(2)}) collective-permute-start(bf16[112,640]{1,0:T(8,128)(2,1)S(1)} %collective-permute-done.29.refs_3_), channel_id=1, source_target_pairs={{0,1},{1,2},{2,3},{3,4},{4,5},{5,6},{6,7},{7,0},{8,9},{9,10},{10,1... | collective-permute-start | bytes 430088 | tf_op jit(solution)/shard_map/ppermute | solution.py:172
  44.5 1.2 %collective-permute-done.36.refs_13_ = bf16[112,640]{1,0:T(8,128)(2,1)S(1)} collective-permute-done((bf16[112,640]{1,0:T(8,128)(2,1)S(1)}, bf16[112,640]{1,0:T(8,128)(2,1)S(1)}, u32[]{:S(2)}, u32[]{:S(2)}) %collective-permute-start.36) | collective-permute-done | bytes 143392 | tf_op jit(solution)/shard_map/ppermute | solution.py:173
  45.9 2.6 %collective-permute-done.40.refs_12_ = bf16[112,640]{1,0:T(8,128)(2,1)S(1)} collective-permute-done((bf16[112,640]{1,0:T(8,128)(2,1)S(1)}, bf16[112,640]{1,0:T(8,128)(2,1)S(1)}, u32[]{:S(2)}, u32[]{:S(2)}) %collective-permute-start.40) | collective-permute-done | bytes 143392 | tf_op jit(solution)/shard_map/ppermute | solution.py:173
  48.6 3.2 %collective-permute-start.33 = (bf16[112,640]{1,0:T(8,128)(2,1)S(1)}, bf16[112,640]{1,0:T(8,128)(2,1)}, u32[]{:S(2)}, u32[]{:S(2)}) collective-permute-start(bf16[112,640]{1,0:T(8,128)(2,1)S(1)} %collective-permute-done.31.refs_5_), channel_id=1, source_target_pairs={{0,1},{1,2},{2,3},{3,4},{4,5},{5,6},{6,7},{7,0},{8,9},{9,10},{10,1... | collective-permute-start | bytes 430088 | tf_op jit(solution)/shard_map/ppermute | solution.py:172
  51.8 1.1 %collective-permute-start.34 = (bf16[112,640]{1,0:T(8,128)(2,1)S(1)}, bf16[112,640]{1,0:T(8,128)(2,1)}, u32[]{:S(2)}, u32[]{:S(2)}) collective-permute-start(bf16[112,640]{1,0:T(8,128)(2,1)S(1)} %collective-permute-done.32.refs_6_), channel_id=1, source_target_pairs={{0,1},{1,2},{2,3},{3,4},{4,5},{5,6},{6,7},{7,0},{8,9},{9,10},{10,1... | collective-permute-start | bytes 430088 | tf_op jit(solution)/shard_map/ppermute | solution.py:176
  53.3 0.6 collective-permute-start.38
  53.9 0.6 reshape.29.energy_row
  54.6 0.7 %reduce_max.9 = s32[]{:T(128)} reduce(s32[8]{0:T(128)S(1)} %convert_reduce_fusion, s32[]{:T(128)} %constant.5.clone.1), dimensions={0}, to_apply=%region_1.0 | reduce | flops 7 | bytes 40 | tf_op jit(solution)/shard_map/reduce_max | solution.py:207
  55.4 1.7 %collective-permute-done.34.refs_8_ = bf16[112,640]{1,0:T(8,128)(2,1)} collective-permute-done((bf16[112,640]{1,0:T(8,128)(2,1)S(1)}, bf16[112,640]{1,0:T(8,128)(2,1)}, u32[]{:S(2)}, u32[]{:S(2)}) %collective-permute-start.34) | collective-permute-done | bytes 143392 | tf_op jit(solution)/shard_map/ppermute | solution.py:176
  57.0 2.9 %collective-permute-done.38.refs_9_ = bf16[112,640]{1,0:T(8,128)(2,1)} collective-permute-done((bf16[112,640]{1,0:T(8,128)(2,1)}, bf16[112,640]{1,0:T(8,128)(2,1)}, u32[]{:S(2)}, u32[]{:S(2)}) %collective-permute-start.38) | collective-permute-done | bytes 143392 | tf_op jit(solution)/shard_map/ppermute | solution.py:176
  60.0 0.9 %copy-done.13 = bf16[256,2048]{1,0:T(8,128)(2,1)} copy-done((bf16[256,2048]{1,0:T(8,128)(2,1)}, bf16[256,2048]{1,0:T(8,128)(2,1)S(1)}, u32[]{:S(2)}) %copy-start.13) | copy-done | bytes 1048600
  60.9 4.8 %contract.2 = f32[512,640]{1,0:T(8,128)S(1)} custom-call(s32[640]{0:T(1024)S(1)} %copy-done.14, f32[640]{0:T(1024)S(1)} %copy-done.15, s32[64]{0:T(128)S(1)} %copy-done.16, f32[64]{0:T(128)S(1)} %copy-done.28, s32[2]{0:T(128)S(1)} %copy-done.29, s32[1,640]{1,0:T(1,128)} %reshape.28.irrep_row, f32[1,640]{1,0:T(1,128)} %reshape.29.energy_row, ...), custom_call_target="tpu_custom_call" | custom-call | tf_op jit(solution)/shard_map/contract/pallas_call | solution.py:183
  65.8 0.8 %while.11 = (s32[]{:T(128)}, f32[512,640]{1,0:T(8,128)S(1)}, s32[]{:T(128)}, s32[640]{0:T(1024)S(1)}, f32[640]{0:T(1024)S(1)}, /*index=5*/s32[64]{0:T(128)S(1)},...) while((s32[]{:T(128)}, f32[512,640]{1,0:T(8,128)S(1)}, ...), condition=%wide.wide.region_3.0_spmd, body=%wide.wide.region_2.0_spmd.sunk | while | flops 327682 | bytes 28263636 | solution.py:220
  66.6 1.0 %copy-done.1 = f32[512,640]{1,0:T(8,128)} copy-done((f32[512,640]{1,0:T(8,128)}, f32[512,640]{1,0:T(8,128)S(1)}, u32[]{:S(2)}) %copy-start.1) | copy-done | bytes 1310744
  (68 shorter events, 2.0 us)
Async XLA Ops:
  5.1 22.3 %copy-start.17 = (bf16[112,640]{1,0:T(8,128)(2,1)S(1)}, bf16[112,640]{1,0:T(8,128)(2,1)}, u32[]{:S(2)}) copy-start(bf16[112,640]{1,0:T(8,128)(2,1)} %get-tuple-element.70.refs_0_) | copy-start | bytes 430084
  5.1 25.5 %copy-start.18 = (bf16[112,640]{1,0:T(8,128)(2,1)S(1)}, bf16[112,640]{1,0:T(8,128)(2,1)}, u32[]{:S(2)}) copy-start(bf16[112,640]{1,0:T(8,128)(2,1)} %get-tuple-element.71.refs_1_) | copy-start | bytes 430084
  5.1 48.8 %copy-start.15 = (f32[640]{0:T(1024)S(1)}, f32[640]{0:T(1024)}, u32[]{:S(2)}) copy-start(f32[640]{0:T(1024)} %energy_s.1) | copy-start | bytes 7684
  5.1 49.4 %copy-start.14 = (s32[640]{0:T(1024)S(1)}, s32[640]{0:T(1024)}, u32[]{:S(2)}) copy-start(s32[640]{0:T(1024)} %irrep_s.3) | copy-start | bytes 7684
  5.1 55.8 %copy-start.16 = (s32[64]{0:T(128)S(1)}, s32[64]{0:T(128)}, u32[]{:S(2)}) copy-start(s32[64]{0:T(128)} %occ_irrep_s.1) | copy-start | bytes 772
  5.1 55.8 %copy-start.28 = (f32[64]{0:T(128)S(1)}, f32[64]{0:T(128)}, u32[]{:S(2)}) copy-start(f32[64]{0:T(128)} %occ_energy_s.1) | copy-start | bytes 772
  5.1 55.8 %copy-start.29 = (s32[2]{0:T(128)S(1)}, s32[2]{0:T(128)}, u32[]{:S(2)}) copy-start(s32[2]{0:T(128)} %tiles_a_s.3) | copy-start | bytes 28
  5.1 10.0 %collective-permute-start.23 = (bf16[16,2048]{1,0:T(8,128)(2,1)}, bf16[16,2048]{1,0:T(8,128)(2,1)S(1)}, u32[]{:S(2)}, u32[]{:S(2)}) collective-permute-start(bf16[16,2048]{1,0:T(8,128)(2,1)} %get-tuple-element.69), channel_id=1, source_target_pairs={{0,32},{8,136},{16,48},{24,152},{32,0},{40,168},{48,16},{56,184},{... | collective-permute-start | bytes 196616 | tf_op jit(solution)/shard_map/ppermute | solution.py:147
  8.2 6.8 %collective-permute-start.22 = (bf16[16,2048]{1,0:T(8,128)(2,1)}, bf16[16,2048]{1,0:T(8,128)(2,1)S(1)}, u32[]{:S(2)}, u32[]{:S(2)}) collective-permute-start(bf16[16,2048]{1,0:T(8,128)(2,1)} %get-tuple-element.69), channel_id=1, source_target_pairs={{0,48},{8,200},{16,0},{24,216},{32,16},{40,232},{48,32},{56,248},{... | collective-permute-start | bytes 196616 | tf_op jit(solution)/shard_map/ppermute | solution.py:147
  9.4 5.7 %collective-permute-start.21 = (bf16[16,2048]{1,0:T(8,128)(2,1)}, bf16[16,2048]{1,0:T(8,128)(2,1)S(1)}, u32[]{:S(2)}, u32[]{:S(2)}) collective-permute-start(bf16[16,2048]{1,0:T(8,128)(2,1)} %get-tuple-element.69), channel_id=1, source_target_pairs={{0,16},{8,72},{16,32},{24,88},{32,48},{40,104},{48,0},{56,120},{64... | collective-permute-start | bytes 196616 | tf_op jit(solution)/shard_map/ppermute | solution.py:147
  15.1 7.8 %collective-permute-start.24 = (bf16[64,2048]{1,0:T(8,128)(2,1)S(1)}, bf16[64,2048]{1,0:T(8,128)(2,1)S(1)}, u32[]{:S(2)}, u32[]{:S(2)}) collective-permute-start(bf16[64,2048]{1,0:T(8,128)(2,1)S(1)} %get-tuple-element.103), channel_id=1, source_target_pairs={{0,64},{8,24},{16,80},{24,40},{32,96},{40,56},{48,112},{56,8},{64,... | collective-permute-start | bytes 786440 | tf_op jit(solution)/shard_map/ppermute | solution.py:147
  16.8 8.6 %collective-permute-start.25 = (bf16[64,2048]{1,0:T(8,128)(2,1)S(1)}, bf16[64,2048]{1,0:T(8,128)(2,1)S(1)}, u32[]{:S(2)}, u32[]{:S(2)}) collective-permute-start(bf16[64,2048]{1,0:T(8,128)(2,1)S(1)} %get-tuple-element.103), channel_id=1, source_target_pairs={{0,192},{8,56},{16,208},{24,8},{32,224},{40,24},{48,240},{56,40},{... | collective-permute-start | bytes 786440 | tf_op jit(solution)/shard_map/ppermute | solution.py:147
  18.7 8.5 %collective-permute-start.26 = (bf16[64,2048]{1,0:T(8,128)(2,1)S(1)}, bf16[64,2048]{1,0:T(8,128)(2,1)S(1)}, u32[]{:S(2)}, u32[]{:S(2)}) collective-permute-start(bf16[64,2048]{1,0:T(8,128)(2,1)S(1)} %get-tuple-element.103), channel_id=1, source_target_pairs={{0,128},{8,40},{16,144},{24,56},{32,160},{40,8},{48,176},{56,24},{... | collective-permute-start | bytes 786440 | tf_op jit(solution)/shard_map/ppermute | solution.py:147
  27.2 32.7 %copy-start.12 = (bf16[256,2048]{1,0:T(8,128)(2,1)}, bf16[256,2048]{1,0:T(8,128)(2,1)S(1)}, u32[]{:S(2)}) copy-start(bf16[256,2048]{1,0:T(8,128)(2,1)S(1)} %constant_dynamic-update-slice_fusion.15.own) | copy-start | bytes 3145732
  27.2 32.7 %collective-permute-start.27 = (bf16[256,2048]{1,0:T(8,128)(2,1)S(1)}, bf16[256,2048]{1,0:T(8,128)(2,1)S(1)}, u32[]{:S(2)}, u32[]{:S(2)}) collective-permute-start(bf16[256,2048]{1,0:T(8,128)(2,1)S(1)} %constant_dynamic-update-slice_fusion.15.own), channel_id=1, source_target_pairs={{0,8},{8,0},{16,24},{24,16},{32,40},{40,32},{48,56},{56,48},{64,72... | collective-permute-start | bytes 3145736 | tf_op jit(solution)/shard_map/ppermute | solution.py:181
  27.3 7.1 %collective-permute-start.28 = (bf16[112,640]{1,0:T(8,128)(2,1)S(1)}, bf16[112,640]{1,0:T(8,128)(2,1)S(1)}, u32[]{:S(2)}, u32[]{:S(2)}) collective-permute-start(bf16[112,640]{1,0:T(8,128)(2,1)S(1)} %copy-done.17), channel_id=1, source_target_pairs={{0,1},{1,2},{2,3},{3,4},{4,5},{5,6},{6,7},{7,0},{8,9},{9,10},{10,1... | collective-permute-start | bytes 430088 | tf_op jit(solution)/shard_map/ppermute | solution.py:172
  30.5 7.8 %collective-permute-start.35 = (bf16[112,640]{1,0:T(8,128)(2,1)S(1)}, bf16[112,640]{1,0:T(8,128)(2,1)S(1)}, u32[]{:S(2)}, u32[]{:S(2)}) collective-permute-start(bf16[112,640]{1,0:T(8,128)(2,1)S(1)} %copy-done.18), channel_id=1, source_target_pairs={{0,7},{1,0},{2,1},{3,2},{4,3},{5,4},{6,5},{7,6},{8,15},{9,8},{10,9... | collective-permute-start | bytes 430088 | tf_op jit(solution)/shard_map/ppermute | solution.py:173
  30.6 10.1 %collective-permute-start.39 = (bf16[112,640]{1,0:T(8,128)(2,1)S(1)}, bf16[112,640]{1,0:T(8,128)(2,1)S(1)}, u32[]{:S(2)}, u32[]{:S(2)}) collective-permute-start(bf16[112,640]{1,0:T(8,128)(2,1)S(1)} %copy-done.17), channel_id=1, source_target_pairs={{0,7},{1,0},{2,1},{3,2},{4,3},{5,4},{6,5},{7,6},{8,15},{9,8},{10,9... | collective-permute-start | bytes 430088 | tf_op jit(solution)/shard_map/ppermute | solution.py:173
  30.6 10.1 %collective-permute-start.29 = (bf16[112,640]{1,0:T(8,128)(2,1)S(1)}, bf16[112,640]{1,0:T(8,128)(2,1)S(1)}, u32[]{:S(2)}, u32[]{:S(2)}) collective-permute-start(bf16[112,640]{1,0:T(8,128)(2,1)S(1)} %copy-done.18), channel_id=1, source_target_pairs={{0,1},{1,2},{2,3},{3,4},{4,5},{5,6},{6,7},{7,0},{8,9},{9,10},{10,1... | collective-permute-start | bytes 430088 | tf_op jit(solution)/shard_map/ppermute | solution.py:172
  34.4 25.5 %copy-start.19 = (bf16[112,640]{1,0:T(8,128)(2,1)}, bf16[112,640]{1,0:T(8,128)(2,1)S(1)}, u32[]{:S(2)}) copy-start(bf16[112,640]{1,0:T(8,128)(2,1)S(1)} %collective-permute-done.28.refs_2_) | copy-start | bytes 430084
  34.5 9.4 %collective-permute-start.30 = (bf16[112,640]{1,0:T(8,128)(2,1)S(1)}, bf16[112,640]{1,0:T(8,128)(2,1)S(1)}, u32[]{:S(2)}, u32[]{:S(2)}) collective-permute-start(bf16[112,640]{1,0:T(8,128)(2,1)S(1)} %collective-permute-done.28.refs_2_), channel_id=1, source_target_pairs={{0,1},{1,2},{2,3},{3,4},{4,5},{5,6},{6,7},{7,0},{8,9},{9,10},{10,1... | collective-permute-start | bytes 430088 | tf_op jit(solution)/shard_map/ppermute | solution.py:172
  38.4 21.6 %copy-start.20 = (bf16[112,640]{1,0:T(8,128)(2,1)}, bf16[112,640]{1,0:T(8,128)(2,1)S(1)}, u32[]{:S(2)}) copy-start(bf16[112,640]{1,0:T(8,128)(2,1)S(1)} %collective-permute-done.35.refs_15_) | copy-start | bytes 430084
  38.4 7.3 %collective-permute-start.36 = (bf16[112,640]{1,0:T(8,128)(2,1)S(1)}, bf16[112,640]{1,0:T(8,128)(2,1)S(1)}, u32[]{:S(2)}, u32[]{:S(2)}) collective-permute-start(bf16[112,640]{1,0:T(8,128)(2,1)S(1)} %collective-permute-done.35.refs_15_), channel_id=1, source_target_pairs={{0,7},{1,0},{2,1},{3,2},{4,3},{5,4},{6,5},{7,6},{8,15},{9,8},{10,9... | collective-permute-start | bytes 430088 | tf_op jit(solution)/shard_map/ppermute | solution.py:173
  40.6 19.3 %copy-start.21 = (bf16[112,640]{1,0:T(8,128)(2,1)}, bf16[112,640]{1,0:T(8,128)(2,1)S(1)}, u32[]{:S(2)}) copy-start(bf16[112,640]{1,0:T(8,128)(2,1)S(1)} %collective-permute-done.39.refs_14_) | copy-start | bytes 430084
  40.6 7.9 %collective-permute-start.40 = (bf16[112,640]{1,0:T(8,128)(2,1)S(1)}, bf16[112,640]{1,0:T(8,128)(2,1)S(1)}, u32[]{:S(2)}, u32[]{:S(2)}) collective-permute-start(bf16[112,640]{1,0:T(8,128)(2,1)S(1)} %collective-permute-done.39.refs_14_), channel_id=1, source_target_pairs={{0,7},{1,0},{2,1},{3,2},{4,3},{5,4},{6,5},{7,6},{8,15},{9,8},{10,9... | collective-permute-start | bytes 430088 | tf_op jit(solution)/shard_map/ppermute | solution.py:173
  40.7 7.9 %collective-permute-start.31 = (bf16[112,640]{1,0:T(8,128)(2,1)S(1)}, bf16[112,640]{1,0:T(8,128)(2,1)S(1)}, u32[]{:S(2)}, u32[]{:S(2)}) collective-permute-start(bf16[112,640]{1,0:T(8,128)(2,1)S(1)} %collective-permute-done.29.refs_3_), channel_id=1, source_target_pairs={{0,1},{1,2},{2,3},{3,4},{4,5},{5,6},{6,7},{7,0},{8,9},{9,10},{10,1... | collective-permute-start | bytes 430088 | tf_op jit(solution)/shard_map/ppermute | solution.py:172
  43.9 7.9 %collective-permute-start.32 = (bf16[112,640]{1,0:T(8,128)(2,1)S(1)}, bf16[112,640]{1,0:T(8,128)(2,1)S(1)}, u32[]{:S(2)}, u32[]{:S(2)}) collective-permute-start(bf16[112,640]{1,0:T(8,128)(2,1)S(1)} %collective-permute-done.30.refs_4_), channel_id=1, source_target_pairs={{0,1},{1,2},{2,3},{3,4},{4,5},{5,6},{6,7},{7,0},{8,9},{9,10},{10,1... | collective-permute-start | bytes 430088 | tf_op jit(solution)/shard_map/ppermute | solution.py:172
  45.6 7.6 %collective-permute-start.37 = (bf16[112,640]{1,0:T(8,128)(2,1)S(1)}, bf16[112,640]{1,0:T(8,128)(2,1)}, u32[]{:S(2)}, u32[]{:S(2)}) collective-permute-start(bf16[112,640]{1,0:T(8,128)(2,1)S(1)} %collective-permute-done.36.refs_13_), channel_id=1, source_target_pairs={{0,7},{1,0},{2,1},{3,2},{4,3},{5,4},{6,5},{7,6},{8,15},{9,8},{10,9... | collective-permute-start | bytes 430088 | tf_op jit(solution)/shard_map/ppermute | solution.py:173
  48.6 6.8 %collective-permute-start.41 = (bf16[112,640]{1,0:T(8,128)(2,1)S(1)}, bf16[112,640]{1,0:T(8,128)(2,1)}, u32[]{:S(2)}, u32[]{:S(2)}) collective-permute-start(bf16[112,640]{1,0:T(8,128)(2,1)S(1)} %collective-permute-done.40.refs_12_), channel_id=1, source_target_pairs={{0,7},{1,0},{2,1},{3,2},{4,3},{5,4},{6,5},{7,6},{8,15},{9,8},{10,9... | collective-permute-start | bytes 430088 | tf_op jit(solution)/shard_map/ppermute | solution.py:173
  48.6 6.8 %collective-permute-start.33 = (bf16[112,640]{1,0:T(8,128)(2,1)S(1)}, bf16[112,640]{1,0:T(8,128)(2,1)}, u32[]{:S(2)}, u32[]{:S(2)}) collective-permute-start(bf16[112,640]{1,0:T(8,128)(2,1)S(1)} %collective-permute-done.31.refs_5_), channel_id=1, source_target_pairs={{0,1},{1,2},{2,3},{3,4},{4,5},{5,6},{6,7},{7,0},{8,9},{9,10},{10,1... | collective-permute-start | bytes 430088 | tf_op jit(solution)/shard_map/ppermute | solution.py:172
  51.8 5.2 %collective-permute-start.34 = (bf16[112,640]{1,0:T(8,128)(2,1)S(1)}, bf16[112,640]{1,0:T(8,128)(2,1)}, u32[]{:S(2)}, u32[]{:S(2)}) collective-permute-start(bf16[112,640]{1,0:T(8,128)(2,1)S(1)} %collective-permute-done.32.refs_6_), channel_id=1, source_target_pairs={{0,1},{1,2},{2,3},{3,4},{4,5},{5,6},{6,7},{7,0},{8,9},{9,10},{10,1... | collective-permute-start | bytes 430088 | tf_op jit(solution)/shard_map/ppermute | solution.py:176
  53.3 6.6 %collective-permute-start.38 = (bf16[112,640]{1,0:T(8,128)(2,1)}, bf16[112,640]{1,0:T(8,128)(2,1)}, u32[]{:S(2)}, u32[]{:S(2)}) collective-permute-start(bf16[112,640]{1,0:T(8,128)(2,1)} %collective-permute-done.37.refs_11_), channel_id=1, source_target_pairs={{0,7},{1,0},{2,1},{3,2},{4,3},{5,4},{6,5},{7,6},{8,15},{9,8},{10,9... | collective-permute-start | bytes 430088 | tf_op jit(solution)/shard_map/ppermute | solution.py:176
  (10 other events, 93.3 us)

commit v3 on v2

v3 whole, which is shorter than its diff:
```python
import jax
import jax.numpy as jnp
from jax import lax
from jax.experimental import pallas as pl
from jax.experimental.pallas import tpu as pltpu
from jax.sharding import PartitionSpec as P

TILE = 16
NVIR = 640
NOCC = 64
IRREPS = 8
CAP = 112
PITCH = 128
E_LOCAL = 2
RING = 8
SIDE = 4
ROWS = 16

SMEM = pl.BlockSpec(memory_space=pltpu.SMEM)
VMEM = pl.BlockSpec(memory_space=pltpu.VMEM)
ANY = pl.BlockSpec(memory_space=pl.ANY)
HBM = pl.BlockSpec(memory_space=pltpu.HBM)


def params(mib):
    return pltpu.CompilerParams(vmem_limit_bytes=mib * 1024 * 1024)


def pack_integrals(
    base_s, irrep_s, tiles_e_s, tiles_a_s, irrep_ref, panel_hbm,
    strip_ref, picks_ref, most_s, panel_ref, arrived,
):
    fetches = [
        pltpu.make_async_copy(
            panel_hbm.at[pl.ds(local * NVIR, NVIR), :], panel_ref.at[local], arrived.at[local]
        )
        for local in range(E_LOCAL)
    ]
    for fetch in fetches:
        fetch.start()
    wide, narrow = lax.axis_index("wide"), lax.axis_index("narrow")
    irreps = irrep_ref[...].reshape(1, NVIR)
    group = lax.broadcasted_iota(jnp.int32, (IRREPS, NVIR), 0)
    member = irreps == group
    earlier = lax.broadcasted_iota(jnp.int32, (NVIR, NVIR), 0) < lax.broadcasted_iota(
        jnp.int32, (NVIR, NVIR), 1
    )
    before = jnp.dot(
        member.astype(jnp.bfloat16),
        earlier.astype(jnp.bfloat16),
        preferred_element_type=jnp.float32,
    )
    rank = jnp.sum(jnp.where(member, before, 0.0), axis=0, keepdims=True).astype(jnp.int32)
    most_s[0] = jnp.max(rank) + 1
    slots = lax.broadcasted_iota(jnp.int32, (PITCH, NVIR), 0)
    picks = ((slots == rank - base_s[0]) & (slots < CAP)).astype(jnp.bfloat16)
    picks_ref[...] = picks

    a = tiles_a_s[wide // TILE] * TILE + wide % TILE
    labels = jnp.broadcast_to(irreps, (PITCH, NVIR)).astype(jnp.float32)
    label_col = jnp.transpose(labels).astype(jnp.bfloat16)
    for local in range(E_LOCAL):
        e = tiles_e_s[0] * TILE + narrow * E_LOCAL + local
        wanted = (irreps ^ (irrep_s[a] ^ irrep_s[e])).astype(jnp.float32).astype(jnp.bfloat16)
        fetches[local].wait()
        for tile in range(NVIR // PITCH):
            lanes = slice(tile * PITCH, (tile + 1) * PITCH)
            held = panel_ref[local, :, lanes]
            kept = jnp.where(label_col == wanted[:, lanes], held, jnp.zeros_like(held))
            strip_ref[local * CAP:(local + 1) * CAP, lanes] = jnp.dot(
                picks[:CAP, :], kept, preferred_element_type=jnp.float32
            ).astype(strip_ref.dtype)


def pack_amplitudes(irrep_s, occ_s, tiles_e_s, irrep_ref, picks_ref, rows_ref, out_ref, stacked):
    wide, narrow = lax.axis_index("wide"), lax.axis_index("narrow")
    irreps = irrep_ref[...].reshape(1, NVIR)
    first = (narrow * 32 + wide) * ROWS
    line = lax.broadcasted_iota(jnp.int32, (ROWS, NVIR), 0)
    occ = jnp.zeros((ROWS, NVIR), jnp.int32)
    for row in range(ROWS):
        pair = first + row
        occ = jnp.where(line == row, occ_s[pair // NOCC] ^ occ_s[pair % NOCC], occ)
    kin = (occ ^ irreps).astype(jnp.float32).astype(jnp.bfloat16)
    for e in range(TILE):
        held = rows_ref[:, e * NVIR:(e + 1) * NVIR]
        label = irrep_s[tiles_e_s[0] * TILE + e].astype(jnp.float32).astype(jnp.bfloat16)
        stacked[e * ROWS:(e + 1) * ROWS, :] = jnp.where(kin == label, held, jnp.zeros_like(held))
    picked = lax.dot_general(
        stacked[...], picks_ref[...], (((1,), (1,)), ((), ())), preferred_element_type=jnp.float32
    ).astype(out_ref.dtype)
    for e in range(TILE):
        out_ref[:, e * PITCH:(e + 1) * PITCH] = picked[e * ROWS:(e + 1) * ROWS, :]


def stack(parts, after=()):
    height, width = parts[0].shape

    def place(*refs):
        for index in range(len(parts)):
            refs[-1][index * height:(index + 1) * height, :] = refs[index][...]

    return pl.pallas_call(
        place,
        out_shape=jax.ShapeDtypeStruct((len(parts) * height, width), parts[0].dtype),
        in_specs=[VMEM] * len(parts) + [ANY] * len(after),
        out_specs=VMEM,
        compiler_params=params(6),
        name="stack",
    )(*parts, *after)


def as_column(row):
    width = row.shape[1]
    across = lax.broadcasted_iota(jnp.int32, (width, width), 1)
    down = lax.broadcasted_iota(jnp.int32, (width, width), 0)
    return jnp.sum(jnp.where(across == down, row, jnp.zeros_like(row)), axis=1, keepdims=True)


def reach(index):
    return (0, -1, 1, 2)[index]


def fill(panel, strips):
    blank = jnp.zeros((PITCH - CAP, NVIR), panel.dtype)
    for index, strip in enumerate(strips):
        for local in range(E_LOCAL):
            start = (index * E_LOCAL + local) * PITCH
            panel[start:start + CAP, :] = strip[local * CAP:(local + 1) * CAP, :]
            panel[start + CAP:start + PITCH, :] = blank


def columns_of(amplitudes, step):
    way = 1 - 2 * (lax.axis_index("wide") % 2)
    source = (lax.axis_index("narrow") - way * step + RING) % RING
    start = pl.multiple_of(source * E_LOCAL * PITCH, E_LOCAL * PITCH)
    return amplitudes[:, pl.ds(start, E_LOCAL * PITCH)]


def contract_early(steps, late_steps, other, own, twin, *refs):
    strips, (sum_ref, late_ref, amplitudes, ordered, panel) = refs[:-5], refs[-5:]
    wide = lax.axis_index("wide")
    y, x, core = wide // 8, wide // 2 % SIDE, wide % 2
    for ref, side in ((own, core), (twin, 1 - core)):
        for outer in range(SIDE):
            for inner in range(SIDE):
                dx = jnp.where(side == 0, reach(inner), reach(outer))
                dy = jnp.where(side == 0, reach(outer), reach(inner))
                place = (y + dy + SIDE) % SIDE * 8 + (x + dx + SIDE) % SIDE * 2 + side
                block = (outer * SIDE + inner) * ROWS
                amplitudes[pl.ds(pl.multiple_of(place * ROWS, ROWS), ROWS), :] = ref[
                    block:block + ROWS, :
                ]
    span = E_LOCAL * PITCH
    for index, step in enumerate(late_steps):
        late_ref[:, index * span:(index + 1) * span] = columns_of(amplitudes, step)
    for index, step in enumerate(steps):
        ordered[:, index * span:(index + 1) * span] = columns_of(amplitudes, step)
    fill(panel, strips)
    sum_ref[...] = other[...].astype(jnp.float32) + jnp.dot(
        ordered[...], panel[...], preferred_element_type=jnp.float32
    )


def contract_late(
    irrep_s, energy_s, occ_irrep_s, occ_energy_s, tiles_a_s,
    irrep_ref, energy_ref, occ_irrep_ref, occ_energy_ref, sum_ref, late, *refs,
):
    strips, (out_hbm, panel, out, left) = refs[:-4], refs[-4:]
    wide, narrow = lax.axis_index("wide"), lax.axis_index("narrow")
    fill(panel, strips)
    a = tiles_a_s[wide // TILE] * TILE + wide % TILE
    col_sym = irrep_ref[...].reshape(1, NVIR) ^ irrep_s[a]
    col_energy = energy_s[a] + energy_ref[...].reshape(1, NVIR)
    j_sym = as_column(occ_irrep_ref[...].reshape(1, NOCC))
    j_energy = as_column(occ_energy_ref[...].reshape(1, NOCC))
    i_count = out.shape[0] // NOCC
    out[...] = jnp.dot(late[...], panel[...], preferred_element_type=jnp.float32)
    copies = []
    for local in range(i_count):
        i = narrow * i_count + local
        rows = slice(local * NOCC, (local + 1) * NOCC)
        summed = out[rows, :] + sum_ref[rows, :]
        denom = (occ_energy_s[i] + j_energy) - col_energy
        same = (j_sym ^ occ_irrep_s[i]) == col_sym
        out[rows, :] = jnp.where(same, summed / denom, 0.0)
        copies.append(
            pltpu.make_async_copy(out.at[rows, :], out_hbm.at[rows, :], left.at[local])
        )
        copies[-1].start()
    for copy in copies:
        copy.wait()


def along_ring():
    pairs = []
    for wide in range(32):
        for n in range(RING):
            to = (n + (1 if wide % 2 == 0 else -1)) % RING
            pairs.append((wide * RING + n, wide * RING + to))
    return pairs


def plane(along_x, along_y):
    pairs = []
    for i in range(32):
        y, x, core = i // 8, i // 2 % SIDE, i % 2
        dx, dy = (along_x, along_y) if core == 0 else (along_y, along_x)
        pairs.append((i, (y + dy) % SIDE * 8 + (x + dx) % SIDE * 2 + core))
    return pairs


def hop(part):
    return lax.ppermute(part, ("wide", "narrow"), along_ring())


def swap(part):
    return lax.ppermute(part, "wide", [(i, i ^ 1) for i in range(32)])


def spread(block, steps, after=()):
    return stack([block] + [lax.ppermute(block, "wide", pairs) for pairs in steps], after)


def one_pass(
    base, amplitudes, integrals, other_terms,
    occ_energy, virt_energy, occ_irrep, virt_irrep, tiles_e, tiles_a,
):
    span = E_LOCAL * PITCH
    height = other_terms.shape[0]
    mine, picks, most = pl.pallas_call(
        pack_integrals,
        out_shape=(
            jax.ShapeDtypeStruct((E_LOCAL * CAP, NVIR), integrals.dtype),
            jax.ShapeDtypeStruct((PITCH, NVIR), jnp.bfloat16),
            jax.ShapeDtypeStruct((1,), jnp.int32),
        ),
        in_specs=[SMEM] * 4 + [VMEM, ANY],
        out_specs=(VMEM, VMEM, SMEM),
        scratch_shapes=[
            pltpu.VMEM((E_LOCAL, NVIR, NVIR), integrals.dtype),
            pltpu.SemaphoreType.DMA((E_LOCAL,)),
        ],
        compiler_params=params(8),
        name="pack_integrals",
    )(base, virt_irrep, tiles_e, tiles_a, virt_irrep, integrals)
    block = pl.pallas_call(
        pack_amplitudes,
        out_shape=jax.ShapeDtypeStruct((ROWS, TILE * PITCH), amplitudes.dtype),
        in_specs=[SMEM] * 3 + [VMEM] * 3,
        out_specs=VMEM,
        scratch_shapes=[pltpu.VMEM((TILE * ROWS, NVIR), amplitudes.dtype)],
        compiler_params=params(6),
        name="pack_amplitudes",
    )(virt_irrep, occ_irrep, tiles_e, virt_irrep, picks, amplitudes)

    strips = [mine]
    twins = swap(mine)
    rounds = []
    for _ in range(RING // 2 - 1):
        mine, twins = hop(mine), hop(twins)
        rounds.append((mine, twins))
        strips += [mine, swap(twins)]
    strips.append(hop(mine))

    own = spread(block, [plane(1, 0), plane(-1, 0), plane(2, 0)], rounds[0])
    own = spread(own, [plane(0, 1), plane(0, -1), plane(0, 2)], rounds[1])
    twin = swap(own)

    steps = [0] + [sign * r for r in range(1, RING // 2) for sign in (1, -1)] + [RING // 2]
    early = 5
    sums, late = pl.pallas_call(
        lambda *refs: contract_early(steps[:early], steps[early:], *refs),
        out_shape=(
            jax.ShapeDtypeStruct(other_terms.shape, jnp.float32),
            jax.ShapeDtypeStruct((height, (RING - early) * span), amplitudes.dtype),
        ),
        in_specs=[VMEM] * (3 + early),
        out_specs=(VMEM, VMEM),
        scratch_shapes=[
            pltpu.VMEM((height, RING * span), amplitudes.dtype),
            pltpu.VMEM((height, early * span), amplitudes.dtype),
            pltpu.VMEM((early * span, NVIR), integrals.dtype),
        ],
        compiler_params=params(20),
        name="contract_early",
    )(other_terms, own, twin, *strips[:early])
    updated = pl.pallas_call(
        contract_late,
        out_shape=jax.ShapeDtypeStruct(other_terms.shape, jnp.float32),
        in_specs=[SMEM] * 5 + [VMEM] * (6 + RING - early),
        out_specs=HBM,
        scratch_shapes=[
            pltpu.VMEM(((RING - early) * span, NVIR), integrals.dtype),
            pltpu.VMEM(other_terms.shape, jnp.float32),
            pltpu.SemaphoreType.DMA((height // NOCC,)),
        ],
        compiler_params=params(16),
        name="contract_late",
    )(
        virt_irrep, virt_energy, occ_irrep, occ_energy, tiles_a,
        virt_irrep, virt_energy, occ_irrep, occ_energy, sums, late, *strips[early:],
    )
    return updated, most[0]


def shards(amplitudes, integrals, other_terms, *tables):
    def more(state):
        return state[0] < state[2]

    def add_pass(state):
        base, total, most = state
        part, _ = one_pass(
            base.reshape(1), amplitudes, integrals, jnp.zeros_like(other_terms), *tables
        )
        return base + CAP, total + part, most

    whole, most = one_pass(
        jnp.zeros((1,), jnp.int32), amplitudes, integrals, other_terms, *tables
    )
    return lax.while_loop(more, add_pass, (jnp.int32(CAP), whole, most))[1]


def solution(mesh):
    in_specs = (
        P(("narrow", "wide"), None),
        P("narrow", "wide"),
        P("narrow", "wide"),
        P(),
        P(),
        P(),
        P(),
        P(),
        P(),
    )
    out_specs = P("narrow", "wide")
    return jax.shard_map(shards, mesh=mesh, in_specs=in_specs, out_specs=out_specs, check_vma=False)
```

time: 67.9 us -> 51.6 us (0.76)
  the two profiles are of different devices: /device:TPU:96 before, /device:TPU:1 now
where the time goes in v3:
time: 51.6 us; the launch traced here: 51.4 us
  starting transfers between devices  30.6 us (59%)
  Pallas kernels  9.75 us (19%)
  waiting for transfers between devices  8 us (16%)
  between operations  1.09 us (2%)
  local copies, waits for them, and re-layouts  1 us (2%)
  loops' own time  0.94 us (2%)
    ppermute x7, starting transfers between devices, hop(): return lax.ppermute(part, ('wide', 'narrow'), along_ring())  15.2 us
    ppermute x6, starting transfers between devices, spread(): lax.ppermute(block, 'wide', pairs)  8.79 us
    ppermute x5, starting transfers between devices, swap(): return lax.ppermute(part, 'wide', [(i, i ^ 1) for i in range(32)])  6.67 us
    ppermute x6, waiting for transfers between devices, spread(): lax.ppermute(block, 'wide', pairs)  6.41 us
    pallas_call x1, Pallas kernels, one_pass(): pl.pallas_call(contract_late, out_shape=jax.ShapeDtypeStruct(other_terms....  3.3 us
    pallas_call x1, Pallas kernels, one_pass(): pl.pallas_call(pack_integrals, out_shape=(jax.ShapeDtypeStruct((E_LOCAL *...  2.82 us
    pallas_call x1, Pallas kernels, one_pass(): pl.pallas_call(lambda *refs: contract_early(steps[:early], steps[early:],...  2.61 us
    ppermute x7, waiting for transfers between devices, hop(): return lax.ppermute(part, ('wide', 'narrow'), along_ring())  1.58 us
  transfers between devices with their start and end apart: 18, of which 3 were waited for; matrix products, arithmetic and copies ran while one was open for 0% of the time, Pallas kernels for 7%

profile of v3, /device:TPU:1, one launch (start us, length us, event | category | flops | bytes accessed | tf_op | source)
XLA Modules:
  0.0 51.4 jit_solution(3865250158437292125)
XLA Ops:
  0.7 2.8 %pack_integrals.2 = (bf16[224,640]{1,0:T(8,128)(2,1)S(1)}, bf16[128,640]{1,0:T(8,128)(2,1)S(1)}, s32[1]{0:T(128)}) custom-call(s32[1]{0:T(128)} %constant.3.clone.1.base_s, s32[640]{0:T(1024)} %irrep_ref.5, s32[1]{0:T(128)S(6)} %copy.16.tiles_e_s, s32[2]{0:T(128)} %tiles_a_s.3, s32[640]{0:T(1024)} %irrep_ref.5, bf16[1280,640]{1,0:T(8,128)(2,1)} %panel_hbm.1), custom_call_target="tpu_custom_call" | custom-call | tf_op jit(solution)/shard_map/pack_integrals/pallas_call | solution.py:231
  3.5 0.0 copy-start.1
  3.5 3.3 %collective-permute-start.22 = (bf16[224,640]{1,0:T(8,128)(2,1)S(1)}, bf16[224,640]{1,0:T(8,128)(2,1)S(1)}, u32[]{:S(2)}, u32[]{:S(2)}) collective-permute-start(bf16[224,640]{1,0:T(8,128)(2,1)S(1)} %get-tuple-element.73.refs_3_), channel_id=1, source_target_pairs={{0,8},{8,0},{16,24},{24,16},{32,40},{40,32},{48,56},{56,48},{64,72... | collective-permute-start | bytes 860168 | tf_op jit(solution)/shard_map/ppermute | solution.py:218
  6.9 3.8 %collective-permute-start.21 = (bf16[224,640]{1,0:T(8,128)(2,1)S(1)}, bf16[224,640]{1,0:T(8,128)(2,1)S(1)}, u32[]{:S(2)}, u32[]{:S(2)}) collective-permute-start(bf16[224,640]{1,0:T(8,128)(2,1)S(1)} %get-tuple-element.73.refs_3_), channel_id=1, source_target_pairs={{0,1},{1,2},{2,3},{3,4},{4,5},{5,6},{6,7},{7,0},{8,15},{9,8},{10,9... | collective-permute-start | bytes 860168 | tf_op jit(solution)/shard_map/ppermute | solution.py:214
  10.7 1.2 %collective-permute-start.23 = (bf16[224,640]{1,0:T(8,128)(2,1)S(1)}, bf16[224,640]{1,0:T(8,128)(2,1)}, u32[]{:S(2)}, u32[]{:S(2)}) collective-permute-start(bf16[224,640]{1,0:T(8,128)(2,1)S(1)} %collective-permute-done.22), channel_id=1, source_target_pairs={{0,1},{1,2},{2,3},{3,4},{4,5},{5,6},{6,7},{7,0},{8,15},{9,8},{10,9... | collective-permute-start | bytes 860168 | tf_op jit(solution)/shard_map/ppermute | solution.py:214
  11.9 0.9 %pack_amplitudes.2.refs_0_ = bf16[16,2048]{1,0:T(8,128)(2,1)S(1)} custom-call(s32[640]{0:T(1024)S(1)} %copy-done.8, s32[64]{0:T(128)S(1)} %copy-done.10, s32[1]{0:T(128)S(6)} %copy.16.tiles_e_s, s32[640]{0:T(1024)S(1)} %copy-done.8, bf16[128,640]{1,0:T(8,128)(2,1)S(1)} %get-tuple-element.72.picks_ref, bf16[16,10240]{1,0:T(8,128)(2,1)S(1)} %copy-done.5), custom_call_target="tpu_custom_call" | custom-call | tf_op jit(solution)/shard_map/pack_amplitudes/pallas_call | solution.py:247
  12.9 1.4 %collective-permute-start.18 = (bf16[16,2048]{1,0:T(8,128)(2,1)S(1)}, bf16[16,2048]{1,0:T(8,128)(2,1)S(1)}, u32[]{:S(2)}, u32[]{:S(2)}) collective-permute-start(bf16[16,2048]{1,0:T(8,128)(2,1)S(1)} %pack_amplitudes.2.refs_0_), channel_id=1, source_target_pairs={{0,16},{8,72},{16,32},{24,88},{32,48},{40,104},{48,0},{56,120},{64... | collective-permute-start | bytes 196616 | tf_op jit(solution)/shard_map/ppermute | solution.py:222
  14.2 1.5 %collective-permute-start.19 = (bf16[16,2048]{1,0:T(8,128)(2,1)S(1)}, bf16[16,2048]{1,0:T(8,128)(2,1)S(1)}, u32[]{:S(2)}, u32[]{:S(2)}) collective-permute-start(bf16[16,2048]{1,0:T(8,128)(2,1)S(1)} %pack_amplitudes.2.refs_0_), channel_id=1, source_target_pairs={{0,48},{8,200},{16,0},{24,216},{32,16},{40,232},{48,32},{56,248},{... | collective-permute-start | bytes 196616 | tf_op jit(solution)/shard_map/ppermute | solution.py:222
  15.8 1.6 %collective-permute-start.20 = (bf16[16,2048]{1,0:T(8,128)(2,1)S(1)}, bf16[16,2048]{1,0:T(8,128)(2,1)S(1)}, u32[]{:S(2)}, u32[]{:S(2)}) collective-permute-start(bf16[16,2048]{1,0:T(8,128)(2,1)S(1)} %pack_amplitudes.2.refs_0_), channel_id=1, source_target_pairs={{0,32},{8,136},{16,48},{24,152},{32,0},{40,168},{48,16},{56,184},{... | collective-permute-start | bytes 196616 | tf_op jit(solution)/shard_map/ppermute | solution.py:222
  17.3 0.7 %collective-permute-start.27 = (bf16[224,640]{1,0:T(8,128)(2,1)S(1)}, bf16[224,640]{1,0:T(8,128)(2,1)S(1)}, u32[]{:S(2)}, u32[]{:S(2)}) collective-permute-start(bf16[224,640]{1,0:T(8,128)(2,1)S(1)} %collective-permute-done.21.refs_4_), channel_id=1, source_target_pairs={{0,1},{1,2},{2,3},{3,4},{4,5},{5,6},{6,7},{7,0},{8,15},{9,8},{10,9... | collective-permute-start | bytes 860168 | tf_op jit(solution)/shard_map/ppermute | solution.py:214
  18.0 2.5 %collective-permute-start.28 = (bf16[224,640]{1,0:T(8,128)(2,1)}, bf16[224,640]{1,0:T(8,128)(2,1)}, u32[]{:S(2)}, u32[]{:S(2)}) collective-permute-start(bf16[224,640]{1,0:T(8,128)(2,1)} %collective-permute-done.23.refs_5_), channel_id=1, source_target_pairs={{0,1},{1,2},{2,3},{3,4},{4,5},{5,6},{6,7},{7,0},{8,15},{9,8},{10,9... | collective-permute-start | bytes 860168 | tf_op jit(solution)/shard_map/ppermute | solution.py:214
  20.6 1.3 %collective-permute-start.24 = (bf16[64,2048]{1,0:T(8,128)(2,1)S(1)}, bf16[64,2048]{1,0:T(8,128)(2,1)S(1)}, u32[]{:S(2)}, u32[]{:S(2)}) collective-permute-start(bf16[64,2048]{1,0:T(8,128)(2,1)S(1)} %stack.4.refs_0_), channel_id=1, source_target_pairs={{0,64},{8,24},{16,80},{24,40},{32,96},{40,56},{48,112},{56,8},{64,... | collective-permute-start | bytes 786440 | tf_op jit(solution)/shard_map/ppermute | solution.py:222
  22.0 1.5 %collective-permute-start.25 = (bf16[64,2048]{1,0:T(8,128)(2,1)S(1)}, bf16[64,2048]{1,0:T(8,128)(2,1)S(1)}, u32[]{:S(2)}, u32[]{:S(2)}) collective-permute-start(bf16[64,2048]{1,0:T(8,128)(2,1)S(1)} %stack.4.refs_0_), channel_id=1, source_target_pairs={{0,192},{8,56},{16,208},{24,8},{32,224},{40,24},{48,240},{56,40},{... | collective-permute-start | bytes 786440 | tf_op jit(solution)/shard_map/ppermute | solution.py:222
  23.4 1.5 %collective-permute-start.26 = (bf16[64,2048]{1,0:T(8,128)(2,1)S(1)}, bf16[64,2048]{1,0:T(8,128)(2,1)S(1)}, u32[]{:S(2)}, u32[]{:S(2)}) collective-permute-start(bf16[64,2048]{1,0:T(8,128)(2,1)S(1)} %stack.4.refs_0_), channel_id=1, source_target_pairs={{0,128},{8,40},{16,144},{24,56},{32,160},{40,8},{48,176},{56,24},{... | collective-permute-start | bytes 786440 | tf_op jit(solution)/shard_map/ppermute | solution.py:222
  25.0 2.5 %collective-permute-done.24.refs_1_ = bf16[64,2048]{1,0:T(8,128)(2,1)S(1)} collective-permute-done((bf16[64,2048]{1,0:T(8,128)(2,1)S(1)}, bf16[64,2048]{1,0:T(8,128)(2,1)S(1)}, u32[]{:S(2)}, u32[]{:S(2)}) %collective-permute-start.24) | collective-permute-done | bytes 262176 | tf_op jit(solution)/shard_map/ppermute | solution.py:222
  27.4 0.0 collective-permute-done.25.refs_2_
  27.5 3.9 %collective-permute-done.26.refs_3_ = bf16[64,2048]{1,0:T(8,128)(2,1)S(1)} collective-permute-done((bf16[64,2048]{1,0:T(8,128)(2,1)S(1)}, bf16[64,2048]{1,0:T(8,128)(2,1)S(1)}, u32[]{:S(2)}, u32[]{:S(2)}) %collective-permute-start.26) | collective-permute-done | bytes 262176 | tf_op jit(solution)/shard_map/ppermute | solution.py:222
  31.4 0.1 stack.5.refs_1_
  31.5 0.7 %collective-permute-start.29 = (bf16[256,2048]{1,0:T(8,128)(2,1)S(1)}, bf16[256,2048]{1,0:T(8,128)(2,1)S(1)}, u32[]{:S(2)}, u32[]{:S(2)}) collective-permute-start(bf16[256,2048]{1,0:T(8,128)(2,1)S(1)} %stack.5.refs_1_), channel_id=1, source_target_pairs={{0,8},{8,0},{16,24},{24,16},{32,40},{40,32},{48,56},{56,48},{64,72... | collective-permute-start | bytes 3145736 | tf_op jit(solution)/shard_map/ppermute | solution.py:218
  32.1 2.1 %collective-permute-start.32 = (bf16[224,640]{1,0:T(8,128)(2,1)S(1)}, bf16[224,640]{1,0:T(8,128)(2,1)}, u32[]{:S(2)}, u32[]{:S(2)}) collective-permute-start(bf16[224,640]{1,0:T(8,128)(2,1)S(1)} %collective-permute-done.27.refs_4_.refs_6_), channel_id=1, source_target_pairs={{0,1},{1,2},{2,3},{3,4},{4,5},{5,6},{6,7},{7,0},{8,15},{9,8},{10,9... | collective-permute-start | bytes 860168 | tf_op jit(solution)/shard_map/ppermute | solution.py:214
  34.2 1.7 %collective-permute-start.33 = (bf16[224,640]{1,0:T(8,128)(2,1)}, bf16[224,640]{1,0:T(8,128)(2,1)}, u32[]{:S(2)}, u32[]{:S(2)}) collective-permute-start(bf16[224,640]{1,0:T(8,128)(2,1)} %collective-permute-done.28.refs_5_), channel_id=1, source_target_pairs={{0,1},{1,2},{2,3},{3,4},{4,5},{5,6},{6,7},{7,0},{8,15},{9,8},{10,9... | collective-permute-start | bytes 860168 | tf_op jit(solution)/shard_map/ppermute | solution.py:214
  36.0 0.3 collective-permute-start.30
  36.3 0.2 collective-permute-start.31
  36.5 1.5 %collective-permute-done.32.refs_0_ = bf16[224,640]{1,0:T(8,128)(2,1)} collective-permute-done((bf16[224,640]{1,0:T(8,128)(2,1)S(1)}, bf16[224,640]{1,0:T(8,128)(2,1)}, u32[]{:S(2)}, u32[]{:S(2)}) %collective-permute-start.32) | collective-permute-done | bytes 286752 | tf_op jit(solution)/shard_map/ppermute | solution.py:214
  38.0 3.0 %collective-permute-start.35 = (bf16[224,640]{1,0:T(8,128)(2,1)}, bf16[224,640]{1,0:T(8,128)(2,1)}, u32[]{:S(2)}, u32[]{:S(2)}) collective-permute-start(bf16[224,640]{1,0:T(8,128)(2,1)} %collective-permute-done.32.refs_0_), channel_id=1, source_target_pairs={{0,1},{1,2},{2,3},{3,4},{4,5},{5,6},{6,7},{7,0},{8,15},{9,8},{10,9... | collective-permute-start | bytes 860168 | tf_op jit(solution)/shard_map/ppermute | solution.py:214
  41.0 0.0 collective-permute-done.33
  41.1 2.2 %collective-permute-start.34 = (bf16[224,640]{1,0:T(8,128)(2,1)}, bf16[224,640]{1,0:T(8,128)(2,1)}, u32[]{:S(2)}, u32[]{:S(2)}) collective-permute-start(bf16[224,640]{1,0:T(8,128)(2,1)} %collective-permute-done.33), channel_id=1, source_target_pairs={{0,8},{8,0},{16,24},{24,16},{32,40},{40,32},{48,56},{56,48},{64,72... | collective-permute-start | bytes 860168 | tf_op jit(solution)/shard_map/ppermute | solution.py:218
  43.3 0.0 copy-start.2
  43.3 0.9 %copy-done.2 = bf16[224,640]{1,0:T(8,128)(2,1)S(1)} copy-done((bf16[224,640]{1,0:T(8,128)(2,1)S(1)}, bf16[224,640]{1,0:T(8,128)(2,1)}, u32[]{:S(2)}) %copy-start.2) | copy-done | bytes 286744
  44.2 2.6 %contract_early.2 = (f32[512,640]{1,0:T(8,128)S(1)}, bf16[512,768]{1,0:T(8,128)(2,1)S(1)}) custom-call(bf16[512,640]{1,0:T(8,128)(2,1)S(1)} %copy-done, bf16[256,2048]{1,0:T(8,128)(2,1)S(1)} %stack.5.refs_1_, bf16[256,2048]{1,0:T(8,128)(2,1)S(1)} %collective-permute-done.29.refs_2_, bf16[224,640]{1,0:T(8,128)(2,1)S(1)} %copy-done.2, ...), custom_call_target="tpu_custom_call" | custom-call | tf_op jit(solution)/shard_map/contract_early/pallas_call | solution.py:272
  46.9 3.3 %contract_late.2 = f32[512,640]{1,0:T(8,128)} custom-call(s32[640]{0:T(1024)S(1)} %copy-done.8, f32[640]{0:T(1024)S(1)} %copy-done.9, s32[64]{0:T(128)S(1)} %copy-done.10, f32[64]{0:T(128)S(1)} %copy-done.11, s32[2]{0:T(128)S(1)} %copy-done.12, s32[640]{0:T(1024)S(1)} %copy-done.8, f32[640]{0:T(1024)S(1)} %copy-done.9, s32[64]{0:T(128)S(1)} %copy-done.10, ...), custom_call_target="tpu_custom_call" | custom-call | tf_op jit(solution)/shard_map/contract_late/pallas_call | solution.py:288
  50.3 0.9 %while.10 = (s32[]{:T(128)}, f32[512,640]{1,0:T(8,128)}, s32[]{:T(128)}, s32[640]{0:T(1024)S(1)}, s32[1]{0:T(128)}, /*index=5*/s32[2]{0:T(128)S(1)}, bf16[1280,6...) while((s32[]{:T(128)}, f32[512,640]{1,0:T(8,128)}, ...), condition=%wide.region_1.0_spmd, body=%wide.region_0.0_spmd.sunk | while | flops 327682 | bytes 33194904 | solution.py:321
  (33 shorter events, 0.1 us)
Async XLA Ops:
  0.0 11.9 %copy-start.8 = (s32[640]{0:T(1024)S(1)}, s32[640]{0:T(1024)}, u32[]{:S(2)}) copy-start(s32[640]{0:T(1024)} %irrep_ref.5) | copy-start | bytes 7684
  0.0 11.9 %copy-start.5 = (bf16[16,10240]{1,0:T(8,128)(2,1)S(1)}, bf16[16,10240]{1,0:T(8,128)(2,1)}, u32[]{:S(2)}) copy-start(bf16[16,10240]{1,0:T(8,128)(2,1)} %rows_ref.1) | copy-start | bytes 983044
  0.0 11.9 %copy-start.10 = (s32[64]{0:T(128)S(1)}, s32[64]{0:T(128)}, u32[]{:S(2)}) copy-start(s32[64]{0:T(128)} %occ_irrep_ref.1) | copy-start | bytes 772
  3.5 27.9 %copy-start.1 = (bf16[224,640]{1,0:T(8,128)(2,1)}, bf16[224,640]{1,0:T(8,128)(2,1)S(1)}, u32[]{:S(2)}) copy-start(bf16[224,640]{1,0:T(8,128)(2,1)S(1)} %get-tuple-element.73.refs_3_) | copy-start | bytes 860164
  3.5 7.2 %collective-permute-start.22 = (bf16[224,640]{1,0:T(8,128)(2,1)S(1)}, bf16[224,640]{1,0:T(8,128)(2,1)S(1)}, u32[]{:S(2)}, u32[]{:S(2)}) collective-permute-start(bf16[224,640]{1,0:T(8,128)(2,1)S(1)} %get-tuple-element.73.refs_3_), channel_id=1, source_target_pairs={{0,8},{8,0},{16,24},{24,16},{32,40},{40,32},{48,56},{56,48},{64,72... | collective-permute-start | bytes 860168 | tf_op jit(solution)/shard_map/ppermute | solution.py:218
  6.9 10.4 %collective-permute-start.21 = (bf16[224,640]{1,0:T(8,128)(2,1)S(1)}, bf16[224,640]{1,0:T(8,128)(2,1)S(1)}, u32[]{:S(2)}, u32[]{:S(2)}) collective-permute-start(bf16[224,640]{1,0:T(8,128)(2,1)S(1)} %get-tuple-element.73.refs_3_), channel_id=1, source_target_pairs={{0,1},{1,2},{2,3},{3,4},{4,5},{5,6},{6,7},{7,0},{8,15},{9,8},{10,9... | collective-permute-start | bytes 860168 | tf_op jit(solution)/shard_map/ppermute | solution.py:214
  10.7 7.3 %collective-permute-start.23 = (bf16[224,640]{1,0:T(8,128)(2,1)S(1)}, bf16[224,640]{1,0:T(8,128)(2,1)}, u32[]{:S(2)}, u32[]{:S(2)}) collective-permute-start(bf16[224,640]{1,0:T(8,128)(2,1)S(1)} %collective-permute-done.22), channel_id=1, source_target_pairs={{0,1},{1,2},{2,3},{3,4},{4,5},{5,6},{6,7},{7,0},{8,15},{9,8},{10,9... | collective-permute-start | bytes 860168 | tf_op jit(solution)/shard_map/ppermute | solution.py:214
  12.9 7.7 %collective-permute-start.18 = (bf16[16,2048]{1,0:T(8,128)(2,1)S(1)}, bf16[16,2048]{1,0:T(8,128)(2,1)S(1)}, u32[]{:S(2)}, u32[]{:S(2)}) collective-permute-start(bf16[16,2048]{1,0:T(8,128)(2,1)S(1)} %pack_amplitudes.2.refs_0_), channel_id=1, source_target_pairs={{0,16},{8,72},{16,32},{24,88},{32,48},{40,104},{48,0},{56,120},{64... | collective-permute-start | bytes 196616 | tf_op jit(solution)/shard_map/ppermute | solution.py:222
  14.2 6.4 %collective-permute-start.19 = (bf16[16,2048]{1,0:T(8,128)(2,1)S(1)}, bf16[16,2048]{1,0:T(8,128)(2,1)S(1)}, u32[]{:S(2)}, u32[]{:S(2)}) collective-permute-start(bf16[16,2048]{1,0:T(8,128)(2,1)S(1)} %pack_amplitudes.2.refs_0_), channel_id=1, source_target_pairs={{0,48},{8,200},{16,0},{24,216},{32,16},{40,232},{48,32},{56,248},{... | collective-permute-start | bytes 196616 | tf_op jit(solution)/shard_map/ppermute | solution.py:222
  15.8 4.8 %collective-permute-start.20 = (bf16[16,2048]{1,0:T(8,128)(2,1)S(1)}, bf16[16,2048]{1,0:T(8,128)(2,1)S(1)}, u32[]{:S(2)}, u32[]{:S(2)}) collective-permute-start(bf16[16,2048]{1,0:T(8,128)(2,1)S(1)} %pack_amplitudes.2.refs_0_), channel_id=1, source_target_pairs={{0,32},{8,136},{16,48},{24,152},{32,0},{40,168},{48,16},{56,184},{... | collective-permute-start | bytes 196616 | tf_op jit(solution)/shard_map/ppermute | solution.py:222
  17.3 7.7 %collective-permute-start.27 = (bf16[224,640]{1,0:T(8,128)(2,1)S(1)}, bf16[224,640]{1,0:T(8,128)(2,1)S(1)}, u32[]{:S(2)}, u32[]{:S(2)}) collective-permute-start(bf16[224,640]{1,0:T(8,128)(2,1)S(1)} %collective-permute-done.21.refs_4_), channel_id=1, source_target_pairs={{0,1},{1,2},{2,3},{3,4},{4,5},{5,6},{6,7},{7,0},{8,15},{9,8},{10,9... | collective-permute-start | bytes 860168 | tf_op jit(solution)/shard_map/ppermute | solution.py:214
  18.0 13.3 %collective-permute-start.28 = (bf16[224,640]{1,0:T(8,128)(2,1)}, bf16[224,640]{1,0:T(8,128)(2,1)}, u32[]{:S(2)}, u32[]{:S(2)}) collective-permute-start(bf16[224,640]{1,0:T(8,128)(2,1)} %collective-permute-done.23.refs_5_), channel_id=1, source_target_pairs={{0,1},{1,2},{2,3},{3,4},{4,5},{5,6},{6,7},{7,0},{8,15},{9,8},{10,9... | collective-permute-start | bytes 860168 | tf_op jit(solution)/shard_map/ppermute | solution.py:214
  20.6 22.6 %copy-start = (bf16[512,640]{1,0:T(8,128)(2,1)S(1)}, bf16[512,640]{1,0:T(8,128)(2,1)}, u32[]{:S(2)}) copy-start(bf16[512,640]{1,0:T(8,128)(2,1)} %refs_0_.1) | copy-start | bytes 1966084
  20.6 6.8 %collective-permute-start.24 = (bf16[64,2048]{1,0:T(8,128)(2,1)S(1)}, bf16[64,2048]{1,0:T(8,128)(2,1)S(1)}, u32[]{:S(2)}, u32[]{:S(2)}) collective-permute-start(bf16[64,2048]{1,0:T(8,128)(2,1)S(1)} %stack.4.refs_0_), channel_id=1, source_target_pairs={{0,64},{8,24},{16,80},{24,40},{32,96},{40,56},{48,112},{56,8},{64,... | collective-permute-start | bytes 786440 | tf_op jit(solution)/shard_map/ppermute | solution.py:222
  22.0 5.5 %collective-permute-start.25 = (bf16[64,2048]{1,0:T(8,128)(2,1)S(1)}, bf16[64,2048]{1,0:T(8,128)(2,1)S(1)}, u32[]{:S(2)}, u32[]{:S(2)}) collective-permute-start(bf16[64,2048]{1,0:T(8,128)(2,1)S(1)} %stack.4.refs_0_), channel_id=1, source_target_pairs={{0,192},{8,56},{16,208},{24,8},{32,224},{40,24},{48,240},{56,40},{... | collective-permute-start | bytes 786440 | tf_op jit(solution)/shard_map/ppermute | solution.py:222
  23.4 8.0 %collective-permute-start.26 = (bf16[64,2048]{1,0:T(8,128)(2,1)S(1)}, bf16[64,2048]{1,0:T(8,128)(2,1)S(1)}, u32[]{:S(2)}, u32[]{:S(2)}) collective-permute-start(bf16[64,2048]{1,0:T(8,128)(2,1)S(1)} %stack.4.refs_0_), channel_id=1, source_target_pairs={{0,128},{8,40},{16,144},{24,56},{32,160},{40,8},{48,176},{56,24},{... | collective-permute-start | bytes 786440 | tf_op jit(solution)/shard_map/ppermute | solution.py:222
  31.5 11.8 %collective-permute-start.29 = (bf16[256,2048]{1,0:T(8,128)(2,1)S(1)}, bf16[256,2048]{1,0:T(8,128)(2,1)S(1)}, u32[]{:S(2)}, u32[]{:S(2)}) collective-permute-start(bf16[256,2048]{1,0:T(8,128)(2,1)S(1)} %stack.5.refs_1_), channel_id=1, source_target_pairs={{0,8},{8,0},{16,24},{24,16},{32,40},{40,32},{48,56},{56,48},{64,72... | collective-permute-start | bytes 3145736 | tf_op jit(solution)/shard_map/ppermute | solution.py:218
  32.1 5.9 %collective-permute-start.32 = (bf16[224,640]{1,0:T(8,128)(2,1)S(1)}, bf16[224,640]{1,0:T(8,128)(2,1)}, u32[]{:S(2)}, u32[]{:S(2)}) collective-permute-start(bf16[224,640]{1,0:T(8,128)(2,1)S(1)} %collective-permute-done.27.refs_4_.refs_6_), channel_id=1, source_target_pairs={{0,1},{1,2},{2,3},{3,4},{4,5},{5,6},{6,7},{7,0},{8,15},{9,8},{10,9... | collective-permute-start | bytes 860168 | tf_op jit(solution)/shard_map/ppermute | solution.py:214
  34.2 6.8 %collective-permute-start.33 = (bf16[224,640]{1,0:T(8,128)(2,1)}, bf16[224,640]{1,0:T(8,128)(2,1)}, u32[]{:S(2)}, u32[]{:S(2)}) collective-permute-start(bf16[224,640]{1,0:T(8,128)(2,1)} %collective-permute-done.28.refs_5_), channel_id=1, source_target_pairs={{0,1},{1,2},{2,3},{3,4},{4,5},{5,6},{6,7},{7,0},{8,15},{9,8},{10,9... | collective-permute-start | bytes 860168 | tf_op jit(solution)/shard_map/ppermute | solution.py:214
  36.0 7.3 %collective-permute-start.30 = (bf16[224,640]{1,0:T(8,128)(2,1)}, bf16[224,640]{1,0:T(8,128)(2,1)}, u32[]{:S(2)}, u32[]{:S(2)}) collective-permute-start(bf16[224,640]{1,0:T(8,128)(2,1)} %collective-permute-done.23.refs_5_), channel_id=1, source_target_pairs={{0,8},{8,0},{16,24},{24,16},{32,40},{40,32},{48,56},{56,48},{64,72... | collective-permute-start | bytes 860168 | tf_op jit(solution)/shard_map/ppermute | solution.py:218
  36.3 7.0 %collective-permute-start.31 = (bf16[224,640]{1,0:T(8,128)(2,1)}, bf16[224,640]{1,0:T(8,128)(2,1)}, u32[]{:S(2)}, u32[]{:S(2)}) collective-permute-start(bf16[224,640]{1,0:T(8,128)(2,1)} %collective-permute-done.28.refs_5_), channel_id=1, source_target_pairs={{0,8},{8,0},{16,24},{24,16},{32,40},{40,32},{48,56},{56,48},{64,72... | collective-permute-start | bytes 860168 | tf_op jit(solution)/shard_map/ppermute | solution.py:218
  38.0 8.8 %collective-permute-start.35 = (bf16[224,640]{1,0:T(8,128)(2,1)}, bf16[224,640]{1,0:T(8,128)(2,1)}, u32[]{:S(2)}, u32[]{:S(2)}) collective-permute-start(bf16[224,640]{1,0:T(8,128)(2,1)} %collective-permute-done.32.refs_0_), channel_id=1, source_target_pairs={{0,1},{1,2},{2,3},{3,4},{4,5},{5,6},{6,7},{7,0},{8,15},{9,8},{10,9... | collective-permute-start | bytes 860168 | tf_op jit(solution)/shard_map/ppermute | solution.py:214
  41.1 5.8 %collective-permute-start.34 = (bf16[224,640]{1,0:T(8,128)(2,1)}, bf16[224,640]{1,0:T(8,128)(2,1)}, u32[]{:S(2)}, u32[]{:S(2)}) collective-permute-start(bf16[224,640]{1,0:T(8,128)(2,1)} %collective-permute-done.33), channel_id=1, source_target_pairs={{0,8},{8,0},{16,24},{24,16},{32,40},{40,32},{48,56},{56,48},{64,72... | collective-permute-start | bytes 860168 | tf_op jit(solution)/shard_map/ppermute | solution.py:218
  43.2 3.6 %copy-start.11 = (f32[64]{0:T(128)S(1)}, f32[64]{0:T(128)}, u32[]{:S(2)}) copy-start(f32[64]{0:T(128)} %occ_energy_ref.1) | copy-start | bytes 772
  43.2 3.6 %copy-start.12 = (s32[2]{0:T(128)S(1)}, s32[2]{0:T(128)}, u32[]{:S(2)}) copy-start(s32[2]{0:T(128)} %tiles_a_s.3) | copy-start | bytes 28
  43.3 1.0 %copy-start.2 = (bf16[224,640]{1,0:T(8,128)(2,1)S(1)}, bf16[224,640]{1,0:T(8,128)(2,1)}, u32[]{:S(2)}) copy-start(bf16[224,640]{1,0:T(8,128)(2,1)} %copy-done.1) | copy-start | bytes 860164
  44.2 2.7 %copy-start.9 = (f32[640]{0:T(1024)S(1)}, f32[640]{0:T(1024)}, u32[]{:S(2)}) copy-start(f32[640]{0:T(1024)} %energy_ref.1) | copy-start | bytes 7684
  46.9 3.3 %copy-start.3 = (bf16[1280,640]{1,0:T(8,128)(2,1)S(1)}, bf16[1280,640]{1,0:T(8,128)(2,1)}, u32[]{:S(2)}) copy-start(bf16[1280,640]{1,0:T(8,128)(2,1)} %panel_hbm.1) | copy-start | bytes 4915204
  46.9 3.3 %copy-start.6 = (bf16[16,10240]{1,0:T(8,128)(2,1)S(1)}, bf16[16,10240]{1,0:T(8,128)(2,1)}, u32[]{:S(2)}) copy-start(bf16[16,10240]{1,0:T(8,128)(2,1)} %rows_ref.1) | copy-start | bytes 983044

commit v4 on v3

--- a/solution.py
+++ b/solution.py
@@ -1,3 +1,5 @@
+import functools
+
 import jax
 import jax.numpy as jnp
 from jax import lax
@@ -51,7 +53,6 @@
         preferred_element_type=jnp.float32,
     )
     rank = jnp.sum(jnp.where(member, before, 0.0), axis=0, keepdims=True).astype(jnp.int32)
-    most_s[0] = jnp.max(rank) + 1
     slots = lax.broadcasted_iota(jnp.int32, (PITCH, NVIR), 0)
     picks = ((slots == rank - base_s[0]) & (slots < CAP)).astype(jnp.bfloat16)
     picks_ref[...] = picks
@@ -63,13 +64,17 @@
         e = tiles_e_s[0] * TILE + narrow * E_LOCAL + local
         wanted = (irreps ^ (irrep_s[a] ^ irrep_s[e])).astype(jnp.float32).astype(jnp.bfloat16)
         fetches[local].wait()
-        for tile in range(NVIR // PITCH):
-            lanes = slice(tile * PITCH, (tile + 1) * PITCH)
-            held = panel_ref[local, :, lanes]
-            kept = jnp.where(label_col == wanted[:, lanes], held, jnp.zeros_like(held))
-            strip_ref[local * CAP:(local + 1) * CAP, lanes] = jnp.dot(
+        for start in range(0, NVIR, 2 * PITCH):
+            kept = []
+            for tile in range(start, min(start + 2 * PITCH, NVIR), PITCH):
+                lanes = slice(tile, tile + PITCH)
+                held = panel_ref[local, :, lanes]
+                kept.append(jnp.where(label_col == wanted[:, lanes], held, jnp.zeros_like(held)))
+            kept = jnp.concatenate(kept, axis=1)
+            strip_ref[local * CAP:(local + 1) * CAP, start:start + kept.shape[1]] = jnp.dot(
                 picks[:CAP, :], kept, preferred_element_type=jnp.float32
             ).astype(strip_ref.dtype)
+    most_s[0] = jnp.max(rank) + 1
 
 
 def pack_amplitudes(irrep_s, occ_s, tiles_e_s, irrep_ref, picks_ref, rows_ref, out_ref, stacked):
@@ -130,62 +135,71 @@
             panel[start + CAP:start + PITCH, :] = blank
 
 
-def columns_of(amplitudes, step):
-    way = 1 - 2 * (lax.axis_index("wide") % 2)
-    source = (lax.axis_index("narrow") - way * step + RING) % RING
-    start = pl.multiple_of(source * E_LOCAL * PITCH, E_LOCAL * PITCH)
-    return amplitudes[:, pl.ds(start, E_LOCAL * PITCH)]
-
-
-def contract_early(steps, late_steps, other, own, twin, *refs):
-    strips, (sum_ref, late_ref, amplitudes, ordered, panel) = refs[:-5], refs[-5:]
-    wide = lax.axis_index("wide")
+def place_rows(steps, split, groups, ordered, late_ref):
+    wide, narrow = lax.axis_index("wide"), lax.axis_index("narrow")
     y, x, core = wide // 8, wide // 2 % SIDE, wide % 2
-    for ref, side in ((own, core), (twin, 1 - core)):
-        for outer in range(SIDE):
-            for inner in range(SIDE):
-                dx = jnp.where(side == 0, reach(inner), reach(outer))
-                dy = jnp.where(side == 0, reach(outer), reach(inner))
-                place = (y + dy + SIDE) % SIDE * 8 + (x + dx + SIDE) % SIDE * 2 + side
-                block = (outer * SIDE + inner) * ROWS
-                amplitudes[pl.ds(pl.multiple_of(place * ROWS, ROWS), ROWS), :] = ref[
-                    block:block + ROWS, :
-                ]
+    way = 1 - 2 * core
     span = E_LOCAL * PITCH
-    for index, step in enumerate(late_steps):
-        late_ref[:, index * span:(index + 1) * span] = columns_of(amplitudes, step)
-    for index, step in enumerate(steps):
-        ordered[:, index * span:(index + 1) * span] = columns_of(amplitudes, step)
+    starts = [
+        pl.multiple_of((narrow - way * step + RING) % RING * span, span) for step in steps
+    ]
+    for piece, outer, twin in groups:
+        side = 1 - core if twin else core
+        for inner in range(SIDE):
+            dx = jnp.where(side == 0, reach(inner), reach(outer))
+            dy = jnp.where(side == 0, reach(outer), reach(inner))
+            place = (y + dy + SIDE) % SIDE * 8 + (x + dx + SIDE) % SIDE * 2 + side
+            to_rows = pl.ds(pl.multiple_of(place * ROWS, ROWS), ROWS)
+            block = slice(inner * ROWS, (inner + 1) * ROWS)
+            for k, start in enumerate(starts):
+                target, at = (ordered, k) if k < split else (late_ref, k - split)
+                target[to_rows, at * span:(at + 1) * span] = piece[block, pl.ds(start, span)]
+
+
+def contract_early(
+    steps, split,
+    irrep_s, energy_s, occ_irrep_s, occ_energy_s, tiles_a_s,
+    irrep_ref, energy_ref, occ_irrep_ref, occ_energy_ref, other_hbm, *refs,
+):
+    pieces_hbm, strips = refs[:2 * SIDE], refs[2 * SIDE:-7]
+    sum_ref, scale_ref, late_ref, other, ordered, panel, arrived = refs[-7:]
+    fetches = [pltpu.make_async_copy(other_hbm, other, arrived.at[0])]
+    for fetch in fetches:
+        fetch.start()
     fill(panel, strips)
-    sum_ref[...] = other[...].astype(jnp.float32) + jnp.dot(
-        ordered[...], panel[...], preferred_element_type=jnp.float32
-    )
-
-
-def contract_late(
-    irrep_s, energy_s, occ_irrep_s, occ_energy_s, tiles_a_s,
-    irrep_ref, energy_ref, occ_irrep_ref, occ_energy_ref, sum_ref, late, *refs,
-):
-    strips, (out_hbm, panel, out, left) = refs[:-4], refs[-4:]
     wide, narrow = lax.axis_index("wide"), lax.axis_index("narrow")
-    fill(panel, strips)
     a = tiles_a_s[wide // TILE] * TILE + wide % TILE
     col_sym = irrep_ref[...].reshape(1, NVIR) ^ irrep_s[a]
     col_energy = energy_s[a] + energy_ref[...].reshape(1, NVIR)
     j_sym = as_column(occ_irrep_ref[...].reshape(1, NOCC))
     j_energy = as_column(occ_energy_ref[...].reshape(1, NOCC))
-    i_count = out.shape[0] // NOCC
-    out[...] = jnp.dot(late[...], panel[...], preferred_element_type=jnp.float32)
-    copies = []
+    i_count = scale_ref.shape[0] // NOCC
     for local in range(i_count):
         i = narrow * i_count + local
-        rows = slice(local * NOCC, (local + 1) * NOCC)
-        summed = out[rows, :] + sum_ref[rows, :]
         denom = (occ_energy_s[i] + j_energy) - col_energy
         same = (j_sym ^ occ_irrep_s[i]) == col_sym
-        out[rows, :] = jnp.where(same, summed / denom, 0.0)
+        scale_ref[local * NOCC:(local + 1) * NOCC, :] = jnp.where(same, 1.0 / denom, 0.0)
+    for fetch in fetches:
+        fetch.wait()
+    groups = [(pieces_hbm[index], index % SIDE, index >= SIDE) for index in range(2 * SIDE)]
+    place_rows(steps, split, groups, ordered, late_ref)
+    sum_ref[...] = other[...].astype(jnp.float32) + jnp.dot(
+        ordered[...], panel[...], preferred_element_type=jnp.float32
+    )
+
+
+def contract_late(sum_ref, scale_ref, late, *refs):
+    strips, (out_hbm, panel, out, left) = refs[:-4], refs[-4:]
+    fill(panel, strips)
+    out[...] = jnp.dot(late[...], panel[...], preferred_element_type=jnp.float32)
+    count = left.shape[0]
+    height = out.shape[0] // count
+    copies = []
+    for index in range(count):
+        rows = slice(index * height, (index + 1) * height)
+        out[rows, :] = (out[rows, :] + sum_ref[rows, :]) * scale_ref[rows, :]
         copies.append(
-            pltpu.make_async_copy(out.at[rows, :], out_hbm.at[rows, :], left.at[local])
+            pltpu.make_async_copy(out.at[rows, :], out_hbm.at[rows, :], left.at[index])
         )
         copies[-1].start()
     for copy in copies:
@@ -218,8 +232,8 @@
     return lax.ppermute(part, "wide", [(i, i ^ 1) for i in range(32)])
 
 
-def spread(block, steps, after=()):
-    return stack([block] + [lax.ppermute(block, "wide", pairs) for pairs in steps], after)
+def to(part, pairs):
+    return lax.ppermute(part, "wide", pairs)
 
 
 def one_pass(
@@ -254,53 +268,60 @@
         name="pack_amplitudes",
     )(virt_irrep, occ_irrep, tiles_e, virt_irrep, picks, amplitudes)
 
-    strips = [mine]
-    twins = swap(mine)
-    rounds = []
-    for _ in range(RING // 2 - 1):
-        mine, twins = hop(mine), hop(twins)
-        rounds.append((mine, twins))
-        strips += [mine, swap(twins)]
-    strips.append(hop(mine))
-
-    own = spread(block, [plane(1, 0), plane(-1, 0), plane(2, 0)], rounds[0])
-    own = spread(own, [plane(0, 1), plane(0, -1), plane(0, 2)], rounds[1])
-    twin = swap(own)
-
-    steps = [0] + [sign * r for r in range(1, RING // 2) for sign in (1, -1)] + [RING // 2]
-    early = 5
-    sums, late = pl.pallas_call(
-        lambda *refs: contract_early(steps[:early], steps[early:], *refs),
+    ready = lax.optimization_barrier
+    mine0, twins0 = mine, swap(mine)
+    mine1, twins1 = hop(mine0), hop(twins0)
+    line = stack(
+        [block] + [to(block, plane(*step)) for step in ((1, 0), (-1, 0), (2, 0))],
+        [mine1, twins1],
+    )
+    line, twins1 = ready((line, twins1))
+    mine2, twins2 = hop(mine1), hop(twins1)
+    mine3, twins3 = hop(mine2), hop(twins2)
+    pieces = [line] + [to(line, plane(0, step)) for step in (1, -1, 2)]
+    pieces += [swap(piece) for piece in pieces]
+    strips = [
+        mine0, mine1, swap(twins1), mine2, swap(twins2), mine3, swap(twins3), hop(mine3)
+    ]
+
+    steps = [0, 1, -1, 2, -2, 3, -3, 4]
+    early = 6
+    full = jax.ShapeDtypeStruct(other_terms.shape, jnp.float32)
+    sums, scale, late = pl.pallas_call(
+        functools.partial(contract_early, steps, early),
         out_shape=(
-            jax.ShapeDtypeStruct(other_terms.shape, jnp.float32),
-            jax.ShapeDtypeStruct((height, (RING - early) * span), amplitudes.dtype),
+            full, full, jax.ShapeDtypeStruct((height, (RING - early) * span), amplitudes.dtype)
         ),
-        in_specs=[VMEM] * (3 + early),
-        out_specs=(VMEM, VMEM),
+        in_specs=[SMEM] * 5 + [VMEM] * 4 + [HBM] + [VMEM] * (2 * SIDE + early),
+        out_specs=(VMEM,) * 3,
         scratch_shapes=[
-            pltpu.VMEM((height, RING * span), amplitudes.dtype),
+            pltpu.VMEM(other_terms.shape, other_terms.dtype),
             pltpu.VMEM((height, early * span), amplitudes.dtype),
             pltpu.VMEM((early * span, NVIR), integrals.dtype),
+            pltpu.SemaphoreType.DMA((2 * SIDE + 1,)),
         ],
-        compiler_params=params(20),
+        cost_estimate=pl.CostEstimate(
+            flops=2 * height * early * span * NVIR, bytes_accessed=40 * 2**20, transcendentals=0
+        ),
+        compiler_params=params(8),
         name="contract_early",
-    )(other_terms, own, twin, *strips[:early])
+    )(
+        virt_irrep, virt_energy, occ_irrep, occ_energy, tiles_a,
+        virt_irrep, virt_energy, occ_irrep, occ_energy, other_terms, *pieces, *strips[:early],
+    )
     updated = pl.pallas_call(
         contract_late,
-        out_shape=jax.ShapeDtypeStruct(other_terms.shape, jnp.float32),
-        in_specs=[SMEM] * 5 + [VMEM] * (6 + RING - early),
+        out_shape=full,
+        in_specs=[VMEM] * (3 + RING - early),
         out_specs=HBM,
         scratch_shapes=[
             pltpu.VMEM(((RING - early) * span, NVIR), integrals.dtype),
             pltpu.VMEM(other_terms.shape, jnp.float32),
-            pltpu.SemaphoreType.DMA((height // NOCC,)),
+            pltpu.SemaphoreType.DMA((4,)),
         ],
-        compiler_params=params(16),
+        compiler_params=params(6),
         name="contract_late",
-    )(
-        virt_irrep, virt_energy, occ_irrep, occ_energy, tiles_a,
-        virt_irrep, virt_energy, occ_irrep, occ_energy, sums, late, *strips[early:],
-    )
+    )(sums, scale, late, *strips[early:])
     return updated, most[0]
 
 

time: 51.6 us -> 47.7 us (0.924)
  waiting for transfers between devices: 8 us -> 3.85 us
  local copies, waits for them, and re-layouts: 1 us -> 3.34 us
  starting transfers between devices: 30.6 us -> 29.1 us
    ppermute x7, starting transfers between devices: 15.2 us -> 10.6 us  [hop(): return lax.ppermute(part, ('wide', 'narrow'), along_ring())]
    ppermute x5 -> x8, starting transfers between devices: 6.67 us -> 10 us  [swap(): return lax.ppermute(part, 'wide', [(i, i ^ 1) for i in range(32)])]
    ppermute x6, waiting for transfers between devices: 6.41 us -> 3.33 us  [to(): return lax.ppermute(part, 'wide', pairs)]
    unnamed x22 -> x26, local copies, waits for them, and re-layouts: 1 us -> 3.34 us
    ppermute x7, waiting for transfers between devices: 1.58 us -> 0.5 us  [hop(): return lax.ppermute(part, ('wide', 'narrow'), along_ring())]
    pallas_call x2, Pallas kernels: 5.92 us -> 5.31 us  [the longest x1 3.59 us: one_pass(): pl.pallas_call(functools.partial(contract_early, steps, early), out_shape...]
  transfers between devices with their start and end apart: 18 -> 21, of which waited for: 3 -> 3; matrix products, arithmetic and copies ran while one was open for 0% -> 0% of each run, Pallas kernels for 7% -> 10%
where the time goes in v4:
time: 47.7 us; the launch traced here: 47.5 us
  starting transfers between devices  29.1 us (61%)
  Pallas kernels  9.37 us (20%)
  waiting for transfers between devices  3.85 us (8%)
  local copies, waits for them, and re-layouts  3.34 us (7%)
  between operations  1.08 us (2%)
  loops' own time  0.81 us (2%)
    ppermute x7, starting transfers between devices, hop(): return lax.ppermute(part, ('wide', 'narrow'), along_ring())  10.6 us
    ppermute x8, starting transfers between devices, swap(): return lax.ppermute(part, 'wide', [(i, i ^ 1) for i in range(32)])  10 us
    ppermute x6, starting transfers between devices, to(): return lax.ppermute(part, 'wide', pairs)  8.43 us
    pallas_call x1, Pallas kernels, one_pass(): pl.pallas_call(functools.partial(contract_early, steps, early), out_shape...  3.59 us
    unnamed x26, local copies, waits for them, and re-layouts  3.34 us
    ppermute x6, waiting for transfers between devices, to(): return lax.ppermute(part, 'wide', pairs)  3.33 us
    pallas_call x1, Pallas kernels, one_pass(): pl.pallas_call(pack_integrals, out_shape=(jax.ShapeDtypeStruct((E_LOCAL *...  3.11 us
    pallas_call x1, Pallas kernels, one_pass(): pl.pallas_call(contract_late, out_shape=full, in_specs=[VMEM] * (3 + RING...  1.73 us
  transfers between devices with their start and end apart: 21, of which 3 were waited for; matrix products, arithmetic and copies ran while one was open for 0% of the time, Pallas kernels for 10%

profile of v4, /device:TPU:1, one launch (start us, length us, event | category | flops | bytes accessed | tf_op | source)
XLA Modules:
  0.0 47.5 jit_solution(17481656214966183161)
XLA Ops:
  0.7 3.1 %pack_integrals.2 = (bf16[224,640]{1,0:T(8,128)(2,1)S(1)}, bf16[128,640]{1,0:T(8,128)(2,1)S(1)}, s32[1]{0:T(128)}) custom-call(s32[1]{0:T(128)} %constant.3.clone.1.base_s, s32[640]{0:T(1024)} %irrep_ref.5, s32[1]{0:T(128)S(6)} %copy.16.tiles_e_s, s32[2]{0:T(128)} %tiles_a_s.3, s32[640]{0:T(1024)} %irrep_ref.5, bf16[1280,640]{1,0:T(8,128)(2,1)} %panel_hbm.1), custom_call_target="tpu_custom_call" | custom-call | tf_op jit(solution)/shard_map/pack_integrals/pallas_call | solution.py:245
  3.9 3.3 %collective-permute-start.25 = (bf16[224,640]{1,0:T(8,128)(2,1)S(1)}, bf16[224,640]{1,0:T(8,128)(2,1)S(1)}, u32[]{:S(2)}, u32[]{:S(2)}) collective-permute-start(bf16[224,640]{1,0:T(8,128)(2,1)S(1)} %get-tuple-element.79.refs_8_), channel_id=1, source_target_pairs={{0,8},{8,0},{16,24},{24,16},{32,40},{40,32},{48,56},{56,48},{64,72... | collective-permute-start | bytes 860168 | tf_op jit(solution)/shard_map/ppermute | solution.py:232
  7.2 3.8 %collective-permute-start.24 = (bf16[224,640]{1,0:T(8,128)(2,1)S(1)}, bf16[224,640]{1,0:T(8,128)(2,1)S(1)}, u32[]{:S(2)}, u32[]{:S(2)}) collective-permute-start(bf16[224,640]{1,0:T(8,128)(2,1)S(1)} %get-tuple-element.79.refs_8_), channel_id=1, source_target_pairs={{0,1},{1,2},{2,3},{3,4},{4,5},{5,6},{6,7},{7,0},{8,15},{9,8},{10,9... | collective-permute-start | bytes 860168 | tf_op jit(solution)/shard_map/ppermute | solution.py:228
  11.0 1.2 %collective-permute-start.26 = (bf16[224,640]{1,0:T(8,128)(2,1)S(1)}, bf16[224,640]{1,0:T(8,128)(2,1)S(1)}, u32[]{:S(2)}, u32[]{:S(2)}) collective-permute-start(bf16[224,640]{1,0:T(8,128)(2,1)S(1)} %collective-permute-done.25), channel_id=1, source_target_pairs={{0,1},{1,2},{2,3},{3,4},{4,5},{5,6},{6,7},{7,0},{8,15},{9,8},{10,9... | collective-permute-start | bytes 860168 | tf_op jit(solution)/shard_map/ppermute | solution.py:228
  12.2 0.9 %pack_amplitudes.2.refs_0_ = bf16[16,2048]{1,0:T(8,128)(2,1)S(1)} custom-call(s32[640]{0:T(1024)S(1)} %copy-done.14, s32[64]{0:T(128)S(1)} %copy-done.16, s32[1]{0:T(128)S(6)} %copy.16.tiles_e_s, s32[640]{0:T(1024)S(1)} %copy-done.14, bf16[128,640]{1,0:T(8,128)(2,1)S(1)} %get-tuple-element.78.picks_ref, bf16[16,10240]{1,0:T(8,128)(2,1)S(1)} %copy-done.11), custom_call_target="tpu_custom_call" | custom-call | tf_op jit(solution)/shard_map/pack_amplitudes/pallas_call | solution.py:261
  13.2 1.4 %collective-permute-start.21 = (bf16[16,2048]{1,0:T(8,128)(2,1)S(1)}, bf16[16,2048]{1,0:T(8,128)(2,1)S(1)}, u32[]{:S(2)}, u32[]{:S(2)}) collective-permute-start(bf16[16,2048]{1,0:T(8,128)(2,1)S(1)} %pack_amplitudes.2.refs_0_), channel_id=1, source_target_pairs={{0,16},{8,72},{16,32},{24,88},{32,48},{40,104},{48,0},{56,120},{64... | collective-permute-start | bytes 196616 | tf_op jit(solution)/shard_map/ppermute | solution.py:236
  14.5 1.5 %collective-permute-start.22 = (bf16[16,2048]{1,0:T(8,128)(2,1)S(1)}, bf16[16,2048]{1,0:T(8,128)(2,1)S(1)}, u32[]{:S(2)}, u32[]{:S(2)}) collective-permute-start(bf16[16,2048]{1,0:T(8,128)(2,1)S(1)} %pack_amplitudes.2.refs_0_), channel_id=1, source_target_pairs={{0,48},{8,200},{16,0},{24,216},{32,16},{40,232},{48,32},{56,248},{... | collective-permute-start | bytes 196616 | tf_op jit(solution)/shard_map/ppermute | solution.py:236
  16.1 1.6 %collective-permute-start.23 = (bf16[16,2048]{1,0:T(8,128)(2,1)S(1)}, bf16[16,2048]{1,0:T(8,128)(2,1)S(1)}, u32[]{:S(2)}, u32[]{:S(2)}) collective-permute-start(bf16[16,2048]{1,0:T(8,128)(2,1)S(1)} %pack_amplitudes.2.refs_0_), channel_id=1, source_target_pairs={{0,32},{8,136},{16,48},{24,152},{32,0},{40,168},{48,16},{56,184},{... | collective-permute-start | bytes 196616 | tf_op jit(solution)/shard_map/ppermute | solution.py:236
  17.6 0.7 %collective-permute-start.35 = (bf16[224,640]{1,0:T(8,128)(2,1)S(1)}, bf16[224,640]{1,0:T(8,128)(2,1)S(1)}, u32[]{:S(2)}, u32[]{:S(2)}) collective-permute-start(bf16[224,640]{1,0:T(8,128)(2,1)S(1)} %collective-permute-done.24.refs_4_.refs_9_), channel_id=1, source_target_pairs={{0,1},{1,2},{2,3},{3,4},{4,5},{5,6},{6,7},{7,0},{8,15},{9,8},{10,9... | collective-permute-start | bytes 860168 | tf_op jit(solution)/shard_map/ppermute | solution.py:228
  18.4 2.3 %collective-permute-done.23.refs_3_ = bf16[16,2048]{1,0:T(8,128)(2,1)S(1)} collective-permute-done((bf16[16,2048]{1,0:T(8,128)(2,1)S(1)}, bf16[16,2048]{1,0:T(8,128)(2,1)S(1)}, u32[]{:S(2)}, u32[]{:S(2)}) %collective-permute-start.23) | collective-permute-done | bytes 65568 | tf_op jit(solution)/shard_map/ppermute | solution.py:236
  20.7 1.3 %collective-permute-start.27 = (bf16[64,2048]{1,0:T(8,128)(2,1)S(1)}, bf16[64,2048]{1,0:T(8,128)(2,1)S(1)}, u32[]{:S(2)}, u32[]{:S(2)}) collective-permute-start(bf16[64,2048]{1,0:T(8,128)(2,1)S(1)} %stack.2.refs_0_), channel_id=1, source_target_pairs={{0,64},{8,24},{16,80},{24,40},{32,96},{40,56},{48,112},{56,8},{64,... | collective-permute-start | bytes 786440 | tf_op jit(solution)/shard_map/ppermute | solution.py:236
  22.0 1.5 %collective-permute-start.28 = (bf16[64,2048]{1,0:T(8,128)(2,1)S(1)}, bf16[64,2048]{1,0:T(8,128)(2,1)}, u32[]{:S(2)}, u32[]{:S(2)}) collective-permute-start(bf16[64,2048]{1,0:T(8,128)(2,1)S(1)} %stack.2.refs_0_), channel_id=1, source_target_pairs={{0,192},{8,56},{16,208},{24,8},{32,224},{40,24},{48,240},{56,40},{... | collective-permute-start | bytes 786440 | tf_op jit(solution)/shard_map/ppermute | solution.py:236
  23.5 1.0 %collective-permute-start.36 = (bf16[224,640]{1,0:T(8,128)(2,1)S(1)}, bf16[224,640]{1,0:T(8,128)(2,1)}, u32[]{:S(2)}, u32[]{:S(2)}) collective-permute-start(bf16[224,640]{1,0:T(8,128)(2,1)S(1)} %collective-permute-done.26.refs_5_), channel_id=1, source_target_pairs={{0,1},{1,2},{2,3},{3,4},{4,5},{5,6},{6,7},{7,0},{8,15},{9,8},{10,9... | collective-permute-start | bytes 860168 | tf_op jit(solution)/shard_map/ppermute | solution.py:228
  24.5 1.2 %collective-permute-start.29 = (bf16[64,2048]{1,0:T(8,128)(2,1)S(1)}, bf16[64,2048]{1,0:T(8,128)(2,1)}, u32[]{:S(2)}, u32[]{:S(2)}) collective-permute-start(bf16[64,2048]{1,0:T(8,128)(2,1)S(1)} %stack.2.refs_0_), channel_id=1, source_target_pairs={{0,128},{8,40},{16,144},{24,56},{32,160},{40,8},{48,176},{56,24},{... | collective-permute-start | bytes 786440 | tf_op jit(solution)/shard_map/ppermute | solution.py:236
  25.7 0.9 %collective-permute-start.34 = (bf16[224,640]{1,0:T(8,128)(2,1)S(1)}, bf16[224,640]{1,0:T(8,128)(2,1)S(1)}, u32[]{:S(2)}, u32[]{:S(2)}) collective-permute-start(bf16[224,640]{1,0:T(8,128)(2,1)S(1)} %collective-permute-done.26.refs_5_), channel_id=1, source_target_pairs={{0,8},{8,0},{16,24},{24,16},{32,40},{40,32},{48,56},{56,48},{64,72... | collective-permute-start | bytes 860168 | tf_op jit(solution)/shard_map/ppermute | solution.py:232
  26.6 1.0 %collective-permute-done.27.refs_1_ = bf16[64,2048]{1,0:T(8,128)(2,1)S(1)} collective-permute-done((bf16[64,2048]{1,0:T(8,128)(2,1)S(1)}, bf16[64,2048]{1,0:T(8,128)(2,1)S(1)}, u32[]{:S(2)}, u32[]{:S(2)}) %collective-permute-start.27) | collective-permute-done | bytes 262176 | tf_op jit(solution)/shard_map/ppermute | solution.py:236
  27.6 0.9 %collective-permute-start.38 = (bf16[224,640]{1,0:T(8,128)(2,1)S(1)}, bf16[224,640]{1,0:T(8,128)(2,1)S(1)}, u32[]{:S(2)}, u32[]{:S(2)}) collective-permute-start(bf16[224,640]{1,0:T(8,128)(2,1)S(1)} %collective-permute-done.35.refs_11_), channel_id=1, source_target_pairs={{0,1},{1,2},{2,3},{3,4},{4,5},{5,6},{6,7},{7,0},{8,15},{9,8},{10,9... | collective-permute-start | bytes 860168 | tf_op jit(solution)/shard_map/ppermute | solution.py:228
  28.6 1.9 %collective-permute-start.30 = (bf16[64,2048]{1,0:T(8,128)(2,1)S(1)}, bf16[64,2048]{1,0:T(8,128)(2,1)S(1)}, u32[]{:S(2)}, u32[]{:S(2)}) collective-permute-start(bf16[64,2048]{1,0:T(8,128)(2,1)S(1)} %stack.2.refs_0_), channel_id=1, source_target_pairs={{0,8},{8,0},{16,24},{24,16},{32,40},{40,32},{48,56},{56,48},{64,72... | collective-permute-start | bytes 786440 | tf_op jit(solution)/shard_map/ppermute | solution.py:232
  30.5 1.1 %collective-permute-start.39 = (bf16[224,640]{1,0:T(8,128)(2,1)}, bf16[224,640]{1,0:T(8,128)(2,1)}, u32[]{:S(2)}, u32[]{:S(2)}) collective-permute-start(bf16[224,640]{1,0:T(8,128)(2,1)} %collective-permute-done.36), channel_id=1, source_target_pairs={{0,1},{1,2},{2,3},{3,4},{4,5},{5,6},{6,7},{7,0},{8,15},{9,8},{10,9... | collective-permute-start | bytes 860168 | tf_op jit(solution)/shard_map/ppermute | solution.py:228
  31.6 1.1 %collective-permute-start.31 = (bf16[64,2048]{1,0:T(8,128)(2,1)S(1)}, bf16[64,2048]{1,0:T(8,128)(2,1)S(1)}, u32[]{:S(2)}, u32[]{:S(2)}) collective-permute-start(bf16[64,2048]{1,0:T(8,128)(2,1)S(1)} %collective-permute-done.27.refs_1_), channel_id=1, source_target_pairs={{0,8},{8,0},{16,24},{24,16},{32,40},{40,32},{48,56},{56,48},{64,72... | collective-permute-start | bytes 786440 | tf_op jit(solution)/shard_map/ppermute | solution.py:232
  32.7 0.7 %copy-done.5 = bf16[64,2048]{1,0:T(8,128)(2,1)} copy-done((bf16[64,2048]{1,0:T(8,128)(2,1)}, bf16[64,2048]{1,0:T(8,128)(2,1)S(1)}, u32[]{:S(2)}) %copy-start.5) | copy-done | bytes 262168
  33.4 0.5 %collective-permute-start.32 = (bf16[64,2048]{1,0:T(8,128)(2,1)}, bf16[64,2048]{1,0:T(8,128)(2,1)}, u32[]{:S(2)}, u32[]{:S(2)}) collective-permute-start(bf16[64,2048]{1,0:T(8,128)(2,1)} %collective-permute-done.28.refs_2_), channel_id=1, source_target_pairs={{0,8},{8,0},{16,24},{24,16},{32,40},{40,32},{48,56},{56,48},{64,72... | collective-permute-start | bytes 786440 | tf_op jit(solution)/shard_map/ppermute | solution.py:232
  33.9 0.5 %collective-permute-done.38.refs_13_ = bf16[224,640]{1,0:T(8,128)(2,1)S(1)} collective-permute-done((bf16[224,640]{1,0:T(8,128)(2,1)S(1)}, bf16[224,640]{1,0:T(8,128)(2,1)S(1)}, u32[]{:S(2)}, u32[]{:S(2)}) %collective-permute-start.38) | collective-permute-done | bytes 286752 | tf_op jit(solution)/shard_map/ppermute | solution.py:228
  34.4 0.8 %collective-permute-start.33 = (bf16[64,2048]{1,0:T(8,128)(2,1)}, bf16[64,2048]{1,0:T(8,128)(2,1)}, u32[]{:S(2)}, u32[]{:S(2)}) collective-permute-start(bf16[64,2048]{1,0:T(8,128)(2,1)} %collective-permute-done.29.refs_3_), channel_id=1, source_target_pairs={{0,8},{8,0},{16,24},{24,16},{32,40},{40,32},{48,56},{56,48},{64,72... | collective-permute-start | bytes 786440 | tf_op jit(solution)/shard_map/ppermute | solution.py:232
  35.2 0.7 %copy-done.7 = bf16[64,2048]{1,0:T(8,128)(2,1)} copy-done((bf16[64,2048]{1,0:T(8,128)(2,1)}, bf16[64,2048]{1,0:T(8,128)(2,1)S(1)}, u32[]{:S(2)}) %copy-start.7) | copy-done | bytes 262168
  35.9 1.7 %collective-permute-start.41 = (bf16[224,640]{1,0:T(8,128)(2,1)S(1)}, bf16[224,640]{1,0:T(8,128)(2,1)S(1)}, u32[]{:S(2)}, u32[]{:S(2)}) collective-permute-start(bf16[224,640]{1,0:T(8,128)(2,1)S(1)} %collective-permute-done.38.refs_13_), channel_id=1, source_target_pairs={{0,1},{1,2},{2,3},{3,4},{4,5},{5,6},{6,7},{7,0},{8,15},{9,8},{10,9... | collective-permute-start | bytes 860168 | tf_op jit(solution)/shard_map/ppermute | solution.py:228
  37.7 1.5 %collective-permute-start.40 = (bf16[224,640]{1,0:T(8,128)(2,1)}, bf16[224,640]{1,0:T(8,128)(2,1)S(1)}, u32[]{:S(2)}, u32[]{:S(2)}) collective-permute-start(bf16[224,640]{1,0:T(8,128)(2,1)} %collective-permute-done.39), channel_id=1, source_target_pairs={{0,8},{8,0},{16,24},{24,16},{32,40},{40,32},{48,56},{56,48},{64,72... | collective-permute-start | bytes 860168 | tf_op jit(solution)/shard_map/ppermute | solution.py:232
  39.2 0.9 %copy-done.6 = bf16[64,2048]{1,0:T(8,128)(2,1)S(1)} copy-done((bf16[64,2048]{1,0:T(8,128)(2,1)S(1)}, bf16[64,2048]{1,0:T(8,128)(2,1)}, u32[]{:S(2)}) %copy-start.6) | copy-done | bytes 262168
  40.2 0.9 %copy-done.8 = bf16[64,2048]{1,0:T(8,128)(2,1)S(1)} copy-done((bf16[64,2048]{1,0:T(8,128)(2,1)S(1)}, bf16[64,2048]{1,0:T(8,128)(2,1)}, u32[]{:S(2)}) %copy-start.8) | copy-done | bytes 262168
  41.1 3.6 %contract_early.2 = (f32[512,640]{1,0:T(8,128)S(1)}, f32[512,640]{1,0:T(8,128)S(1)}, bf16[512,512]{1,0:T(8,128)(2,1)S(1)}) custom-call(s32[640]{0:T(1024)S(1)} %copy-done.14, f32[640]{0:T(1024)S(1)} %copy-done.15, s32[64]{0:T(128)S(1)} %copy-done.16, f32[64]{0:T(128)S(1)} %copy-done.17, s32[2]{0:T(128)S(1)} %copy-done.18, s32[640]{0:T(1024)S(1)} %copy-done.14, ...), custom_call_target="tpu_custom_call" | custom-call | flops 1006632960 | bytes 41943040 | tf_op jit(solution)/shard_map/contract_early/pallas_call | solution.py:290
  44.7 1.7 %contract_late.2 = f32[512,640]{1,0:T(8,128)} custom-call(f32[512,640]{1,0:T(8,128)S(1)} %get-tuple-element.82.sum_ref, f32[512,640]{1,0:T(8,128)S(1)} %get-tuple-element.83.scale_ref, bf16[512,512]{1,0:T(8,128)(2,1)S(1)} %get-tuple-element.84.late, bf16[224,640]{1,0:T(8,128)(2,1)S(1)} %collective-permute-done.40.refs_0_, ...), custom_call_target="tpu_custom_call" | custom-call | tf_op jit(solution)/shard_map/contract_late/pallas_call | solution.py:312
  46.5 0.8 %while.10 = (s32[]{:T(128)}, f32[512,640]{1,0:T(8,128)}, s32[]{:T(128)}, s32[640]{0:T(1024)S(1)}, s32[1]{0:T(128)}, /*index=5*/s32[2]{0:T(128)S(1)}, bf16[1280,6...) while((s32[]{:T(128)}, f32[512,640]{1,0:T(8,128)}, ...), condition=%wide.region_1.0_spmd, body=%wide.region_0.0_spmd.sunk | while | flops 1006960640 | bytes 79332488 | solution.py:342
  (42 shorter events, 0.1 us)
Async XLA Ops:
  0.0 12.2 %copy-start.14 = (s32[640]{0:T(1024)S(1)}, s32[640]{0:T(1024)}, u32[]{:S(2)}) copy-start(s32[640]{0:T(1024)} %irrep_ref.5) | copy-start | bytes 7684
  0.0 12.2 %copy-start.11 = (bf16[16,10240]{1,0:T(8,128)(2,1)S(1)}, bf16[16,10240]{1,0:T(8,128)(2,1)}, u32[]{:S(2)}) copy-start(bf16[16,10240]{1,0:T(8,128)(2,1)} %rows_ref.1) | copy-start | bytes 983044
  0.0 12.2 %copy-start.16 = (s32[64]{0:T(128)S(1)}, s32[64]{0:T(128)}, u32[]{:S(2)}) copy-start(s32[64]{0:T(128)} %occ_irrep_ref.1) | copy-start | bytes 772
  0.7 38.5 %copy-start.4 = (bf16[512,640]{1,0:T(8,128)(2,1)S(1)}, bf16[512,640]{1,0:T(8,128)(2,1)}, u32[]{:S(2)}) copy-start(bf16[512,640]{1,0:T(8,128)(2,1)} %other_hbm.1) | copy-start | bytes 1966084
  0.7 38.5 %copy-start.15 = (f32[640]{0:T(1024)S(1)}, f32[640]{0:T(1024)}, u32[]{:S(2)}) copy-start(f32[640]{0:T(1024)} %energy_ref.1) | copy-start | bytes 7684
  0.7 38.5 %copy-start.17 = (f32[64]{0:T(128)S(1)}, f32[64]{0:T(128)}, u32[]{:S(2)}) copy-start(f32[64]{0:T(128)} %occ_energy_ref.1) | copy-start | bytes 772
  0.7 38.5 %copy-start.18 = (s32[2]{0:T(128)S(1)}, s32[2]{0:T(128)}, u32[]{:S(2)}) copy-start(s32[2]{0:T(128)} %tiles_a_s.3) | copy-start | bytes 28
  3.9 7.2 %collective-permute-start.25 = (bf16[224,640]{1,0:T(8,128)(2,1)S(1)}, bf16[224,640]{1,0:T(8,128)(2,1)S(1)}, u32[]{:S(2)}, u32[]{:S(2)}) collective-permute-start(bf16[224,640]{1,0:T(8,128)(2,1)S(1)} %get-tuple-element.79.refs_8_), channel_id=1, source_target_pairs={{0,8},{8,0},{16,24},{24,16},{32,40},{40,32},{48,56},{56,48},{64,72... | collective-permute-start | bytes 860168 | tf_op jit(solution)/shard_map/ppermute | solution.py:232
  7.2 10.4 %collective-permute-start.24 = (bf16[224,640]{1,0:T(8,128)(2,1)S(1)}, bf16[224,640]{1,0:T(8,128)(2,1)S(1)}, u32[]{:S(2)}, u32[]{:S(2)}) collective-permute-start(bf16[224,640]{1,0:T(8,128)(2,1)S(1)} %get-tuple-element.79.refs_8_), channel_id=1, source_target_pairs={{0,1},{1,2},{2,3},{3,4},{4,5},{5,6},{6,7},{7,0},{8,15},{9,8},{10,9... | collective-permute-start | bytes 860168 | tf_op jit(solution)/shard_map/ppermute | solution.py:228
  11.0 9.7 %collective-permute-start.26 = (bf16[224,640]{1,0:T(8,128)(2,1)S(1)}, bf16[224,640]{1,0:T(8,128)(2,1)S(1)}, u32[]{:S(2)}, u32[]{:S(2)}) collective-permute-start(bf16[224,640]{1,0:T(8,128)(2,1)S(1)} %collective-permute-done.25), channel_id=1, source_target_pairs={{0,1},{1,2},{2,3},{3,4},{4,5},{5,6},{6,7},{7,0},{8,15},{9,8},{10,9... | collective-permute-start | bytes 860168 | tf_op jit(solution)/shard_map/ppermute | solution.py:228
  13.2 5.2 %collective-permute-start.21 = (bf16[16,2048]{1,0:T(8,128)(2,1)S(1)}, bf16[16,2048]{1,0:T(8,128)(2,1)S(1)}, u32[]{:S(2)}, u32[]{:S(2)}) collective-permute-start(bf16[16,2048]{1,0:T(8,128)(2,1)S(1)} %pack_amplitudes.2.refs_0_), channel_id=1, source_target_pairs={{0,16},{8,72},{16,32},{24,88},{32,48},{40,104},{48,0},{56,120},{64... | collective-permute-start | bytes 196616 | tf_op jit(solution)/shard_map/ppermute | solution.py:236
  14.5 3.8 %collective-permute-start.22 = (bf16[16,2048]{1,0:T(8,128)(2,1)S(1)}, bf16[16,2048]{1,0:T(8,128)(2,1)S(1)}, u32[]{:S(2)}, u32[]{:S(2)}) collective-permute-start(bf16[16,2048]{1,0:T(8,128)(2,1)S(1)} %pack_amplitudes.2.refs_0_), channel_id=1, source_target_pairs={{0,48},{8,200},{16,0},{24,216},{32,16},{40,232},{48,32},{56,248},{... | collective-permute-start | bytes 196616 | tf_op jit(solution)/shard_map/ppermute | solution.py:236
  16.1 4.6 %collective-permute-start.23 = (bf16[16,2048]{1,0:T(8,128)(2,1)S(1)}, bf16[16,2048]{1,0:T(8,128)(2,1)S(1)}, u32[]{:S(2)}, u32[]{:S(2)}) collective-permute-start(bf16[16,2048]{1,0:T(8,128)(2,1)S(1)} %pack_amplitudes.2.refs_0_), channel_id=1, source_target_pairs={{0,32},{8,136},{16,48},{24,152},{32,0},{40,168},{48,16},{56,184},{... | collective-permute-start | bytes 196616 | tf_op jit(solution)/shard_map/ppermute | solution.py:236
  17.6 8.1 %collective-permute-start.35 = (bf16[224,640]{1,0:T(8,128)(2,1)S(1)}, bf16[224,640]{1,0:T(8,128)(2,1)S(1)}, u32[]{:S(2)}, u32[]{:S(2)}) collective-permute-start(bf16[224,640]{1,0:T(8,128)(2,1)S(1)} %collective-permute-done.24.refs_4_.refs_9_), channel_id=1, source_target_pairs={{0,1},{1,2},{2,3},{3,4},{4,5},{5,6},{6,7},{7,0},{8,15},{9,8},{10,9... | collective-permute-start | bytes 860168 | tf_op jit(solution)/shard_map/ppermute | solution.py:228
  20.7 6.9 %collective-permute-start.27 = (bf16[64,2048]{1,0:T(8,128)(2,1)S(1)}, bf16[64,2048]{1,0:T(8,128)(2,1)S(1)}, u32[]{:S(2)}, u32[]{:S(2)}) collective-permute-start(bf16[64,2048]{1,0:T(8,128)(2,1)S(1)} %stack.2.refs_0_), channel_id=1, source_target_pairs={{0,64},{8,24},{16,80},{24,40},{32,96},{40,56},{48,112},{56,8},{64,... | collective-permute-start | bytes 786440 | tf_op jit(solution)/shard_map/ppermute | solution.py:236
  22.0 6.5 %collective-permute-start.28 = (bf16[64,2048]{1,0:T(8,128)(2,1)S(1)}, bf16[64,2048]{1,0:T(8,128)(2,1)}, u32[]{:S(2)}, u32[]{:S(2)}) collective-permute-start(bf16[64,2048]{1,0:T(8,128)(2,1)S(1)} %stack.2.refs_0_), channel_id=1, source_target_pairs={{0,192},{8,56},{16,208},{24,8},{32,224},{40,24},{48,240},{56,40},{... | collective-permute-start | bytes 786440 | tf_op jit(solution)/shard_map/ppermute | solution.py:236
  23.5 7.0 %collective-permute-start.36 = (bf16[224,640]{1,0:T(8,128)(2,1)S(1)}, bf16[224,640]{1,0:T(8,128)(2,1)}, u32[]{:S(2)}, u32[]{:S(2)}) collective-permute-start(bf16[224,640]{1,0:T(8,128)(2,1)S(1)} %collective-permute-done.26.refs_5_), channel_id=1, source_target_pairs={{0,1},{1,2},{2,3},{3,4},{4,5},{5,6},{6,7},{7,0},{8,15},{9,8},{10,9... | collective-permute-start | bytes 860168 | tf_op jit(solution)/shard_map/ppermute | solution.py:228
  24.5 7.1 %collective-permute-start.29 = (bf16[64,2048]{1,0:T(8,128)(2,1)S(1)}, bf16[64,2048]{1,0:T(8,128)(2,1)}, u32[]{:S(2)}, u32[]{:S(2)}) collective-permute-start(bf16[64,2048]{1,0:T(8,128)(2,1)S(1)} %stack.2.refs_0_), channel_id=1, source_target_pairs={{0,128},{8,40},{16,144},{24,56},{32,160},{40,8},{48,176},{56,24},{... | collective-permute-start | bytes 786440 | tf_op jit(solution)/shard_map/ppermute | solution.py:236
  25.7 7.7 %collective-permute-start.34 = (bf16[224,640]{1,0:T(8,128)(2,1)S(1)}, bf16[224,640]{1,0:T(8,128)(2,1)S(1)}, u32[]{:S(2)}, u32[]{:S(2)}) collective-permute-start(bf16[224,640]{1,0:T(8,128)(2,1)S(1)} %collective-permute-done.26.refs_5_), channel_id=1, source_target_pairs={{0,8},{8,0},{16,24},{24,16},{32,40},{40,32},{48,56},{56,48},{64,72... | collective-permute-start | bytes 860168 | tf_op jit(solution)/shard_map/ppermute | solution.py:232
  27.6 6.8 %collective-permute-start.38 = (bf16[224,640]{1,0:T(8,128)(2,1)S(1)}, bf16[224,640]{1,0:T(8,128)(2,1)S(1)}, u32[]{:S(2)}, u32[]{:S(2)}) collective-permute-start(bf16[224,640]{1,0:T(8,128)(2,1)S(1)} %collective-permute-done.35.refs_11_), channel_id=1, source_target_pairs={{0,1},{1,2},{2,3},{3,4},{4,5},{5,6},{6,7},{7,0},{8,15},{9,8},{10,9... | collective-permute-start | bytes 860168 | tf_op jit(solution)/shard_map/ppermute | solution.py:228
  28.6 4.2 %collective-permute-start.30 = (bf16[64,2048]{1,0:T(8,128)(2,1)S(1)}, bf16[64,2048]{1,0:T(8,128)(2,1)S(1)}, u32[]{:S(2)}, u32[]{:S(2)}) collective-permute-start(bf16[64,2048]{1,0:T(8,128)(2,1)S(1)} %stack.2.refs_0_), channel_id=1, source_target_pairs={{0,8},{8,0},{16,24},{24,16},{32,40},{40,32},{48,56},{56,48},{64,72... | collective-permute-start | bytes 786440 | tf_op jit(solution)/shard_map/ppermute | solution.py:232
  30.5 7.2 %collective-permute-start.39 = (bf16[224,640]{1,0:T(8,128)(2,1)}, bf16[224,640]{1,0:T(8,128)(2,1)}, u32[]{:S(2)}, u32[]{:S(2)}) collective-permute-start(bf16[224,640]{1,0:T(8,128)(2,1)} %collective-permute-done.36), channel_id=1, source_target_pairs={{0,1},{1,2},{2,3},{3,4},{4,5},{5,6},{6,7},{7,0},{8,15},{9,8},{10,9... | collective-permute-start | bytes 860168 | tf_op jit(solution)/shard_map/ppermute | solution.py:228
  31.6 3.6 %collective-permute-start.31 = (bf16[64,2048]{1,0:T(8,128)(2,1)S(1)}, bf16[64,2048]{1,0:T(8,128)(2,1)S(1)}, u32[]{:S(2)}, u32[]{:S(2)}) collective-permute-start(bf16[64,2048]{1,0:T(8,128)(2,1)S(1)} %collective-permute-done.27.refs_1_), channel_id=1, source_target_pairs={{0,8},{8,0},{16,24},{24,16},{32,40},{40,32},{48,56},{56,48},{64,72... | collective-permute-start | bytes 786440 | tf_op jit(solution)/shard_map/ppermute | solution.py:232
  33.4 5.7 %collective-permute-start.37 = (bf16[224,640]{1,0:T(8,128)(2,1)}, bf16[224,640]{1,0:T(8,128)(2,1)S(1)}, u32[]{:S(2)}, u32[]{:S(2)}) collective-permute-start(bf16[224,640]{1,0:T(8,128)(2,1)} %collective-permute-done.36), channel_id=1, source_target_pairs={{0,8},{8,0},{16,24},{24,16},{32,40},{40,32},{48,56},{56,48},{64,72... | collective-permute-start | bytes 860168 | tf_op jit(solution)/shard_map/ppermute | solution.py:232
  33.4 5.7 %collective-permute-start.32 = (bf16[64,2048]{1,0:T(8,128)(2,1)}, bf16[64,2048]{1,0:T(8,128)(2,1)}, u32[]{:S(2)}, u32[]{:S(2)}) collective-permute-start(bf16[64,2048]{1,0:T(8,128)(2,1)} %collective-permute-done.28.refs_2_), channel_id=1, source_target_pairs={{0,8},{8,0},{16,24},{24,16},{32,40},{40,32},{48,56},{56,48},{64,72... | collective-permute-start | bytes 786440 | tf_op jit(solution)/shard_map/ppermute | solution.py:232
  34.4 4.7 %collective-permute-start.33 = (bf16[64,2048]{1,0:T(8,128)(2,1)}, bf16[64,2048]{1,0:T(8,128)(2,1)}, u32[]{:S(2)}, u32[]{:S(2)}) collective-permute-start(bf16[64,2048]{1,0:T(8,128)(2,1)} %collective-permute-done.29.refs_3_), channel_id=1, source_target_pairs={{0,8},{8,0},{16,24},{24,16},{32,40},{40,32},{48,56},{56,48},{64,72... | collective-permute-start | bytes 786440 | tf_op jit(solution)/shard_map/ppermute | solution.py:232
  35.9 8.8 %collective-permute-start.41 = (bf16[224,640]{1,0:T(8,128)(2,1)S(1)}, bf16[224,640]{1,0:T(8,128)(2,1)S(1)}, u32[]{:S(2)}, u32[]{:S(2)}) collective-permute-start(bf16[224,640]{1,0:T(8,128)(2,1)S(1)} %collective-permute-done.38.refs_13_), channel_id=1, source_target_pairs={{0,1},{1,2},{2,3},{3,4},{4,5},{5,6},{6,7},{7,0},{8,15},{9,8},{10,9... | collective-permute-start | bytes 860168 | tf_op jit(solution)/shard_map/ppermute | solution.py:228
  37.7 7.0 %collective-permute-start.40 = (bf16[224,640]{1,0:T(8,128)(2,1)}, bf16[224,640]{1,0:T(8,128)(2,1)S(1)}, u32[]{:S(2)}, u32[]{:S(2)}) collective-permute-start(bf16[224,640]{1,0:T(8,128)(2,1)} %collective-permute-done.39), channel_id=1, source_target_pairs={{0,8},{8,0},{16,24},{24,16},{32,40},{40,32},{48,56},{56,48},{64,72... | collective-permute-start | bytes 860168 | tf_op jit(solution)/shard_map/ppermute | solution.py:232
  39.2 1.0 %copy-start.6 = (bf16[64,2048]{1,0:T(8,128)(2,1)S(1)}, bf16[64,2048]{1,0:T(8,128)(2,1)}, u32[]{:S(2)}) copy-start(bf16[64,2048]{1,0:T(8,128)(2,1)} %copy-done.5) | copy-start | bytes 786436
  40.2 0.9 %copy-start.8 = (bf16[64,2048]{1,0:T(8,128)(2,1)S(1)}, bf16[64,2048]{1,0:T(8,128)(2,1)}, u32[]{:S(2)}) copy-start(bf16[64,2048]{1,0:T(8,128)(2,1)} %copy-done.7) | copy-start | bytes 786436
  44.7 1.8 %copy-start.9 = (bf16[1280,640]{1,0:T(8,128)(2,1)S(1)}, bf16[1280,640]{1,0:T(8,128)(2,1)}, u32[]{:S(2)}) copy-start(bf16[1280,640]{1,0:T(8,128)(2,1)} %panel_hbm.1) | copy-start | bytes 4915204
  44.7 1.8 %copy-start.12 = (bf16[16,10240]{1,0:T(8,128)(2,1)S(1)}, bf16[16,10240]{1,0:T(8,128)(2,1)}, u32[]{:S(2)}) copy-start(bf16[16,10240]{1,0:T(8,128)(2,1)} %rows_ref.1) | copy-start | bytes 983044
  (2 other events, 1.4 us)

commit v5 on v4

--- a/solution.py
+++ b/solution.py
@@ -26,6 +26,27 @@
 
 def params(mib):
     return pltpu.CompilerParams(vmem_limit_bytes=mib * 1024 * 1024)
+
+
+def ranks(irreps):
+    tiles = [irreps[:, tile:tile + PITCH] for tile in range(0, NVIR, PITCH)]
+    group = lax.broadcasted_iota(jnp.int32, (IRREPS, PITCH), 0)
+    members = [jnp.where(tile == group, 1.0, 0.0) for tile in tiles]
+    earlier = lax.broadcasted_iota(jnp.int32, (PITCH, PITCH), 0) < lax.broadcasted_iota(
+        jnp.int32, (PITCH, PITCH), 1
+    )
+    inside = jnp.dot(
+        jnp.concatenate(members, axis=0).astype(jnp.bfloat16),
+        earlier.astype(jnp.bfloat16),
+        preferred_element_type=jnp.float32,
+    )
+    found = []
+    so_far = jnp.zeros((IRREPS, 1), jnp.float32)
+    for index, member in enumerate(members):
+        before = inside[index * IRREPS:(index + 1) * IRREPS, :] + so_far
+        found.append(jnp.sum(member * before, axis=0, keepdims=True))
+        so_far = so_far + jnp.sum(member, axis=1, keepdims=True)
+    return jnp.concatenate(found, axis=1).astype(jnp.int32)
 
 
 def pack_integrals(
@@ -42,17 +63,7 @@
         fetch.start()
     wide, narrow = lax.axis_index("wide"), lax.axis_index("narrow")
     irreps = irrep_ref[...].reshape(1, NVIR)
-    group = lax.broadcasted_iota(jnp.int32, (IRREPS, NVIR), 0)
-    member = irreps == group
-    earlier = lax.broadcasted_iota(jnp.int32, (NVIR, NVIR), 0) < lax.broadcasted_iota(
-        jnp.int32, (NVIR, NVIR), 1
-    )
-    before = jnp.dot(
-        member.astype(jnp.bfloat16),
-        earlier.astype(jnp.bfloat16),
-        preferred_element_type=jnp.float32,
-    )
-    rank = jnp.sum(jnp.where(member, before, 0.0), axis=0, keepdims=True).astype(jnp.int32)
+    rank = ranks(irreps)
     slots = lax.broadcasted_iota(jnp.int32, (PITCH, NVIR), 0)
     picks = ((slots == rank - base_s[0]) & (slots < CAP)).astype(jnp.bfloat16)
     picks_ref[...] = picks
@@ -159,13 +170,10 @@
 def contract_early(
     steps, split,
     irrep_s, energy_s, occ_irrep_s, occ_energy_s, tiles_a_s,
-    irrep_ref, energy_ref, occ_irrep_ref, occ_energy_ref, other_hbm, *refs,
+    irrep_ref, energy_ref, occ_irrep_ref, occ_energy_ref, other, *refs,
 ):
-    pieces_hbm, strips = refs[:2 * SIDE], refs[2 * SIDE:-7]
-    sum_ref, scale_ref, late_ref, other, ordered, panel, arrived = refs[-7:]
-    fetches = [pltpu.make_async_copy(other_hbm, other, arrived.at[0])]
-    for fetch in fetches:
-        fetch.start()
+    pieces_hbm, strips = refs[:2 * SIDE], refs[2 * SIDE:-5]
+    sum_ref, scale_ref, late_ref, ordered, panel = refs[-5:]
     fill(panel, strips)
     wide, narrow = lax.axis_index("wide"), lax.axis_index("narrow")
     a = tiles_a_s[wide // TILE] * TILE + wide % TILE
@@ -179,8 +187,6 @@
         denom = (occ_energy_s[i] + j_energy) - col_energy
         same = (j_sym ^ occ_irrep_s[i]) == col_sym
         scale_ref[local * NOCC:(local + 1) * NOCC, :] = jnp.where(same, 1.0 / denom, 0.0)
-    for fetch in fetches:
-        fetch.wait()
     groups = [(pieces_hbm[index], index % SIDE, index >= SIDE) for index in range(2 * SIDE)]
     place_rows(steps, split, groups, ordered, late_ref)
     sum_ref[...] = other[...].astype(jnp.float32) + jnp.dot(
@@ -292,13 +298,11 @@
         out_shape=(
             full, full, jax.ShapeDtypeStruct((height, (RING - early) * span), amplitudes.dtype)
         ),
-        in_specs=[SMEM] * 5 + [VMEM] * 4 + [HBM] + [VMEM] * (2 * SIDE + early),
+        in_specs=[SMEM] * 5 + [VMEM] * 4 + [VMEM] * (1 + 2 * SIDE + early),
         out_specs=(VMEM,) * 3,
         scratch_shapes=[
-            pltpu.VMEM(other_terms.shape, other_terms.dtype),
             pltpu.VMEM((height, early * span), amplitudes.dtype),
             pltpu.VMEM((early * span, NVIR), integrals.dtype),
-            pltpu.SemaphoreType.DMA((2 * SIDE + 1,)),
         ],
         cost_estimate=pl.CostEstimate(
             flops=2 * height * early * span * NVIR, bytes_accessed=40 * 2**20, transcendentals=0

time: 47.7 us -> 47.3 us (level)
  Pallas kernels: 9.37 us -> 8.89 us
    pallas_call x1, Pallas kernels: 3.59 us -> 3.11 us  [one_pass(): pl.pallas_call(functools.partial(contract_early, steps, early), out_shape...]
  transfers between devices with their start and end apart: 21 -> 21, of which waited for: 3 -> 3; matrix products, arithmetic and copies ran while one was open for 0% -> 0% of each run, Pallas kernels for 10% -> 9%
where the time goes in v5:
time: 47.3 us; the launch traced here: 47 us
  starting transfers between devices  29.1 us (62%)
  Pallas kernels  8.89 us (19%)
  waiting for transfers between devices  3.85 us (8%)
  local copies, waits for them, and re-layouts  3.34 us (7%)
  between operations  1.08 us (2%)
  loops' own time  0.81 us (2%)
    ppermute x7, starting transfers between devices, hop(): return lax.ppermute(part, ('wide', 'narrow'), along_ring())  10.6 us
    ppermute x8, starting transfers between devices, swap(): return lax.ppermute(part, 'wide', [(i, i ^ 1) for i in range(32)])  10 us
    ppermute x6, starting transfers between devices, to(): return lax.ppermute(part, 'wide', pairs)  8.44 us
    unnamed x26, local copies, waits for them, and re-layouts  3.34 us
    ppermute x6, waiting for transfers between devices, to(): return lax.ppermute(part, 'wide', pairs)  3.33 us
    pallas_call x1, Pallas kernels, one_pass(): pl.pallas_call(pack_integrals, out_shape=(jax.ShapeDtypeStruct((E_LOCAL *...  3.11 us
    pallas_call x1, Pallas kernels, one_pass(): pl.pallas_call(functools.partial(contract_early, steps, early), out_shape...  3.11 us
    pallas_call x1, Pallas kernels, one_pass(): pl.pallas_call(contract_late, out_shape=full, in_specs=[VMEM] * (3 + RING...  1.73 us
  transfers between devices with their start and end apart: 21, of which 3 were waited for; matrix products, arithmetic and copies ran while one was open for 0% of the time, Pallas kernels for 9%

profile of v5, /device:TPU:1, one launch (start us, length us, event | category | flops | bytes accessed | tf_op | source)
XLA Modules:
  0.0 47.0 jit_solution(14446875558887876421)
XLA Ops:
  0.7 3.1 %pack_integrals.2 = (bf16[224,640]{1,0:T(8,128)(2,1)S(1)}, bf16[128,640]{1,0:T(8,128)(2,1)S(1)}, s32[1]{0:T(128)}) custom-call(s32[1]{0:T(128)} %constant.3.clone.1.base_s, s32[640]{0:T(1024)} %irrep_ref.5, s32[1]{0:T(128)S(6)} %copy.16.tiles_e_s, s32[2]{0:T(128)} %tiles_a_s.3, s32[640]{0:T(1024)} %irrep_ref.5, bf16[1280,640]{1,0:T(8,128)(2,1)} %panel_hbm.1), custom_call_target="tpu_custom_call" | custom-call | tf_op jit(solution)/shard_map/pack_integrals/pallas_call | solution.py:251
  3.9 3.3 %collective-permute-start.25 = (bf16[224,640]{1,0:T(8,128)(2,1)S(1)}, bf16[224,640]{1,0:T(8,128)(2,1)S(1)}, u32[]{:S(2)}, u32[]{:S(2)}) collective-permute-start(bf16[224,640]{1,0:T(8,128)(2,1)S(1)} %get-tuple-element.79.refs_8_), channel_id=1, source_target_pairs={{0,8},{8,0},{16,24},{24,16},{32,40},{40,32},{48,56},{56,48},{64,72... | collective-permute-start | bytes 860168 | tf_op jit(solution)/shard_map/ppermute | solution.py:238
  7.2 3.8 %collective-permute-start.24 = (bf16[224,640]{1,0:T(8,128)(2,1)S(1)}, bf16[224,640]{1,0:T(8,128)(2,1)S(1)}, u32[]{:S(2)}, u32[]{:S(2)}) collective-permute-start(bf16[224,640]{1,0:T(8,128)(2,1)S(1)} %get-tuple-element.79.refs_8_), channel_id=1, source_target_pairs={{0,1},{1,2},{2,3},{3,4},{4,5},{5,6},{6,7},{7,0},{8,15},{9,8},{10,9... | collective-permute-start | bytes 860168 | tf_op jit(solution)/shard_map/ppermute | solution.py:234
  11.0 1.2 %collective-permute-start.26 = (bf16[224,640]{1,0:T(8,128)(2,1)S(1)}, bf16[224,640]{1,0:T(8,128)(2,1)S(1)}, u32[]{:S(2)}, u32[]{:S(2)}) collective-permute-start(bf16[224,640]{1,0:T(8,128)(2,1)S(1)} %collective-permute-done.25), channel_id=1, source_target_pairs={{0,1},{1,2},{2,3},{3,4},{4,5},{5,6},{6,7},{7,0},{8,15},{9,8},{10,9... | collective-permute-start | bytes 860168 | tf_op jit(solution)/shard_map/ppermute | solution.py:234
  12.2 0.9 %pack_amplitudes.2.refs_0_ = bf16[16,2048]{1,0:T(8,128)(2,1)S(1)} custom-call(s32[640]{0:T(1024)S(1)} %copy-done.14, s32[64]{0:T(128)S(1)} %copy-done.16, s32[1]{0:T(128)S(6)} %copy.16.tiles_e_s, s32[640]{0:T(1024)S(1)} %copy-done.14, bf16[128,640]{1,0:T(8,128)(2,1)S(1)} %get-tuple-element.78.picks_ref, bf16[16,10240]{1,0:T(8,128)(2,1)S(1)} %copy-done.11), custom_call_target="tpu_custom_call" | custom-call | tf_op jit(solution)/shard_map/pack_amplitudes/pallas_call | solution.py:267
  13.2 1.4 %collective-permute-start.21 = (bf16[16,2048]{1,0:T(8,128)(2,1)S(1)}, bf16[16,2048]{1,0:T(8,128)(2,1)S(1)}, u32[]{:S(2)}, u32[]{:S(2)}) collective-permute-start(bf16[16,2048]{1,0:T(8,128)(2,1)S(1)} %pack_amplitudes.2.refs_0_), channel_id=1, source_target_pairs={{0,16},{8,72},{16,32},{24,88},{32,48},{40,104},{48,0},{56,120},{64... | collective-permute-start | bytes 196616 | tf_op jit(solution)/shard_map/ppermute | solution.py:242
  14.6 1.5 %collective-permute-start.22 = (bf16[16,2048]{1,0:T(8,128)(2,1)S(1)}, bf16[16,2048]{1,0:T(8,128)(2,1)S(1)}, u32[]{:S(2)}, u32[]{:S(2)}) collective-permute-start(bf16[16,2048]{1,0:T(8,128)(2,1)S(1)} %pack_amplitudes.2.refs_0_), channel_id=1, source_target_pairs={{0,48},{8,200},{16,0},{24,216},{32,16},{40,232},{48,32},{56,248},{... | collective-permute-start | bytes 196616 | tf_op jit(solution)/shard_map/ppermute | solution.py:242
  16.1 1.6 %collective-permute-start.23 = (bf16[16,2048]{1,0:T(8,128)(2,1)S(1)}, bf16[16,2048]{1,0:T(8,128)(2,1)S(1)}, u32[]{:S(2)}, u32[]{:S(2)}) collective-permute-start(bf16[16,2048]{1,0:T(8,128)(2,1)S(1)} %pack_amplitudes.2.refs_0_), channel_id=1, source_target_pairs={{0,32},{8,136},{16,48},{24,152},{32,0},{40,168},{48,16},{56,184},{... | collective-permute-start | bytes 196616 | tf_op jit(solution)/shard_map/ppermute | solution.py:242
  17.6 0.7 %collective-permute-start.35 = (bf16[224,640]{1,0:T(8,128)(2,1)S(1)}, bf16[224,640]{1,0:T(8,128)(2,1)S(1)}, u32[]{:S(2)}, u32[]{:S(2)}) collective-permute-start(bf16[224,640]{1,0:T(8,128)(2,1)S(1)} %collective-permute-done.24.refs_4_.refs_9_), channel_id=1, source_target_pairs={{0,1},{1,2},{2,3},{3,4},{4,5},{5,6},{6,7},{7,0},{8,15},{9,8},{10,9... | collective-permute-start | bytes 860168 | tf_op jit(solution)/shard_map/ppermute | solution.py:234
  18.4 2.3 %collective-permute-done.23.refs_3_ = bf16[16,2048]{1,0:T(8,128)(2,1)S(1)} collective-permute-done((bf16[16,2048]{1,0:T(8,128)(2,1)S(1)}, bf16[16,2048]{1,0:T(8,128)(2,1)S(1)}, u32[]{:S(2)}, u32[]{:S(2)}) %collective-permute-start.23) | collective-permute-done | bytes 65568 | tf_op jit(solution)/shard_map/ppermute | solution.py:242
  20.7 1.3 %collective-permute-start.27 = (bf16[64,2048]{1,0:T(8,128)(2,1)S(1)}, bf16[64,2048]{1,0:T(8,128)(2,1)S(1)}, u32[]{:S(2)}, u32[]{:S(2)}) collective-permute-start(bf16[64,2048]{1,0:T(8,128)(2,1)S(1)} %stack.2.refs_0_), channel_id=1, source_target_pairs={{0,64},{8,24},{16,80},{24,40},{32,96},{40,56},{48,112},{56,8},{64,... | collective-permute-start | bytes 786440 | tf_op jit(solution)/shard_map/ppermute | solution.py:242
  22.0 1.5 %collective-permute-start.28 = (bf16[64,2048]{1,0:T(8,128)(2,1)S(1)}, bf16[64,2048]{1,0:T(8,128)(2,1)}, u32[]{:S(2)}, u32[]{:S(2)}) collective-permute-start(bf16[64,2048]{1,0:T(8,128)(2,1)S(1)} %stack.2.refs_0_), channel_id=1, source_target_pairs={{0,192},{8,56},{16,208},{24,8},{32,224},{40,24},{48,240},{56,40},{... | collective-permute-start | bytes 786440 | tf_op jit(solution)/shard_map/ppermute | solution.py:242
  23.5 1.0 %collective-permute-start.36 = (bf16[224,640]{1,0:T(8,128)(2,1)S(1)}, bf16[224,640]{1,0:T(8,128)(2,1)}, u32[]{:S(2)}, u32[]{:S(2)}) collective-permute-start(bf16[224,640]{1,0:T(8,128)(2,1)S(1)} %collective-permute-done.26.refs_5_), channel_id=1, source_target_pairs={{0,1},{1,2},{2,3},{3,4},{4,5},{5,6},{6,7},{7,0},{8,15},{9,8},{10,9... | collective-permute-start | bytes 860168 | tf_op jit(solution)/shard_map/ppermute | solution.py:234
  24.5 1.2 %collective-permute-start.29 = (bf16[64,2048]{1,0:T(8,128)(2,1)S(1)}, bf16[64,2048]{1,0:T(8,128)(2,1)}, u32[]{:S(2)}, u32[]{:S(2)}) collective-permute-start(bf16[64,2048]{1,0:T(8,128)(2,1)S(1)} %stack.2.refs_0_), channel_id=1, source_target_pairs={{0,128},{8,40},{16,144},{24,56},{32,160},{40,8},{48,176},{56,24},{... | collective-permute-start | bytes 786440 | tf_op jit(solution)/shard_map/ppermute | solution.py:242
  25.7 0.9 %collective-permute-start.34 = (bf16[224,640]{1,0:T(8,128)(2,1)S(1)}, bf16[224,640]{1,0:T(8,128)(2,1)S(1)}, u32[]{:S(2)}, u32[]{:S(2)}) collective-permute-start(bf16[224,640]{1,0:T(8,128)(2,1)S(1)} %collective-permute-done.26.refs_5_), channel_id=1, source_target_pairs={{0,8},{8,0},{16,24},{24,16},{32,40},{40,32},{48,56},{56,48},{64,72... | collective-permute-start | bytes 860168 | tf_op jit(solution)/shard_map/ppermute | solution.py:238
  26.7 1.0 %collective-permute-done.27.refs_1_ = bf16[64,2048]{1,0:T(8,128)(2,1)S(1)} collective-permute-done((bf16[64,2048]{1,0:T(8,128)(2,1)S(1)}, bf16[64,2048]{1,0:T(8,128)(2,1)S(1)}, u32[]{:S(2)}, u32[]{:S(2)}) %collective-permute-start.27) | collective-permute-done | bytes 262176 | tf_op jit(solution)/shard_map/ppermute | solution.py:242
  27.6 0.9 %collective-permute-start.38 = (bf16[224,640]{1,0:T(8,128)(2,1)S(1)}, bf16[224,640]{1,0:T(8,128)(2,1)S(1)}, u32[]{:S(2)}, u32[]{:S(2)}) collective-permute-start(bf16[224,640]{1,0:T(8,128)(2,1)S(1)} %collective-permute-done.35.refs_11_), channel_id=1, source_target_pairs={{0,1},{1,2},{2,3},{3,4},{4,5},{5,6},{6,7},{7,0},{8,15},{9,8},{10,9... | collective-permute-start | bytes 860168 | tf_op jit(solution)/shard_map/ppermute | solution.py:234
  28.6 1.9 %collective-permute-start.30 = (bf16[64,2048]{1,0:T(8,128)(2,1)S(1)}, bf16[64,2048]{1,0:T(8,128)(2,1)S(1)}, u32[]{:S(2)}, u32[]{:S(2)}) collective-permute-start(bf16[64,2048]{1,0:T(8,128)(2,1)S(1)} %stack.2.refs_0_), channel_id=1, source_target_pairs={{0,8},{8,0},{16,24},{24,16},{32,40},{40,32},{48,56},{56,48},{64,72... | collective-permute-start | bytes 786440 | tf_op jit(solution)/shard_map/ppermute | solution.py:238
  30.5 1.1 %collective-permute-start.39 = (bf16[224,640]{1,0:T(8,128)(2,1)}, bf16[224,640]{1,0:T(8,128)(2,1)}, u32[]{:S(2)}, u32[]{:S(2)}) collective-permute-start(bf16[224,640]{1,0:T(8,128)(2,1)} %collective-permute-done.36), channel_id=1, source_target_pairs={{0,1},{1,2},{2,3},{3,4},{4,5},{5,6},{6,7},{7,0},{8,15},{9,8},{10,9... | collective-permute-start | bytes 860168 | tf_op jit(solution)/shard_map/ppermute | solution.py:234
  31.6 1.1 %collective-permute-start.31 = (bf16[64,2048]{1,0:T(8,128)(2,1)S(1)}, bf16[64,2048]{1,0:T(8,128)(2,1)S(1)}, u32[]{:S(2)}, u32[]{:S(2)}) collective-permute-start(bf16[64,2048]{1,0:T(8,128)(2,1)S(1)} %collective-permute-done.27.refs_1_), channel_id=1, source_target_pairs={{0,8},{8,0},{16,24},{24,16},{32,40},{40,32},{48,56},{56,48},{64,72... | collective-permute-start | bytes 786440 | tf_op jit(solution)/shard_map/ppermute | solution.py:238
  32.7 0.7 %copy-done.5 = bf16[64,2048]{1,0:T(8,128)(2,1)} copy-done((bf16[64,2048]{1,0:T(8,128)(2,1)}, bf16[64,2048]{1,0:T(8,128)(2,1)S(1)}, u32[]{:S(2)}) %copy-start.5) | copy-done | bytes 262168
  33.4 0.5 %collective-permute-start.32 = (bf16[64,2048]{1,0:T(8,128)(2,1)}, bf16[64,2048]{1,0:T(8,128)(2,1)}, u32[]{:S(2)}, u32[]{:S(2)}) collective-permute-start(bf16[64,2048]{1,0:T(8,128)(2,1)} %collective-permute-done.28.refs_2_), channel_id=1, source_target_pairs={{0,8},{8,0},{16,24},{24,16},{32,40},{40,32},{48,56},{56,48},{64,72... | collective-permute-start | bytes 786440 | tf_op jit(solution)/shard_map/ppermute | solution.py:238
  33.9 0.5 %collective-permute-done.38.refs_13_ = bf16[224,640]{1,0:T(8,128)(2,1)S(1)} collective-permute-done((bf16[224,640]{1,0:T(8,128)(2,1)S(1)}, bf16[224,640]{1,0:T(8,128)(2,1)S(1)}, u32[]{:S(2)}, u32[]{:S(2)}) %collective-permute-start.38) | collective-permute-done | bytes 286752 | tf_op jit(solution)/shard_map/ppermute | solution.py:234
  34.4 0.8 %collective-permute-start.33 = (bf16[64,2048]{1,0:T(8,128)(2,1)}, bf16[64,2048]{1,0:T(8,128)(2,1)}, u32[]{:S(2)}, u32[]{:S(2)}) collective-permute-start(bf16[64,2048]{1,0:T(8,128)(2,1)} %collective-permute-done.29.refs_3_), channel_id=1, source_target_pairs={{0,8},{8,0},{16,24},{24,16},{32,40},{40,32},{48,56},{56,48},{64,72... | collective-permute-start | bytes 786440 | tf_op jit(solution)/shard_map/ppermute | solution.py:238
  35.2 0.7 %copy-done.7 = bf16[64,2048]{1,0:T(8,128)(2,1)} copy-done((bf16[64,2048]{1,0:T(8,128)(2,1)}, bf16[64,2048]{1,0:T(8,128)(2,1)S(1)}, u32[]{:S(2)}) %copy-start.7) | copy-done | bytes 262168
  35.9 1.7 %collective-permute-start.41 = (bf16[224,640]{1,0:T(8,128)(2,1)S(1)}, bf16[224,640]{1,0:T(8,128)(2,1)S(1)}, u32[]{:S(2)}, u32[]{:S(2)}) collective-permute-start(bf16[224,640]{1,0:T(8,128)(2,1)S(1)} %collective-permute-done.38.refs_13_), channel_id=1, source_target_pairs={{0,1},{1,2},{2,3},{3,4},{4,5},{5,6},{6,7},{7,0},{8,15},{9,8},{10,9... | collective-permute-start | bytes 860168 | tf_op jit(solution)/shard_map/ppermute | solution.py:234
  37.7 1.5 %collective-permute-start.40 = (bf16[224,640]{1,0:T(8,128)(2,1)}, bf16[224,640]{1,0:T(8,128)(2,1)S(1)}, u32[]{:S(2)}, u32[]{:S(2)}) collective-permute-start(bf16[224,640]{1,0:T(8,128)(2,1)} %collective-permute-done.39), channel_id=1, source_target_pairs={{0,8},{8,0},{16,24},{24,16},{32,40},{40,32},{48,56},{56,48},{64,72... | collective-permute-start | bytes 860168 | tf_op jit(solution)/shard_map/ppermute | solution.py:238
  39.2 0.9 %copy-done.6 = bf16[64,2048]{1,0:T(8,128)(2,1)S(1)} copy-done((bf16[64,2048]{1,0:T(8,128)(2,1)S(1)}, bf16[64,2048]{1,0:T(8,128)(2,1)}, u32[]{:S(2)}) %copy-start.6) | copy-done | bytes 262168
  40.2 0.9 %copy-done.8 = bf16[64,2048]{1,0:T(8,128)(2,1)S(1)} copy-done((bf16[64,2048]{1,0:T(8,128)(2,1)S(1)}, bf16[64,2048]{1,0:T(8,128)(2,1)}, u32[]{:S(2)}) %copy-start.8) | copy-done | bytes 262168
  41.1 3.1 %contract_early.2 = (f32[512,640]{1,0:T(8,128)S(1)}, f32[512,640]{1,0:T(8,128)S(1)}, bf16[512,512]{1,0:T(8,128)(2,1)S(1)}) custom-call(s32[640]{0:T(1024)S(1)} %copy-done.14, f32[640]{0:T(1024)S(1)} %copy-done.15, s32[64]{0:T(128)S(1)} %copy-done.16, f32[64]{0:T(128)S(1)} %copy-done.17, s32[2]{0:T(128)S(1)} %copy-done.18, s32[640]{0:T(1024)S(1)} %copy-done.14, ...), custom_call_target="tpu_custom_call" | custom-call | flops 1006632960 | bytes 41943040 | tf_op jit(solution)/shard_map/contract_early/pallas_call | solution.py:296
  44.3 1.7 %contract_late.2 = f32[512,640]{1,0:T(8,128)} custom-call(f32[512,640]{1,0:T(8,128)S(1)} %get-tuple-element.82.sum_ref, f32[512,640]{1,0:T(8,128)S(1)} %get-tuple-element.83.scale_ref, bf16[512,512]{1,0:T(8,128)(2,1)S(1)} %get-tuple-element.84.late, bf16[224,640]{1,0:T(8,128)(2,1)S(1)} %collective-permute-done.40.refs_0_, ...), custom_call_target="tpu_custom_call" | custom-call | tf_op jit(solution)/shard_map/contract_late/pallas_call | solution.py:316
  46.0 0.8 %while.10 = (s32[]{:T(128)}, f32[512,640]{1,0:T(8,128)}, s32[]{:T(128)}, s32[640]{0:T(1024)S(1)}, s32[1]{0:T(128)}, /*index=5*/s32[2]{0:T(128)S(1)}, bf16[1280,6...) while((s32[]{:T(128)}, f32[512,640]{1,0:T(8,128)}, ...), condition=%wide.region_1.0_spmd, body=%wide.region_0.0_spmd.sunk | while | flops 1006960640 | bytes 79332488 | solution.py:346
  (42 shorter events, 0.1 us)
Async XLA Ops:
  0.0 12.2 %copy-start.14 = (s32[640]{0:T(1024)S(1)}, s32[640]{0:T(1024)}, u32[]{:S(2)}) copy-start(s32[640]{0:T(1024)} %irrep_ref.5) | copy-start | bytes 7684
  0.0 12.2 %copy-start.11 = (bf16[16,10240]{1,0:T(8,128)(2,1)S(1)}, bf16[16,10240]{1,0:T(8,128)(2,1)}, u32[]{:S(2)}) copy-start(bf16[16,10240]{1,0:T(8,128)(2,1)} %rows_ref.1) | copy-start | bytes 983044
  0.0 12.2 %copy-start.16 = (s32[64]{0:T(128)S(1)}, s32[64]{0:T(128)}, u32[]{:S(2)}) copy-start(s32[64]{0:T(128)} %occ_irrep_ref.1) | copy-start | bytes 772
  0.7 38.5 %copy-start.4 = (bf16[512,640]{1,0:T(8,128)(2,1)S(1)}, bf16[512,640]{1,0:T(8,128)(2,1)}, u32[]{:S(2)}) copy-start(bf16[512,640]{1,0:T(8,128)(2,1)} %other.1) | copy-start | bytes 1966084
  0.7 38.5 %copy-start.15 = (f32[640]{0:T(1024)S(1)}, f32[640]{0:T(1024)}, u32[]{:S(2)}) copy-start(f32[640]{0:T(1024)} %energy_ref.1) | copy-start | bytes 7684
  0.7 38.5 %copy-start.17 = (f32[64]{0:T(128)S(1)}, f32[64]{0:T(128)}, u32[]{:S(2)}) copy-start(f32[64]{0:T(128)} %occ_energy_ref.1) | copy-start | bytes 772
  0.7 38.5 %copy-start.18 = (s32[2]{0:T(128)S(1)}, s32[2]{0:T(128)}, u32[]{:S(2)}) copy-start(s32[2]{0:T(128)} %tiles_a_s.3) | copy-start | bytes 28
  3.9 7.2 %collective-permute-start.25 = (bf16[224,640]{1,0:T(8,128)(2,1)S(1)}, bf16[224,640]{1,0:T(8,128)(2,1)S(1)}, u32[]{:S(2)}, u32[]{:S(2)}) collective-permute-start(bf16[224,640]{1,0:T(8,128)(2,1)S(1)} %get-tuple-element.79.refs_8_), channel_id=1, source_target_pairs={{0,8},{8,0},{16,24},{24,16},{32,40},{40,32},{48,56},{56,48},{64,72... | collective-permute-start | bytes 860168 | tf_op jit(solution)/shard_map/ppermute | solution.py:238
  7.2 10.4 %collective-permute-start.24 = (bf16[224,640]{1,0:T(8,128)(2,1)S(1)}, bf16[224,640]{1,0:T(8,128)(2,1)S(1)}, u32[]{:S(2)}, u32[]{:S(2)}) collective-permute-start(bf16[224,640]{1,0:T(8,128)(2,1)S(1)} %get-tuple-element.79.refs_8_), channel_id=1, source_target_pairs={{0,1},{1,2},{2,3},{3,4},{4,5},{5,6},{6,7},{7,0},{8,15},{9,8},{10,9... | collective-permute-start | bytes 860168 | tf_op jit(solution)/shard_map/ppermute | solution.py:234
  11.0 9.7 %collective-permute-start.26 = (bf16[224,640]{1,0:T(8,128)(2,1)S(1)}, bf16[224,640]{1,0:T(8,128)(2,1)S(1)}, u32[]{:S(2)}, u32[]{:S(2)}) collective-permute-start(bf16[224,640]{1,0:T(8,128)(2,1)S(1)} %collective-permute-done.25), channel_id=1, source_target_pairs={{0,1},{1,2},{2,3},{3,4},{4,5},{5,6},{6,7},{7,0},{8,15},{9,8},{10,9... | collective-permute-start | bytes 860168 | tf_op jit(solution)/shard_map/ppermute | solution.py:234
  13.2 5.2 %collective-permute-start.21 = (bf16[16,2048]{1,0:T(8,128)(2,1)S(1)}, bf16[16,2048]{1,0:T(8,128)(2,1)S(1)}, u32[]{:S(2)}, u32[]{:S(2)}) collective-permute-start(bf16[16,2048]{1,0:T(8,128)(2,1)S(1)} %pack_amplitudes.2.refs_0_), channel_id=1, source_target_pairs={{0,16},{8,72},{16,32},{24,88},{32,48},{40,104},{48,0},{56,120},{64... | collective-permute-start | bytes 196616 | tf_op jit(solution)/shard_map/ppermute | solution.py:242
  14.6 3.8 %collective-permute-start.22 = (bf16[16,2048]{1,0:T(8,128)(2,1)S(1)}, bf16[16,2048]{1,0:T(8,128)(2,1)S(1)}, u32[]{:S(2)}, u32[]{:S(2)}) collective-permute-start(bf16[16,2048]{1,0:T(8,128)(2,1)S(1)} %pack_amplitudes.2.refs_0_), channel_id=1, source_target_pairs={{0,48},{8,200},{16,0},{24,216},{32,16},{40,232},{48,32},{56,248},{... | collective-permute-start | bytes 196616 | tf_op jit(solution)/shard_map/ppermute | solution.py:242
  16.1 4.6 %collective-permute-start.23 = (bf16[16,2048]{1,0:T(8,128)(2,1)S(1)}, bf16[16,2048]{1,0:T(8,128)(2,1)S(1)}, u32[]{:S(2)}, u32[]{:S(2)}) collective-permute-start(bf16[16,2048]{1,0:T(8,128)(2,1)S(1)} %pack_amplitudes.2.refs_0_), channel_id=1, source_target_pairs={{0,32},{8,136},{16,48},{24,152},{32,0},{40,168},{48,16},{56,184},{... | collective-permute-start | bytes 196616 | tf_op jit(solution)/shard_map/ppermute | solution.py:242
  17.6 8.1 %collective-permute-start.35 = (bf16[224,640]{1,0:T(8,128)(2,1)S(1)}, bf16[224,640]{1,0:T(8,128)(2,1)S(1)}, u32[]{:S(2)}, u32[]{:S(2)}) collective-permute-start(bf16[224,640]{1,0:T(8,128)(2,1)S(1)} %collective-permute-done.24.refs_4_.refs_9_), channel_id=1, source_target_pairs={{0,1},{1,2},{2,3},{3,4},{4,5},{5,6},{6,7},{7,0},{8,15},{9,8},{10,9... | collective-permute-start | bytes 860168 | tf_op jit(solution)/shard_map/ppermute | solution.py:234
  20.7 6.9 %collective-permute-start.27 = (bf16[64,2048]{1,0:T(8,128)(2,1)S(1)}, bf16[64,2048]{1,0:T(8,128)(2,1)S(1)}, u32[]{:S(2)}, u32[]{:S(2)}) collective-permute-start(bf16[64,2048]{1,0:T(8,128)(2,1)S(1)} %stack.2.refs_0_), channel_id=1, source_target_pairs={{0,64},{8,24},{16,80},{24,40},{32,96},{40,56},{48,112},{56,8},{64,... | collective-permute-start | bytes 786440 | tf_op jit(solution)/shard_map/ppermute | solution.py:242
  22.0 6.5 %collective-permute-start.28 = (bf16[64,2048]{1,0:T(8,128)(2,1)S(1)}, bf16[64,2048]{1,0:T(8,128)(2,1)}, u32[]{:S(2)}, u32[]{:S(2)}) collective-permute-start(bf16[64,2048]{1,0:T(8,128)(2,1)S(1)} %stack.2.refs_0_), channel_id=1, source_target_pairs={{0,192},{8,56},{16,208},{24,8},{32,224},{40,24},{48,240},{56,40},{... | collective-permute-start | bytes 786440 | tf_op jit(solution)/shard_map/ppermute | solution.py:242
  23.5 7.0 %collective-permute-start.36 = (bf16[224,640]{1,0:T(8,128)(2,1)S(1)}, bf16[224,640]{1,0:T(8,128)(2,1)}, u32[]{:S(2)}, u32[]{:S(2)}) collective-permute-start(bf16[224,640]{1,0:T(8,128)(2,1)S(1)} %collective-permute-done.26.refs_5_), channel_id=1, source_target_pairs={{0,1},{1,2},{2,3},{3,4},{4,5},{5,6},{6,7},{7,0},{8,15},{9,8},{10,9... | collective-permute-start | bytes 860168 | tf_op jit(solution)/shard_map/ppermute | solution.py:234
  24.5 7.1 %collective-permute-start.29 = (bf16[64,2048]{1,0:T(8,128)(2,1)S(1)}, bf16[64,2048]{1,0:T(8,128)(2,1)}, u32[]{:S(2)}, u32[]{:S(2)}) collective-permute-start(bf16[64,2048]{1,0:T(8,128)(2,1)S(1)} %stack.2.refs_0_), channel_id=1, source_target_pairs={{0,128},{8,40},{16,144},{24,56},{32,160},{40,8},{48,176},{56,24},{... | collective-permute-start | bytes 786440 | tf_op jit(solution)/shard_map/ppermute | solution.py:242
  25.7 7.7 %collective-permute-start.34 = (bf16[224,640]{1,0:T(8,128)(2,1)S(1)}, bf16[224,640]{1,0:T(8,128)(2,1)S(1)}, u32[]{:S(2)}, u32[]{:S(2)}) collective-permute-start(bf16[224,640]{1,0:T(8,128)(2,1)S(1)} %collective-permute-done.26.refs_5_), channel_id=1, source_target_pairs={{0,8},{8,0},{16,24},{24,16},{32,40},{40,32},{48,56},{56,48},{64,72... | collective-permute-start | bytes 860168 | tf_op jit(solution)/shard_map/ppermute | solution.py:238
  27.6 6.8 %collective-permute-start.38 = (bf16[224,640]{1,0:T(8,128)(2,1)S(1)}, bf16[224,640]{1,0:T(8,128)(2,1)S(1)}, u32[]{:S(2)}, u32[]{:S(2)}) collective-permute-start(bf16[224,640]{1,0:T(8,128)(2,1)S(1)} %collective-permute-done.35.refs_11_), channel_id=1, source_target_pairs={{0,1},{1,2},{2,3},{3,4},{4,5},{5,6},{6,7},{7,0},{8,15},{9,8},{10,9... | collective-permute-start | bytes 860168 | tf_op jit(solution)/shard_map/ppermute | solution.py:234
  28.6 4.2 %collective-permute-start.30 = (bf16[64,2048]{1,0:T(8,128)(2,1)S(1)}, bf16[64,2048]{1,0:T(8,128)(2,1)S(1)}, u32[]{:S(2)}, u32[]{:S(2)}) collective-permute-start(bf16[64,2048]{1,0:T(8,128)(2,1)S(1)} %stack.2.refs_0_), channel_id=1, source_target_pairs={{0,8},{8,0},{16,24},{24,16},{32,40},{40,32},{48,56},{56,48},{64,72... | collective-permute-start | bytes 786440 | tf_op jit(solution)/shard_map/ppermute | solution.py:238
  30.5 7.2 %collective-permute-start.39 = (bf16[224,640]{1,0:T(8,128)(2,1)}, bf16[224,640]{1,0:T(8,128)(2,1)}, u32[]{:S(2)}, u32[]{:S(2)}) collective-permute-start(bf16[224,640]{1,0:T(8,128)(2,1)} %collective-permute-done.36), channel_id=1, source_target_pairs={{0,1},{1,2},{2,3},{3,4},{4,5},{5,6},{6,7},{7,0},{8,15},{9,8},{10,9... | collective-permute-start | bytes 860168 | tf_op jit(solution)/shard_map/ppermute | solution.py:234
  31.6 3.6 %collective-permute-start.31 = (bf16[64,2048]{1,0:T(8,128)(2,1)S(1)}, bf16[64,2048]{1,0:T(8,128)(2,1)S(1)}, u32[]{:S(2)}, u32[]{:S(2)}) collective-permute-start(bf16[64,2048]{1,0:T(8,128)(2,1)S(1)} %collective-permute-done.27.refs_1_), channel_id=1, source_target_pairs={{0,8},{8,0},{16,24},{24,16},{32,40},{40,32},{48,56},{56,48},{64,72... | collective-permute-start | bytes 786440 | tf_op jit(solution)/shard_map/ppermute | solution.py:238
  33.4 5.7 %collective-permute-start.37 = (bf16[224,640]{1,0:T(8,128)(2,1)}, bf16[224,640]{1,0:T(8,128)(2,1)S(1)}, u32[]{:S(2)}, u32[]{:S(2)}) collective-permute-start(bf16[224,640]{1,0:T(8,128)(2,1)} %collective-permute-done.36), channel_id=1, source_target_pairs={{0,8},{8,0},{16,24},{24,16},{32,40},{40,32},{48,56},{56,48},{64,72... | collective-permute-start | bytes 860168 | tf_op jit(solution)/shard_map/ppermute | solution.py:238
  33.4 5.7 %collective-permute-start.32 = (bf16[64,2048]{1,0:T(8,128)(2,1)}, bf16[64,2048]{1,0:T(8,128)(2,1)}, u32[]{:S(2)}, u32[]{:S(2)}) collective-permute-start(bf16[64,2048]{1,0:T(8,128)(2,1)} %collective-permute-done.28.refs_2_), channel_id=1, source_target_pairs={{0,8},{8,0},{16,24},{24,16},{32,40},{40,32},{48,56},{56,48},{64,72... | collective-permute-start | bytes 786440 | tf_op jit(solution)/shard_map/ppermute | solution.py:238
  34.4 4.7 %collective-permute-start.33 = (bf16[64,2048]{1,0:T(8,128)(2,1)}, bf16[64,2048]{1,0:T(8,128)(2,1)}, u32[]{:S(2)}, u32[]{:S(2)}) collective-permute-start(bf16[64,2048]{1,0:T(8,128)(2,1)} %collective-permute-done.29.refs_3_), channel_id=1, source_target_pairs={{0,8},{8,0},{16,24},{24,16},{32,40},{40,32},{48,56},{56,48},{64,72... | collective-permute-start | bytes 786440 | tf_op jit(solution)/shard_map/ppermute | solution.py:238
  35.9 8.3 %collective-permute-start.41 = (bf16[224,640]{1,0:T(8,128)(2,1)S(1)}, bf16[224,640]{1,0:T(8,128)(2,1)S(1)}, u32[]{:S(2)}, u32[]{:S(2)}) collective-permute-start(bf16[224,640]{1,0:T(8,128)(2,1)S(1)} %collective-permute-done.38.refs_13_), channel_id=1, source_target_pairs={{0,1},{1,2},{2,3},{3,4},{4,5},{5,6},{6,7},{7,0},{8,15},{9,8},{10,9... | collective-permute-start | bytes 860168 | tf_op jit(solution)/shard_map/ppermute | solution.py:234
  37.7 6.6 %collective-permute-start.40 = (bf16[224,640]{1,0:T(8,128)(2,1)}, bf16[224,640]{1,0:T(8,128)(2,1)S(1)}, u32[]{:S(2)}, u32[]{:S(2)}) collective-permute-start(bf16[224,640]{1,0:T(8,128)(2,1)} %collective-permute-done.39), channel_id=1, source_target_pairs={{0,8},{8,0},{16,24},{24,16},{32,40},{40,32},{48,56},{56,48},{64,72... | collective-permute-start | bytes 860168 | tf_op jit(solution)/shard_map/ppermute | solution.py:238
  39.2 1.0 %copy-start.6 = (bf16[64,2048]{1,0:T(8,128)(2,1)S(1)}, bf16[64,2048]{1,0:T(8,128)(2,1)}, u32[]{:S(2)}) copy-start(bf16[64,2048]{1,0:T(8,128)(2,1)} %copy-done.5) | copy-start | bytes 786436
  40.2 0.9 %copy-start.8 = (bf16[64,2048]{1,0:T(8,128)(2,1)S(1)}, bf16[64,2048]{1,0:T(8,128)(2,1)}, u32[]{:S(2)}) copy-start(bf16[64,2048]{1,0:T(8,128)(2,1)} %copy-done.7) | copy-start | bytes 786436
  44.2 1.8 %copy-start.9 = (bf16[1280,640]{1,0:T(8,128)(2,1)S(1)}, bf16[1280,640]{1,0:T(8,128)(2,1)}, u32[]{:S(2)}) copy-start(bf16[1280,640]{1,0:T(8,128)(2,1)} %panel_hbm.1) | copy-start | bytes 4915204
  44.3 1.8 %copy-start.12 = (bf16[16,10240]{1,0:T(8,128)(2,1)S(1)}, bf16[16,10240]{1,0:T(8,128)(2,1)}, u32[]{:S(2)}) copy-start(bf16[16,10240]{1,0:T(8,128)(2,1)} %rows_ref.1) | copy-start | bytes 983044
  (2 other events, 1.4 us)
